TPU v7x, 1024 devices: a whole 4x8x16 slice. The times are simulated.
1024 devices in a mesh: dom: 128 (over y, z), sub: 8 (over x, core).
Axes of the slice: x: 4, y: 8, z: 16, core: 2. Of those that a mesh axis runs over, the one named last changes fastest.
Arguments:
- a_tiles: bfloat16 [8192, 8, 128, 128], P(('dom', 'sub')), may hold values from -0.5 to 0.5
- col_tiles: int32 [8192, 8], P(('dom', 'sub')), may hold values from 0 to 8191, as said below
- counts: int32 [8192], P(('dom', 'sub')), may hold values from 1 to 8, as said below
- aggregate: int32 [8192], P(('dom', 'sub')), may hold values from 0 to 511, as said below
- p_tiles: bfloat16 [8192, 128, 128], P(('dom', 'sub')), may hold values from -0.25 to 0.25
Outputs:
- coarse: float32 [65536, 1536], P(('dom', 'sub'))
Inputs may be any that keep to these rules, and one draw needn't show every extreme that they name: `col_tiles`: slot 0 of each row names the row itself. A column of a row of device (g, s) lies on device (g, s), on device (g - 1 mod 128, s) among its last 2 rows, or on device (g + 1 mod 128, s) among its first 2 rows. `counts`: the first row of every device has 8 live slots. `aggregate`: rows of group g name coarse tiles g * 4 to g * 4 + 3.
All inputs are finite; a program needn't handle non-finite values.
Results may differ from a plain program's by a relative error of at most 0.012.
Values may be sent and summed in bfloat16 or wider, within the bound.
No kernel may reach another device: no remote copies, remote signals or barrier semaphores. Data moves between devices by JAX's collectives and lax.ppermute only.
A program may use at most 32 MiB of HBM per device.

v0:
```python
import jax
import jax.numpy as jnp
from jax import lax
from jax.sharding import PartitionSpec as P

K = 8
CG = 4


def from_behind(block, axis, distance):
    devices = range(lax.axis_size(axis))
    route = [((i - distance) % len(devices), i) for i in devices]
    return lax.ppermute(block, axis, route)


def local(a_tiles, col_tiles, counts, aggregate, p_tiles):
    row_count = a_tiles.shape[0]
    groups = lax.axis_size("dom")
    members = lax.axis_size("sub")
    my_group = lax.axis_index("dom")
    owner_dev = col_tiles // row_count
    local_idx = col_tiles % row_count
    col_group = owner_dev // members
    offset = (col_group - my_group + 1) % groups
    before = from_behind((p_tiles, aggregate), "dom", 1)
    ahead_tiles = from_behind((p_tiles, aggregate), "dom", -1)
    position = offset * row_count + local_idx
    stacked_p = jnp.concatenate([before[0], p_tiles, ahead_tiles[0]], axis=0)
    stacked_agg = jnp.concatenate([before[1], aggregate, ahead_tiles[1]], axis=0)
    coarse_col = offset * CG + stacked_agg[position] - col_group * CG
    coarse_row = aggregate - my_group * CG
    slot_ids = coarse_row[:, None] * (3 * CG) + coarse_col
    slots = 3 * CG * CG
    live = jnp.arange(K, dtype=jnp.int32)[None, :] < counts[:, None]
    onehot = (
        (slot_ids[:, :, None] == jnp.arange(slots, dtype=jnp.int32)[None, None, :])
        & live[:, :, None]
    ).astype(jnp.float32)
    block_rows = 4
    nblocks = row_count // block_rows

    def blocked(array):
        return array.reshape((nblocks, block_rows) + array.shape[1:])

    def accumulate(summed, inputs):
        a_block, pos_block, p_block, hot_block = inputs
        near_p = stacked_p[pos_block]
        prod = jnp.einsum(
            "rkab,rkbc->rkac", a_block, near_p, preferred_element_type=jnp.float32
        ).astype(jnp.bfloat16)
        term = jnp.einsum("rba,rkbc->rkac", p_block, prod, preferred_element_type=jnp.float32)
        summed = summed + jnp.einsum(
            "rks,rkac->sac", hot_block, term, precision=lax.Precision.HIGHEST
        )
        return (summed, None)

    tile = a_tiles.shape[2]
    initial = jnp.zeros((slots, tile, tile), jnp.float32)
    summed, unused = lax.scan(
        accumulate,
        initial,
        (blocked(a_tiles), blocked(position), blocked(p_tiles), blocked(onehot)),
    )
    summed = (
        summed.reshape(CG, 3 * CG, tile, tile)
        .transpose(0, 2, 1, 3)
        .reshape(CG * tile, 3 * CG * tile)
    )
    return lax.psum_scatter(
        summed.astype(jnp.bfloat16), "sub", scatter_dimension=0, tiled=True
    ).astype(jnp.float32)


def solution(mesh):
    in_specs = (
        P(("dom", "sub"), None, None, None),
        P(("dom", "sub"), None),
        P(("dom", "sub")),
        P(("dom", "sub")),
        P(("dom", "sub"), None, None),
    )
    out_specs = P(("dom", "sub"), None)
    return jax.shard_map(local, mesh=mesh, in_specs=in_specs, out_specs=out_specs, check_vma=False)
```

profile of v0, /device:TPU:1, one launch (start us, length us, event | category | flops | bytes accessed | tf_op | source)
XLA Modules:
  0.0 116.2 jit_solution(15091622431647278649)
XLA Ops:
  6.5 4.8 %collective-permute-start = (s32[8]{0:T(128)}, s32[8]{0:T(128)S(1)}, u32[]{:S(2)}, u32[]{:S(2)}) collective-permute-start(s32[8]{0:T(128)} %param.10), channel_id=1, source_target_pairs={{1016,0},{0,8},{8,16},{16,24},{24,32},{32,40},{40,48},{48,56},{56,... | collective-permute-start | bytes 104 | tf_op jit(solution)/shard_map/ppermute | solution.py:13
  11.4 18.8 %collective-permute-start.1 = (s32[8]{0:T(128)}, s32[8]{0:T(128)S(1)}, u32[]{:S(2)}, u32[]{:S(2)}) collective-permute-start(s32[8]{0:T(128)} %param.10), channel_id=1, source_target_pairs={{8,0},{16,8},{24,16},{32,24},{40,32},{48,40},{56,48},{64,56},{72,6... | collective-permute-start | bytes 104 | tf_op jit(solution)/shard_map/ppermute | solution.py:13
  30.1 1.9 %collective-permute-start.2 = (bf16[8,128,128]{2,1,0:T(8,128)(2,1)}, bf16[8,128,128]{2,1,0:T(8,128)(2,1)S(1)}, u32[]{:S(2)}, u32[]{:S(2)}) collective-permute-start(bf16[8,128,128]{2,1,0:T(8,128)(2,1)} %param.11), channel_id=1, source_target_pairs={{1016,0},{0,8},{8,16},{16,24},{24,32},{32,40},{40,48},{48,56},{56,... | collective-permute-start | bytes 786440 | tf_op jit(solution)/shard_map/ppermute | solution.py:13
  32.1 6.7 %collective-permute-start.3 = (bf16[8,128,128]{2,1,0:T(8,128)(2,1)}, bf16[8,128,128]{2,1,0:T(8,128)(2,1)S(1)}, u32[]{:S(2)}, u32[]{:S(2)}) collective-permute-start(bf16[8,128,128]{2,1,0:T(8,128)(2,1)} %param.11), channel_id=1, source_target_pairs={{8,0},{16,8},{24,16},{32,24},{40,32},{48,40},{56,48},{64,56},{72,6... | collective-permute-start | bytes 786440 | tf_op jit(solution)/shard_map/ppermute | solution.py:13
  38.8 0.7 compare_select_fusion.1
  39.6 0.7 subtract_multiply_fusion
  40.3 0.7 lt.50
  41.1 0.7 pad_add_fusion
  41.8 0.8 gather_fusion.1
  42.9 0.6 collective-permute-done.3
  43.5 22.7 %while.11 = (s32[]{:T(128)}, f32[48,128,128]{2,0,1:T(8,128)}, f32[2,4,8,48]{3,2,1,0:T(8,128)S(1)}, bf16[2,4,8,128,128]{4,3,2,1,0:T(8,128)(2,1)}, s32[2,4,8]{2,1,...) while((s32[]{:T(128)}, f32[48,128,128]{2,0,1:T(8,128)}, ...), condition=%wide.region_1.2_spmd.clone, body=%wide.region_0.1_spmd.clone.sunk | while | flops 572523648 | bytes 19027824 | solution.py:59
  43.6 0.7 gather_fusion
  44.4 3.3 %convolution_bitcast_fusion.2 = f32[4,8,128,128]{2,3,1,0:T(8,128)} fusion(bf16[4,8,128,128]{3,2,1,0:T(8,128)(2,1)S(1)} %bitcast.57, bf16[2,4,8,128,128]{4,3,2,1,0:T(8,128)(2,1)} %get-tuple-element.147, s32[]{:T(128)} %get-tuple-element.135, bf16[2,4,128,128]{3,2,1,0:T(8,128)(2,1)S(1)} %get-tuple-element.150), kind=kOutput, calls=%fused_computation.3.clone.1 | convolution fusion | flops 268959744 | bytes 4326400 | tf_op jit(solution)/shard_map/while/body/eval_jaxpr/rba,rkbc->rkac/dot_general | solution.py:51
  47.7 2.4 %copy.33 = f32[4,8,128,128]{3,1,0,2:T(8,128)S(1)} copy(f32[4,8,128,128]{2,3,1,0:T(8,128)} %convolution_bitcast_fusion.2) | data formatting | bytes 4194304 | tf_op jit(solution)/shard_map/while/body/eval_jaxpr/rba,rkbc->rkac/transpose | solution.py:51
  50.1 4.1 %bitcast_add_fusion.2 = f32[48,128,128]{2,0,1:T(8,128)} fusion(f32[48,128,128]{2,0,1:T(8,128)} %get-tuple-element.136, f32[4,8,128,128]{3,1,0,2:T(8,128)S(1)} %copy.33, pred[]{:T(512)S(6)} %compare.9, f32[2,4,8,48]{3,2,1,0:T(8,128)S(1)} %get-tuple-element.146, s32[]{:T(128)} %get-tuple-element.135), kind=kOutput, calls=%fused_computation.2.clone.1 | convolution fusion | flops 303562752 | bytes 8404997 | tf_op jit(solution)/shard_map/while/body/eval_jaxpr/rks,rkac->sac/dot_general | solution.py:52
  54.3 0.7 gather_fusion
  55.0 3.3 %convolution_bitcast_fusion.2 = f32[4,8,128,128]{2,3,1,0:T(8,128)} fusion(bf16[4,8,128,128]{3,2,1,0:T(8,128)(2,1)S(1)} %bitcast.57, bf16[2,4,8,128,128]{4,3,2,1,0:T(8,128)(2,1)} %get-tuple-element.147, s32[]{:T(128)} %get-tuple-element.135, bf16[2,4,128,128]{3,2,1,0:T(8,128)(2,1)S(1)} %get-tuple-element.150), kind=kOutput, calls=%fused_computation.3.clone.1 | convolution fusion | flops 268959744 | bytes 4326400 | tf_op jit(solution)/shard_map/while/body/eval_jaxpr/rba,rkbc->rkac/dot_general | solution.py:51
  58.3 2.4 %copy.33 = f32[4,8,128,128]{3,1,0,2:T(8,128)S(1)} copy(f32[4,8,128,128]{2,3,1,0:T(8,128)} %convolution_bitcast_fusion.2) | data formatting | bytes 4194304 | tf_op jit(solution)/shard_map/while/body/eval_jaxpr/rba,rkbc->rkac/transpose | solution.py:51
  60.7 5.5 %bitcast_add_fusion.2 = f32[48,128,128]{2,0,1:T(8,128)} fusion(f32[48,128,128]{2,0,1:T(8,128)} %get-tuple-element.136, f32[4,8,128,128]{3,1,0,2:T(8,128)S(1)} %copy.33, pred[]{:T(512)S(6)} %compare.9, f32[2,4,8,48]{3,2,1,0:T(8,128)S(1)} %get-tuple-element.146, s32[]{:T(128)} %get-tuple-element.135), kind=kOutput, calls=%fused_computation.2.clone.1 | convolution fusion | flops 303562752 | bytes 8404997 | tf_op jit(solution)/shard_map/while/body/eval_jaxpr/rks,rkac->sac/dot_general | solution.py:52
  66.2 2.9 %copy.30 = bf16[48,128,128]{2,1,0:T(8,128)(2,1)S(1)} copy(f32[48,128,128]{2,0,1:T(8,128)} %get-tuple-element.42) | data formatting | bytes 4718592 | tf_op jit(solution)/shard_map/while | solution.py:59
  69.1 1.1 copy.25
  70.2 1.6 %copy.31 = bf16[64,8,12,128]{3,1,2,0:T(8,128)(2,1)} copy(bf16[64,8,12,128]{3,2,1,0:T(8,128)(2,1)S(1)} %bitcast.59) | data formatting | bytes 3145728
  71.8 35.9 %reduce-scatter.4.cloned.1.call-done = bf16[64,1536]{1,0:T(8,128)(2,1)} async-done(((bf16[512,1536]{1,0:T(8,128)(2,1)}), bf16[64,1536]{1,0:T(8,128)(2,1)}) %reduce-scatter.4.cloned.1.call-update) | async-done | bytes 196624 | tf_op jit(solution)/shard_map/reduce_scatter | solution.py:69
  107.6 1.7 %convert_element_type.27 = f32[64,1536]{1,0:T(8,128)} convert(bf16[64,1536]{1,0:T(8,128)(2,1)} %reduce-scatter.4.cloned.1.call-done) | non-fusion elementwise | flops 98304 | bytes 589824 | tf_op jit(solution)/shard_map/convert_element_type | solution.py:71
  (23 shorter events, 0.7 us)
Async XLA Ops:
  6.5 101.1 %reduce-scatter.4.cloned.1.call-start = ((), (), s32[]{:S(2)}) async-start(), calls=%async_computation.1 | async-start | bytes 1769472 | tf_op jit(solution)/shard_map/reduce_scatter | solution.py:69
  6.5 34.5 %collective-permute-start = (s32[8]{0:T(128)}, s32[8]{0:T(128)S(1)}, u32[]{:S(2)}, u32[]{:S(2)}) collective-permute-start(s32[8]{0:T(128)} %param.10), channel_id=1, source_target_pairs={{1016,0},{0,8},{8,16},{16,24},{24,32},{32,40},{40,48},{48,56},{56,... | collective-permute-start | bytes 104 | tf_op jit(solution)/shard_map/ppermute | solution.py:13
  11.4 29.7 %collective-permute-start.1 = (s32[8]{0:T(128)}, s32[8]{0:T(128)S(1)}, u32[]{:S(2)}, u32[]{:S(2)}) collective-permute-start(s32[8]{0:T(128)} %param.10), channel_id=1, source_target_pairs={{8,0},{16,8},{24,16},{32,24},{40,32},{48,40},{56,48},{64,56},{72,6... | collective-permute-start | bytes 104 | tf_op jit(solution)/shard_map/ppermute | solution.py:13
  30.1 12.7 %collective-permute-start.2 = (bf16[8,128,128]{2,1,0:T(8,128)(2,1)}, bf16[8,128,128]{2,1,0:T(8,128)(2,1)S(1)}, u32[]{:S(2)}, u32[]{:S(2)}) collective-permute-start(bf16[8,128,128]{2,1,0:T(8,128)(2,1)} %param.11), channel_id=1, source_target_pairs={{1016,0},{0,8},{8,16},{16,24},{24,32},{32,40},{40,48},{48,56},{56,... | collective-permute-start | bytes 786440 | tf_op jit(solution)/shard_map/ppermute | solution.py:13
  32.1 11.3 %collective-permute-start.3 = (bf16[8,128,128]{2,1,0:T(8,128)(2,1)}, bf16[8,128,128]{2,1,0:T(8,128)(2,1)S(1)}, u32[]{:S(2)}, u32[]{:S(2)}) collective-permute-start(bf16[8,128,128]{2,1,0:T(8,128)(2,1)} %param.11), channel_id=1, source_target_pairs={{8,0},{16,8},{24,16},{32,24},{40,32},{48,40},{56,48},{64,56},{72,6... | collective-permute-start | bytes 786440 | tf_op jit(solution)/shard_map/ppermute | solution.py:13
  41.8 0.9 copy-start.1
  41.8 1.6 %copy-start = (bf16[8,128,128]{2,1,0:T(8,128)(2,1)S(1)}, bf16[8,128,128]{2,1,0:T(8,128)(2,1)}, u32[]{:S(2)}) copy-start(bf16[8,128,128]{2,1,0:T(8,128)(2,1)} %param.11) | copy-start | bytes 786436
Sparse Core Ops, SparseCore 0:
  71.9 35.6 reduce-scatter.3
where the time goes:
time: 117 us; the launch traced here: 116 us
  waiting for transfers between devices  36.4 us (31%)
  starting transfers between devices  32.2 us (28%)
  matrix products  16.2 us (14%)
  local copies, waits for them, and re-layouts  13.6 us (12%)
  between operations  13.5 us (12%)
  other arithmetic  4.18 us (4%)
    reduce_scatter x1, waiting for transfers between devices, local(): lax.psum_scatter(summed.astype(jnp.bfloat16), 'sub', scatter_dimension=0,...  35.9 us
    ppermute x4, starting transfers between devices, from_behind(): return lax.ppermute(block, axis, route)  32.2 us
    dot_general x2, matrix products, accumulate(): jnp.einsum('rks,rkac->sac', hot_block, term, precision=lax.Precision.HIGH...  9.64 us
    dot_general x2, matrix products, accumulate(): jnp.einsum('rba,rkbc->rkac', p_block, prod, preferred_element_type=jnp.fl...  6.55 us
    transpose x2, local copies, waits for them, and re-layouts, accumulate(): jnp.einsum('rba,rkbc->rkac', p_block, prod, preferred_element_type=jnp.fl...  4.74 us
    while x1, local copies, waits for them, and re-layouts, local(): lax.scan(accumulate, initial, (blocked(a_tiles), blocked(position), block...  2.9 us
    unnamed x6, local copies, waits for them, and re-layouts  2.65 us
  transfers between devices with their start and end apart: 5, of which 2 were waited for; matrix products, arithmetic and copies ran while one was open for 3% of the time, Pallas kernels for 0%

commit v1 on v0

v1 whole, which is shorter than its diff:
```python
import functools

import jax
import jax.numpy as jnp
from jax import lax
from jax.experimental import pallas as pl
from jax.experimental.pallas import tpu as pltpu
from jax.sharding import PartitionSpec as P

CG = 4
HALO = 2
MARK = 16


def front_kernel(groups, members, col_ref, count_ref, agg_ref, a_hbm, p_ref, g_ref, own_ref, a_ref, acc_ref, gown_ref, place_ref, sems):
    rows, slots, tile = a_hbm.shape[0], a_hbm.shape[1], a_hbm.shape[2]
    columns = rows + 2 * HALO
    half = tile // 2
    copies = [pltpu.make_async_copy(a_hbm.at[t], a_ref.at[t], sems.at[t]) for t in range(rows)]
    for copy in copies:
        copy.start()
    acc_ref[...] = jnp.zeros_like(acc_ref)
    device = col_ref[0, 0] // rows
    my_group = device // members
    core = device % 2
    for r in range(rows):
        coarse = agg_ref[r] - my_group * CG
        for j in range(CG):
            place_ref[pl.ds(r * tile, tile), pl.ds(j * tile, tile)] = jnp.where(coarse == j, p_ref[r], jnp.zeros_like(p_ref[r]))
    for t in range(rows):
        coarse = agg_ref[t] - my_group * CG
        p_t = p_ref[t].T
        copies[t].wait()
        for pair in range(slots // 2):
            both = jnp.concatenate([a_ref[t, 2 * pair], a_ref[t, 2 * pair + 1]], axis=1)
            terms = jnp.dot(p_t, both, preferred_element_type=jnp.float32)
            for side in range(2):
                k = 2 * pair + side
                column = col_ref[t, k]
                side_of = column // (rows * members) - my_group + 1 + groups
                side_of = lax.rem(side_of, groups)
                near = lax.rem(column, rows) + rows * side_of - (rows - HALO)
                at = jnp.where(k < count_ref[t], coarse * columns + near, CG * columns)
                at = jnp.clip(at, 0, CG * columns)
                acc_ref[at] += terms[:, side * tile : (side + 1) * tile]
    for i in range(CG):
        for part in range(2):
            first = pl.multiple_of((core if part == 1 else 1 - core) * half, half)
            to = pl.ds((part * CG + i) * half, half)
            for c in range(columns):
                block = acc_ref[i * columns + c, pl.ds(first, half), :].astype(jnp.bfloat16)
                if c < HALO:
                    g_ref[to, pl.ds(c * tile, tile)] = block
                elif c >= HALO + rows:
                    g_ref[to, pl.ds((c - rows) * tile, tile)] = block
                else:
                    gown_ref[to, pl.ds((c - HALO) * tile, tile)] = block
    own_ref[...] = jnp.dot(gown_ref[...], place_ref[...], preferred_element_type=jnp.float32).astype(jnp.bfloat16)


def back_kernel(g_ref, own_ref, before_ref, ahead_ref, out_ref, send_ref, place_ref):
    tile = before_ref.shape[1]
    rows = out_ref.shape[0]
    for side, halo_ref in enumerate((before_ref, ahead_ref)):
        for r in range(HALO):
            block = halo_ref[pl.ds(r * tile, tile), :]
            mark = halo_ref[pl.ds(HALO * tile + r * MARK, MARK), :].astype(jnp.float32)[0:1, :]
            for j in range(CG):
                chosen = jnp.where(mark == float(j), 1.0, 0.0).astype(jnp.bfloat16)
                place_ref[side, pl.ds(r * tile, tile), pl.ds(j * tile, tile)] = block * chosen
    width = CG * tile
    for side in range(2):
        depth = HALO * tile
        result = jnp.dot(g_ref[:, pl.ds(side * depth, depth)], place_ref[side], preferred_element_type=jnp.float32).astype(jnp.bfloat16)
        at = pl.ds(2 * side * width, width)
        send_ref[:, at] = result[:rows]
        out_ref[:, at] = result[rows:]
    send_ref[:, pl.ds(width, width)] = own_ref[pl.ds(0, rows), :]
    out_ref[:, pl.ds(width, width)] = own_ref[pl.ds(rows, rows), :]


def local(groups, members, a_tiles, col_tiles, counts, aggregate, p_tiles):
    rows, slots, tile = a_tiles.shape[0], a_tiles.shape[1], a_tiles.shape[2]
    columns = rows + 2 * HALO
    my_group = lax.axis_index("dom")
    coarse = (aggregate - my_group * CG).astype(jnp.bfloat16)

    def halo(first, step):
        marks = jnp.broadcast_to(coarse[first : first + HALO, None, None], (HALO, MARK, tile)).reshape(HALO * MARK, tile)
        block = jnp.concatenate([p_tiles[first : first + HALO].reshape(HALO * tile, tile), marks], axis=0)
        return lax.ppermute(block, "dom", [(i, (i + step) % groups) for i in range(groups)])

    before = halo(rows - HALO, 1)
    ahead = halo(0, -1)

    smem = pl.BlockSpec(memory_space=pltpu.SMEM)
    vmem = pl.BlockSpec(memory_space=pltpu.VMEM)
    g, own = pl.pallas_call(
        functools.partial(front_kernel, groups, members),
        out_shape=(
            jax.ShapeDtypeStruct((CG * tile, 2 * HALO * tile), jnp.bfloat16),
            jax.ShapeDtypeStruct((CG * tile, CG * tile), jnp.bfloat16),
        ),
        in_specs=[smem, smem, smem, pl.BlockSpec(memory_space=pl.ANY), vmem],
        out_specs=(vmem, vmem),
        scratch_shapes=[
            pltpu.VMEM(a_tiles.shape, jnp.bfloat16),
            pltpu.VMEM((CG * columns + 1, tile, tile), jnp.float32),
            pltpu.VMEM((CG * tile, rows * tile), jnp.bfloat16),
            pltpu.VMEM((rows * tile, CG * tile), jnp.bfloat16),
            pltpu.SemaphoreType.DMA((rows,)),
        ],
        compiler_params=pltpu.CompilerParams(vmem_limit_bytes=24 * 2**20),
        cost_estimate=pl.CostEstimate(flops=2 * 10**9, bytes_accessed=4 * 2**20, transcendentals=0),
        name="front",
    )(col_tiles, counts, aggregate, a_tiles, p_tiles)

    share = CG * tile // 2
    keep, send = pl.pallas_call(
        back_kernel,
        out_shape=(jax.ShapeDtypeStruct((share, 3 * CG * tile), jnp.bfloat16),) * 2,
        in_specs=[vmem] * 4,
        out_specs=(vmem, vmem),
        scratch_shapes=[pltpu.VMEM((2, HALO * tile, CG * tile), jnp.bfloat16)],
        compiler_params=pltpu.CompilerParams(vmem_limit_bytes=24 * 2**20),
        cost_estimate=pl.CostEstimate(flops=3 * 10**8, bytes_accessed=3 * 2**20, transcendentals=0),
        name="back",
    )(g, own, before, ahead)
    other = lax.ppermute(send, "sub", [(i, i ^ 1) for i in range(members)])
    chip = (keep.astype(jnp.float32) + other.astype(jnp.float32)).astype(jnp.bfloat16)
    cores = [list(range(core, members, 2)) for core in range(2)]
    parts = lax.all_to_all(chip.reshape(members // 2, -1, chip.shape[1]), "sub", 0, 0, axis_index_groups=cores)
    return parts.astype(jnp.float32).sum(axis=0)


def solution(mesh):
    in_specs = (
        P(("dom", "sub"), None, None, None),
        P(("dom", "sub"), None),
        P(("dom", "sub")),
        P(("dom", "sub")),
        P(("dom", "sub"), None, None),
    )
    out_specs = P(("dom", "sub"), None)
    body = functools.partial(local, mesh.shape["dom"], mesh.shape["sub"])
    return jax.shard_map(body, mesh=mesh, in_specs=in_specs, out_specs=out_specs, check_vma=False)
```

time: 117 us -> 56.2 us (0.48)
  waiting for transfers between devices: 36.4 us -> 1.9 us
  matrix products: 16.2 us -> 0 us
  blocking collectives: 0 us -> 15.3 us
  between operations: 13.5 us -> 0.09 us
  local copies, waits for them, and re-layouts: 13.6 us -> 5.82 us
  starting transfers between devices: 32.2 us -> 26.4 us
  Pallas kernels: 0 us -> 4.35 us
  other arithmetic: 4.18 us -> 1.92 us
    reduce_scatter x1 -> x0, waiting for transfers between devices: 35.9 us -> none  [local(): lax.psum_scatter(summed.astype(jnp.bfloat16), 'sub', scatter_dimension=0,...]
    dot_general x4 -> x0, matrix products: 16.2 us -> none  [the longest x2 9.64 us: accumulate(): jnp.einsum('rks,rkac->sac', hot_block, term, precision=lax.Precision.HIGH...]
    all_to_all x0 -> x1, blocking collectives: none -> 15.3 us  [local(): lax.all_to_all(chip.reshape(members // 2, -1, chip.shape[1]), 'sub', 0, 0...]
    ppermute x4 -> x3, starting transfers between devices: 32.2 us -> 26.4 us  [the longest x2 23.6 us: halo(): lax.ppermute(block, 'dom', [(i, (i + step) % groups) for i in range(group...]
    transpose x2 -> x0, local copies, waits for them, and re-layouts: 4.74 us -> none  [accumulate(): jnp.einsum('rba,rkbc->rkac', p_block, prod, preferred_element_type=jnp.fl...]
    pallas_call x0 -> x2, Pallas kernels: none -> 4.35 us  [the longest x1 3.87 us: local(): pl.pallas_call(functools.partial(front_kernel, groups, members), out_shap...]
    while x1 -> x0, local copies, waits for them, and re-layouts: 2.9 us -> none  [local(): lax.scan(accumulate, initial, (blocked(a_tiles), blocked(position), block...]
    gather x4 -> x0, local copies, waits for them, and re-layouts: 2.35 us -> none  [the longest x2 1.5 us: accumulate(): near_p = stacked_p[pos_block]]
  transfers between devices with their start and end apart: 5 -> 3, of which waited for: 2 -> 1; matrix products, arithmetic and copies ran while one was open for 3% -> 0% of each run, Pallas kernels for 0% -> 7%
where the time goes in v1:
time: 56.2 us; the launch traced here: 55.8 us
  starting transfers between devices  26.4 us (47%)
  blocking collectives  15.3 us (27%)
  local copies, waits for them, and re-layouts  5.82 us (10%)
  Pallas kernels  4.35 us (8%)
  other arithmetic  1.92 us (3%)
  waiting for transfers between devices  1.9 us (3%)
    ppermute x2, starting transfers between devices, halo(): lax.ppermute(block, 'dom', [(i, (i + step) % groups) for i in range(group...  23.6 us
    all_to_all x1, blocking collectives, local(): lax.all_to_all(chip.reshape(members // 2, -1, chip.shape[1]), 'sub', 0, 0...  15.3 us
    unnamed x10, local copies, waits for them, and re-layouts  4.53 us
    pallas_call x1, Pallas kernels, local(): pl.pallas_call(functools.partial(front_kernel, groups, members), out_shap...  3.87 us
    ppermute x1, starting transfers between devices, local(): other = lax.ppermute(send, 'sub', [(i, i ^ 1) for i in range(members)])  2.85 us
    ppermute x1, waiting for transfers between devices, local(): other = lax.ppermute(send, 'sub', [(i, i ^ 1) for i in range(members)])  1.89 us
  transfers between devices with their start and end apart: 3, of which 1 were waited for; matrix products, arithmetic and copies ran while one was open for 0% of the time, Pallas kernels for 7%

profile of v1, /device:TPU:1, one launch (start us, length us, event | category | flops | bytes accessed | tf_op | source)
XLA Modules:
  0.0 55.8 jit_solution(2163432853017937675)
XLA Ops:
  0.0 0.7 %subtract_convert_fusion = bf16[8]{0:T(256)(128)(2,1)S(1)} fusion(s32[8]{0:T(128)} %agg_ref.1, s32[]{:T(128)S(6)} %mul.3), kind=kLoop, calls=%fused_computation.4 | loop fusion | flops 16 | bytes 52 | tf_op jit(solution)/shard_map/convert_element_type | solution.py:86
  0.7 0.1 fusion.1
  0.7 0.1 broadcast_in_dim.23
  0.8 0.1 reshape.19
  0.9 0.9 %fusion = (bf16[2,128,128]{2,1,0:T(8,128)(2,1)S(1)}, bf16[2,128,128]{2,1,0:T(8,128)(2,1)S(1)}) fusion(bf16[8,128,128]{2,1,0:T(8,128)(2,1)} %p_ref.1), kind=kLoop, calls=%fused_computation.5 | loop fusion | bytes 262144 | tf_op jit(solution)/shard_map/slice | solution.py:90
  1.8 0.1 pad_maximum_fusion.1
  1.9 21.7 %collective-permute-start.1 = (bf16[288,128]{1,0:T(8,128)(2,1)S(1)}, bf16[288,128]{1,0:T(8,128)(2,1)S(1)}, u32[]{:S(2)}, u32[]{:S(2)}) collective-permute-start(bf16[288,128]{1,0:T(8,128)(2,1)S(1)} %pad_maximum_fusion.1), channel_id=1, source_target_pairs={{0,1016},{8,0},{16,8},{24,16},{32,24},{40,32},{48,40},{56,48},{64,... | collective-permute-start | bytes 221192 | tf_op jit(solution)/shard_map/ppermute | solution.py:91
  23.6 0.1 broadcast_in_dim.20
  23.7 0.1 reshape.18
  23.8 0.1 pad_maximum_fusion
  23.9 1.9 %collective-permute-start = (bf16[288,128]{1,0:T(8,128)(2,1)S(1)}, bf16[288,128]{1,0:T(8,128)(2,1)S(1)}, u32[]{:S(2)}, u32[]{:S(2)}) collective-permute-start(bf16[288,128]{1,0:T(8,128)(2,1)S(1)} %pad_maximum_fusion), channel_id=1, source_target_pairs={{0,8},{8,16},{16,24},{24,32},{32,40},{40,48},{48,56},{56,64},{64,7... | collective-permute-start | bytes 221192 | tf_op jit(solution)/shard_map/ppermute | solution.py:91
  25.8 0.0 copy-start
  25.8 0.9 %copy-done = bf16[8,128,128]{2,1,0:T(8,128)(2,1)S(1)} copy-done((bf16[8,128,128]{2,1,0:T(8,128)(2,1)S(1)}, bf16[8,128,128]{2,1,0:T(8,128)(2,1)}, u32[]{:S(2)}) %copy-start) | copy-done | bytes 262168
  26.8 1.6 %copy-done.1 = bf16[8,8,128,128]{3,2,1,0:T(8,128)(2,1)S(1)} copy-done((bf16[8,8,128,128]{3,2,1,0:T(8,128)(2,1)S(1)}, bf16[8,8,128,128]{3,2,1,0:T(8,128)(2,1)}, u32[]{:S(2)}) %copy-start.1) | copy-done | bytes 2097176
  28.3 0.7 %copy-done.2 = s32[8,8]{1,0:T(8,128)S(1)} copy-done((s32[8,8]{1,0:T(8,128)S(1)}, s32[8,8]{1,0:T(8,128)}, u32[]{:S(2)}) %copy-start.2) | copy-done | bytes 280
  29.0 0.7 %copy-done.3 = s32[8]{0:T(128)S(1)} copy-done((s32[8]{0:T(128)S(1)}, s32[8]{0:T(128)}, u32[]{:S(2)}) %copy-start.3) | copy-done | bytes 56
  29.7 0.7 %copy-done.4 = s32[8]{0:T(128)S(1)} copy-done((s32[8]{0:T(128)S(1)}, s32[8]{0:T(128)}, u32[]{:S(2)}) %copy-start.4) | copy-done | bytes 56
  30.3 3.9 %front.1 = (bf16[512,512]{1,0:T(8,128)(2,1)S(1)}, bf16[512,512]{1,0:T(8,128)(2,1)S(1)}) custom-call(s32[8,8]{1,0:T(8,128)S(1)} %copy-done.2, s32[8]{0:T(128)S(1)} %copy-done.3, s32[8]{0:T(128)S(1)} %copy-done.4, bf16[8,8,128,128]{3,2,1,0:T(8,128)(2,1)S(1)} %copy-done.1, bf16[8,128,128]{2,1,0:T(8,128)(2,1)S(1)} %copy-done), custom_call_target="tpu_custom_call" | custom-call | flops 2000000000 | bytes 4194304 | tf_op jit(solution)/shard_map/front/pallas_call | solution.py:98
  34.2 0.5 back.1
  34.7 2.9 %collective-permute-start.2 = (bf16[256,1536]{1,0:T(8,128)(2,1)S(1)}, bf16[256,1536]{1,0:T(8,128)(2,1)S(1)}, u32[]{:S(2)}, u32[]{:S(2)}) collective-permute-start(bf16[256,1536]{1,0:T(8,128)(2,1)S(1)} %get-tuple-element.12), channel_id=1, source_target_pairs={{0,1},{1,0},{2,3},{3,2},{4,5},{5,4},{6,7},{7,6},{8,9},{9,8},{10,11... | collective-permute-start | bytes 2359304 | tf_op jit(solution)/shard_map/ppermute | solution.py:129
  37.6 1.9 %collective-permute-done.2 = bf16[256,1536]{1,0:T(8,128)(2,1)S(1)} collective-permute-done((bf16[256,1536]{1,0:T(8,128)(2,1)S(1)}, bf16[256,1536]{1,0:T(8,128)(2,1)S(1)}, u32[]{:S(2)}, u32[]{:S(2)}) %collective-permute-start.2) | collective-permute-done | bytes 786464 | tf_op jit(solution)/shard_map/ppermute | solution.py:129
  39.5 0.2 add_convert_fusion
  39.7 15.3 %all_to_all.5 = bf16[4,64,1536]{2,1,0:T(8,128)(2,1)S(1)} all-to-all(bf16[4,64,1536]{2,1,0:T(8,128)(2,1)S(1)} %bitcast.3), channel_id=1, replica_groups={{0,2,4,6},{1,3,5,7},{8,10,12,14},{9,11,13,15},{16,18,20,22},{17,19,21,2..., dimensions={0} | all-to-all | bytes 1572864 | tf_op jit(solution)/shard_map/all_to_all | solution.py:132
  54.9 0.9 %convert_reduce_fusion = f32[64,1536]{1,0:T(8,128)} fusion(bf16[4,64,1536]{2,1,0:T(8,128)(2,1)S(1)} %all_to_all.5), kind=kLoop, calls=%fused_computation | loop fusion | flops 688128 | bytes 1179648 | tf_op jit(solution)/shard_map/reduce_sum | solution.py:133
  (8 shorter events, 0.0 us)
Async XLA Ops:
  1.9 32.3 %collective-permute-start.1 = (bf16[288,128]{1,0:T(8,128)(2,1)S(1)}, bf16[288,128]{1,0:T(8,128)(2,1)S(1)}, u32[]{:S(2)}, u32[]{:S(2)}) collective-permute-start(bf16[288,128]{1,0:T(8,128)(2,1)S(1)} %pad_maximum_fusion.1), channel_id=1, source_target_pairs={{0,1016},{8,0},{16,8},{24,16},{32,24},{40,32},{48,40},{56,48},{64,... | collective-permute-start | bytes 221192 | tf_op jit(solution)/shard_map/ppermute | solution.py:91
  23.9 10.4 %collective-permute-start = (bf16[288,128]{1,0:T(8,128)(2,1)S(1)}, bf16[288,128]{1,0:T(8,128)(2,1)S(1)}, u32[]{:S(2)}, u32[]{:S(2)}) collective-permute-start(bf16[288,128]{1,0:T(8,128)(2,1)S(1)} %pad_maximum_fusion), channel_id=1, source_target_pairs={{0,8},{8,16},{16,24},{24,32},{32,40},{40,48},{48,56},{56,64},{64,7... | collective-permute-start | bytes 221192 | tf_op jit(solution)/shard_map/ppermute | solution.py:91
  25.8 1.0 %copy-start = (bf16[8,128,128]{2,1,0:T(8,128)(2,1)S(1)}, bf16[8,128,128]{2,1,0:T(8,128)(2,1)}, u32[]{:S(2)}) copy-start(bf16[8,128,128]{2,1,0:T(8,128)(2,1)} %p_ref.1) | copy-start | bytes 786436
  26.8 1.6 %copy-start.1 = (bf16[8,8,128,128]{3,2,1,0:T(8,128)(2,1)S(1)}, bf16[8,8,128,128]{3,2,1,0:T(8,128)(2,1)}, u32[]{:S(2)}) copy-start(bf16[8,8,128,128]{3,2,1,0:T(8,128)(2,1)} %a_hbm.1) | copy-start | bytes 6291460
  28.3 0.7 %copy-start.2 = (s32[8,8]{1,0:T(8,128)S(1)}, s32[8,8]{1,0:T(8,128)}, u32[]{:S(2)}) copy-start(s32[8,8]{1,0:T(8,128)} %col_ref.1) | copy-start | bytes 772
  29.0 0.7 %copy-start.3 = (s32[8]{0:T(128)S(1)}, s32[8]{0:T(128)}, u32[]{:S(2)}) copy-start(s32[8]{0:T(128)} %count_ref.1) | copy-start | bytes 100
  29.7 0.7 %copy-start.4 = (s32[8]{0:T(128)S(1)}, s32[8]{0:T(128)}, u32[]{:S(2)}) copy-start(s32[8]{0:T(128)} %agg_ref.1) | copy-start | bytes 100
  34.7 4.7 %collective-permute-start.2 = (bf16[256,1536]{1,0:T(8,128)(2,1)S(1)}, bf16[256,1536]{1,0:T(8,128)(2,1)S(1)}, u32[]{:S(2)}, u32[]{:S(2)}) collective-permute-start(bf16[256,1536]{1,0:T(8,128)(2,1)S(1)} %get-tuple-element.12), channel_id=1, source_target_pairs={{0,1},{1,0},{2,3},{3,2},{4,5},{5,4},{6,7},{7,6},{8,9},{9,8},{10,11... | collective-permute-start | bytes 2359304 | tf_op jit(solution)/shard_map/ppermute | solution.py:129

commit v2 on v1

--- a/solution.py
+++ b/solution.py
@@ -10,9 +10,10 @@
 CG = 4
 HALO = 2
 MARK = 16
+CORE = 64
 
 
-def front_kernel(groups, members, col_ref, count_ref, agg_ref, a_hbm, p_ref, g_ref, own_ref, a_ref, acc_ref, gown_ref, place_ref, sems):
+def front_kernel(table_ref, a_hbm, p_ref, g_ref, own_ref, a_ref, acc_ref, gown_ref, place_ref, sems):
     rows, slots, tile = a_hbm.shape[0], a_hbm.shape[1], a_hbm.shape[2]
     columns = rows + 2 * HALO
     half = tile // 2
@@ -20,28 +21,19 @@
     for copy in copies:
         copy.start()
     acc_ref[...] = jnp.zeros_like(acc_ref)
-    device = col_ref[0, 0] // rows
-    my_group = device // members
-    core = device % 2
+    core = table_ref[0, 0] // CORE
     for r in range(rows):
-        coarse = agg_ref[r] - my_group * CG
+        coarse = lax.rem(table_ref[r, 0], CORE) // columns
         for j in range(CG):
             place_ref[pl.ds(r * tile, tile), pl.ds(j * tile, tile)] = jnp.where(coarse == j, p_ref[r], jnp.zeros_like(p_ref[r]))
     for t in range(rows):
-        coarse = agg_ref[t] - my_group * CG
         p_t = p_ref[t].T
         copies[t].wait()
         for pair in range(slots // 2):
             both = jnp.concatenate([a_ref[t, 2 * pair], a_ref[t, 2 * pair + 1]], axis=1)
             terms = jnp.dot(p_t, both, preferred_element_type=jnp.float32)
             for side in range(2):
-                k = 2 * pair + side
-                column = col_ref[t, k]
-                side_of = column // (rows * members) - my_group + 1 + groups
-                side_of = lax.rem(side_of, groups)
-                near = lax.rem(column, rows) + rows * side_of - (rows - HALO)
-                at = jnp.where(k < count_ref[t], coarse * columns + near, CG * columns)
-                at = jnp.clip(at, 0, CG * columns)
+                at = lax.rem(table_ref[t, 2 * pair + side], CORE)
                 acc_ref[at] += terms[:, side * tile : (side + 1) * tile]
     for i in range(CG):
         for part in range(2):
@@ -59,12 +51,12 @@
 
 
 def back_kernel(g_ref, own_ref, before_ref, ahead_ref, out_ref, send_ref, place_ref):
-    tile = before_ref.shape[1]
+    tile = before_ref.shape[2]
     rows = out_ref.shape[0]
     for side, halo_ref in enumerate((before_ref, ahead_ref)):
         for r in range(HALO):
-            block = halo_ref[pl.ds(r * tile, tile), :]
-            mark = halo_ref[pl.ds(HALO * tile + r * MARK, MARK), :].astype(jnp.float32)[0:1, :]
+            block = halo_ref[r, pl.ds(0, tile), :]
+            mark = halo_ref[r, pl.ds(tile, MARK), :].astype(jnp.float32)[0:1, :]
             for j in range(CG):
                 chosen = jnp.where(mark == float(j), 1.0, 0.0).astype(jnp.bfloat16)
                 place_ref[side, pl.ds(r * tile, tile), pl.ds(j * tile, tile)] = block * chosen
@@ -82,26 +74,31 @@
 def local(groups, members, a_tiles, col_tiles, counts, aggregate, p_tiles):
     rows, slots, tile = a_tiles.shape[0], a_tiles.shape[1], a_tiles.shape[2]
     columns = rows + 2 * HALO
-    my_group = lax.axis_index("dom")
-    coarse = (aggregate - my_group * CG).astype(jnp.bfloat16)
+    coarse = lax.rem(aggregate, CG)
+    marks = coarse.astype(jnp.bfloat16)
 
     def halo(first, step):
-        marks = jnp.broadcast_to(coarse[first : first + HALO, None, None], (HALO, MARK, tile)).reshape(HALO * MARK, tile)
-        block = jnp.concatenate([p_tiles[first : first + HALO].reshape(HALO * tile, tile), marks], axis=0)
+        inside = lax.broadcasted_iota(jnp.int32, (HALO, tile + MARK, tile), 1) < tile
+        block = jnp.pad(p_tiles[first : first + HALO], ((0, 0), (0, MARK), (0, 0)))
+        block = jnp.where(inside, block, marks[first : first + HALO, None, None])
         return lax.ppermute(block, "dom", [(i, (i + step) % groups) for i in range(groups)])
 
     before = halo(rows - HALO, 1)
     ahead = halo(0, -1)
 
-    smem = pl.BlockSpec(memory_space=pltpu.SMEM)
     vmem = pl.BlockSpec(memory_space=pltpu.VMEM)
+    side = lax.rem(col_tiles // (rows * members) - (lax.axis_index("dom") - 1 - groups), groups)
+    near = coarse[:, None] * columns + lax.rem(col_tiles, rows) + rows * side - (rows - HALO)
+    live = lax.broadcasted_iota(jnp.int32, col_tiles.shape, 1) < counts[:, None]
+    table = jnp.clip(jnp.where(live, near, CG * columns), 0, CG * columns) + CORE * lax.rem(lax.axis_index("sub"), 2)
+
     g, own = pl.pallas_call(
-        functools.partial(front_kernel, groups, members),
+        front_kernel,
         out_shape=(
             jax.ShapeDtypeStruct((CG * tile, 2 * HALO * tile), jnp.bfloat16),
             jax.ShapeDtypeStruct((CG * tile, CG * tile), jnp.bfloat16),
         ),
-        in_specs=[smem, smem, smem, pl.BlockSpec(memory_space=pl.ANY), vmem],
+        in_specs=[pl.BlockSpec(memory_space=pltpu.SMEM), pl.BlockSpec(memory_space=pl.ANY), vmem],
         out_specs=(vmem, vmem),
         scratch_shapes=[
             pltpu.VMEM(a_tiles.shape, jnp.bfloat16),
@@ -110,10 +107,10 @@
             pltpu.VMEM((rows * tile, CG * tile), jnp.bfloat16),
             pltpu.SemaphoreType.DMA((rows,)),
         ],
-        compiler_params=pltpu.CompilerParams(vmem_limit_bytes=24 * 2**20),
+        compiler_params=pltpu.CompilerParams(vmem_limit_bytes=52 * 2**20),
         cost_estimate=pl.CostEstimate(flops=2 * 10**9, bytes_accessed=4 * 2**20, transcendentals=0),
         name="front",
-    )(col_tiles, counts, aggregate, a_tiles, p_tiles)
+    )(table, a_tiles, p_tiles)
 
     share = CG * tile // 2
     keep, send = pl.pallas_call(

time: 56.2 us -> 54.9 us (0.977)
  local copies, waits for them, and re-layouts: 5.82 us -> 1.91 us
  starting transfers between devices: 26.4 us -> 27.6 us
  Pallas kernels: 4.35 us -> 5.07 us
  other arithmetic: 1.92 us -> 2.61 us
    unnamed x10 -> x2, local copies, waits for them, and re-layouts: 4.53 us -> 0.95 us
    ppermute x1, starting transfers between devices: 2.85 us -> 4.01 us  [local(): other = lax.ppermute(send, 'sub', [(i, i ^ 1) for i in range(members)])]
    add x0 -> x1, other arithmetic: none -> 0.77 us  [local(): jnp.clip(jnp.where(live, near, CG * columns), 0, CG * columns)]
    pallas_call x1, Pallas kernels: 3.87 us -> 4.59 us  [local(): pl.pallas_call(front_kernel, out_shape=(jax.ShapeDtypeStruct((CG * tile,...]
  transfers between devices with their start and end apart: 3 -> 3, of which waited for: 1 -> 2; matrix products, arithmetic and copies ran while one was open for 0% -> 1% of each run, Pallas kernels for 7% -> 8%
where the time goes in v2:
time: 54.9 us; the launch traced here: 54.6 us
  starting transfers between devices  27.6 us (50%)
  blocking collectives  15.2 us (28%)
  Pallas kernels  5.07 us (9%)
  other arithmetic  2.61 us (5%)
  waiting for transfers between devices  2.03 us (4%)
  local copies, waits for them, and re-layouts  1.91 us (3%)
    ppermute x2, starting transfers between devices, halo(): lax.ppermute(block, 'dom', [(i, (i + step) % groups) for i in range(group...  23.6 us
    all_to_all x1, blocking collectives, local(): lax.all_to_all(chip.reshape(members // 2, -1, chip.shape[1]), 'sub', 0, 0...  15.2 us
    pallas_call x1, Pallas kernels, local(): pl.pallas_call(front_kernel, out_shape=(jax.ShapeDtypeStruct((CG * tile,...  4.59 us
    ppermute x1, starting transfers between devices, local(): other = lax.ppermute(send, 'sub', [(i, i ^ 1) for i in range(members)])  4.01 us
    ppermute x1, waiting for transfers between devices, local(): other = lax.ppermute(send, 'sub', [(i, i ^ 1) for i in range(members)])  1.89 us
  transfers between devices with their start and end apart: 3, of which 2 were waited for; matrix products, arithmetic and copies ran while one was open for 1% of the time, Pallas kernels for 8%

profile of v2, /device:TPU:1, one launch (start us, length us, event | category | flops | bytes accessed | tf_op | source)
XLA Modules:
  0.0 54.6 jit_solution(3757110838748340890)
XLA Ops:
  0.0 0.7 %fusion.12 = (bf16[8]{0:T(256)(128)(2,1)S(1)}, s32[8]{0:T(128)S(1)}) fusion(s32[8]{0:T(128)} %param.8), kind=kLoop, calls=%fused_computation.29 | loop fusion | flops 56 | bytes 80 | tf_op jit(solution)/shard_map/convert_element_type | solution.py:78
  0.7 0.1 fusion.14
  0.7 0.9 %fusion.13 = (bf16[2,128,128]{2,1,0:T(8,128)(2,1)S(1)}, bf16[2,128,128]{2,1,0:T(8,128)(2,1)S(1)}) fusion(bf16[8,128,128]{2,1,0:T(8,128)(2,1)} %p_ref.1), kind=kLoop, calls=%fused_computation.30 | loop fusion | bytes 262144 | tf_op jit(solution)/shard_map/slice | solution.py:82
  1.6 0.1 pad_select_fusion
  1.8 21.7 %collective-permute-start.1 = (bf16[2,144,128]{2,1,0:T(8,128)(2,1)S(1)}, bf16[2,144,128]{2,1,0:T(8,128)(2,1)S(1)}, u32[]{:S(2)}, u32[]{:S(2)}) collective-permute-start(bf16[2,144,128]{2,1,0:T(8,128)(2,1)S(1)} %get-tuple-element.17), channel_id=1, source_target_pairs={{0,1016},{8,0},{16,8},{24,16},{32,24},{40,32},{48,40},{56,48},{64,... | collective-permute-start | bytes 221192 | tf_op jit(solution)/shard_map/ppermute | solution.py:84
  23.4 1.9 %collective-permute-start = (bf16[2,144,128]{2,1,0:T(8,128)(2,1)S(1)}, bf16[2,144,128]{2,1,0:T(8,128)(2,1)S(1)}, u32[]{:S(2)}, u32[]{:S(2)}) collective-permute-start(bf16[2,144,128]{2,1,0:T(8,128)(2,1)S(1)} %get-tuple-element.18), channel_id=1, source_target_pairs={{0,8},{8,16},{16,24},{24,32},{32,40},{40,48},{48,56},{56,64},{64,7... | collective-permute-start | bytes 221192 | tf_op jit(solution)/shard_map/ppermute | solution.py:84
  25.4 0.8 %fusion.5.table_ref = s32[8,8]{1,0:T(8,128)S(1)} fusion(s32[8,8]{1,0:T(8,128)} %param.6, s32[]{:T(128)S(6)} %mul.12, s32[]{:T(128)S(6)} %sub.21, s32[8]{0:T(128)S(1)} %broadcast_multiply_fusion, s32[8]{0:T(128)} %param.7), kind=kLoop, calls=%fused_computation.16 | loop fusion | flops 2112 | bytes 584 | tf_op jit(solution)/shard_map/add | solution.py:93
  26.2 0.0 copy-start
  26.2 0.9 %copy-done = bf16[8,128,128]{2,1,0:T(8,128)(2,1)S(1)} copy-done((bf16[8,128,128]{2,1,0:T(8,128)(2,1)S(1)}, bf16[8,128,128]{2,1,0:T(8,128)(2,1)}, u32[]{:S(2)}) %copy-start) | copy-done | bytes 262168
  27.1 4.6 %front.1 = (bf16[512,512]{1,0:T(8,128)(2,1)S(1)}, bf16[512,512]{1,0:T(8,128)(2,1)S(1)}) custom-call(s32[8,8]{1,0:T(8,128)S(1)} %fusion.5.table_ref, bf16[8,8,128,128]{3,2,1,0:T(8,128)(2,1)} %a_hbm.1, bf16[8,128,128]{2,1,0:T(8,128)(2,1)S(1)} %copy-done), custom_call_target="tpu_custom_call" | custom-call | flops 2000000000 | bytes 4194304 | tf_op jit(solution)/shard_map/front/pallas_call | solution.py:95
  31.7 0.0 collective-permute-done.1.ahead_ref
  31.7 0.1 collective-permute-done.before_ref
  31.9 0.5 back.1
  32.4 4.0 %collective-permute-start.2 = (bf16[256,1536]{1,0:T(8,128)(2,1)S(1)}, bf16[256,1536]{1,0:T(8,128)(2,1)S(1)}, u32[]{:S(2)}, u32[]{:S(2)}) collective-permute-start(bf16[256,1536]{1,0:T(8,128)(2,1)S(1)} %get-tuple-element.12), channel_id=1, source_target_pairs={{0,1},{1,0},{2,3},{3,2},{4,5},{5,4},{6,7},{7,6},{8,9},{9,8},{10,11... | collective-permute-start | bytes 2359304 | tf_op jit(solution)/shard_map/ppermute | solution.py:126
  36.4 1.9 %collective-permute-done.2 = bf16[256,1536]{1,0:T(8,128)(2,1)S(1)} collective-permute-done((bf16[256,1536]{1,0:T(8,128)(2,1)S(1)}, bf16[256,1536]{1,0:T(8,128)(2,1)S(1)}, u32[]{:S(2)}, u32[]{:S(2)}) %collective-permute-start.2) | collective-permute-done | bytes 786464 | tf_op jit(solution)/shard_map/ppermute | solution.py:126
  38.3 0.2 add_convert_fusion
  38.5 15.2 %all_to_all.5 = bf16[4,64,1536]{2,1,0:T(8,128)(2,1)S(1)} all-to-all(bf16[4,64,1536]{2,1,0:T(8,128)(2,1)S(1)} %bitcast.1), channel_id=1, replica_groups={{0,2,4,6},{1,3,5,7},{8,10,12,14},{9,11,13,15},{16,18,20,22},{17,19,21,2..., dimensions={0} | all-to-all | bytes 1572864 | tf_op jit(solution)/shard_map/all_to_all | solution.py:129
  53.7 0.9 %convert_reduce_fusion = f32[64,1536]{1,0:T(8,128)} fusion(bf16[4,64,1536]{2,1,0:T(8,128)(2,1)S(1)} %all_to_all.5), kind=kLoop, calls=%fused_computation | loop fusion | flops 688128 | bytes 1179648 | tf_op jit(solution)/shard_map/reduce_sum | solution.py:130
  (2 shorter events, 0.0 us)
Async XLA Ops:
  1.8 30.0 %collective-permute-start.1 = (bf16[2,144,128]{2,1,0:T(8,128)(2,1)S(1)}, bf16[2,144,128]{2,1,0:T(8,128)(2,1)S(1)}, u32[]{:S(2)}, u32[]{:S(2)}) collective-permute-start(bf16[2,144,128]{2,1,0:T(8,128)(2,1)S(1)} %get-tuple-element.17), channel_id=1, source_target_pairs={{0,1016},{8,0},{16,8},{24,16},{32,24},{40,32},{48,40},{56,48},{64,... | collective-permute-start | bytes 221192 | tf_op jit(solution)/shard_map/ppermute | solution.py:84
  23.4 8.4 %collective-permute-start = (bf16[2,144,128]{2,1,0:T(8,128)(2,1)S(1)}, bf16[2,144,128]{2,1,0:T(8,128)(2,1)S(1)}, u32[]{:S(2)}, u32[]{:S(2)}) collective-permute-start(bf16[2,144,128]{2,1,0:T(8,128)(2,1)S(1)} %get-tuple-element.18), channel_id=1, source_target_pairs={{0,8},{8,16},{16,24},{24,32},{32,40},{40,48},{48,56},{56,64},{64,7... | collective-permute-start | bytes 221192 | tf_op jit(solution)/shard_map/ppermute | solution.py:84
  26.2 1.0 %copy-start = (bf16[8,128,128]{2,1,0:T(8,128)(2,1)S(1)}, bf16[8,128,128]{2,1,0:T(8,128)(2,1)}, u32[]{:S(2)}) copy-start(bf16[8,128,128]{2,1,0:T(8,128)(2,1)} %p_ref.1) | copy-start | bytes 786436
  32.4 5.9 %collective-permute-start.2 = (bf16[256,1536]{1,0:T(8,128)(2,1)S(1)}, bf16[256,1536]{1,0:T(8,128)(2,1)S(1)}, u32[]{:S(2)}, u32[]{:S(2)}) collective-permute-start(bf16[256,1536]{1,0:T(8,128)(2,1)S(1)} %get-tuple-element.12), channel_id=1, source_target_pairs={{0,1},{1,0},{2,3},{3,2},{4,5},{5,4},{6,7},{7,6},{8,9},{9,8},{10,11... | collective-permute-start | bytes 2359304 | tf_op jit(solution)/shard_map/ppermute | solution.py:126

commit v3 on v2

--- a/solution.py
+++ b/solution.py
@@ -13,7 +13,7 @@
 CORE = 64
 
 
-def front_kernel(table_ref, a_hbm, p_ref, g_ref, own_ref, a_ref, acc_ref, gown_ref, place_ref, sems):
+def front_kernel(table_ref, a_hbm, block_ref, g_ref, own_ref, a_ref, acc_ref, gown_ref, place_ref, pt_ref, sems):
     rows, slots, tile = a_hbm.shape[0], a_hbm.shape[1], a_hbm.shape[2]
     columns = rows + 2 * HALO
     half = tile // 2
@@ -24,14 +24,17 @@
     core = table_ref[0, 0] // CORE
     for r in range(rows):
         coarse = lax.rem(table_ref[r, 0], CORE) // columns
+        p_r = block_ref[r, pl.ds(0, tile), :]
+        pt_ref[r] = p_r.T
         for j in range(CG):
-            place_ref[pl.ds(r * tile, tile), pl.ds(j * tile, tile)] = jnp.where(coarse == j, p_ref[r], jnp.zeros_like(p_ref[r]))
+            place_ref[pl.ds(r * tile, tile), pl.ds(j * tile, tile)] = jnp.where(coarse == j, p_r, jnp.zeros_like(p_r))
     for t in range(rows):
-        p_t = p_ref[t].T
-        copies[t].wait()
+        if t % (rows // 2) == 0:
+            for copy in copies[t : t + rows // 2]:
+                copy.wait()
         for pair in range(slots // 2):
             both = jnp.concatenate([a_ref[t, 2 * pair], a_ref[t, 2 * pair + 1]], axis=1)
-            terms = jnp.dot(p_t, both, preferred_element_type=jnp.float32)
+            terms = jnp.dot(pt_ref[t], both, preferred_element_type=jnp.float32)
             for side in range(2):
                 at = lax.rem(table_ref[t, 2 * pair + side], CORE)
                 acc_ref[at] += terms[:, side * tile : (side + 1) * tile]
@@ -50,16 +53,16 @@
     own_ref[...] = jnp.dot(gown_ref[...], place_ref[...], preferred_element_type=jnp.float32).astype(jnp.bfloat16)
 
 
-def back_kernel(g_ref, own_ref, before_ref, ahead_ref, out_ref, send_ref, place_ref):
-    tile = before_ref.shape[2]
+def back_kernel(g_ref, own_ref, first_ref, second_ref, out_ref, send_ref, place_ref):
+    tile = first_ref.shape[2]
     rows = out_ref.shape[0]
-    for side, halo_ref in enumerate((before_ref, ahead_ref)):
-        for r in range(HALO):
-            block = halo_ref[r, pl.ds(0, tile), :]
-            mark = halo_ref[r, pl.ds(tile, MARK), :].astype(jnp.float32)[0:1, :]
+    for r in range(HALO):
+        tiles = [ref[r, pl.ds(0, tile), :] for ref in (first_ref, second_ref)]
+        marks = [ref[r, pl.ds(tile, MARK), :].astype(jnp.float32)[0:1, :] for ref in (first_ref, second_ref)]
+        for side in range(2):
             for j in range(CG):
-                chosen = jnp.where(mark == float(j), 1.0, 0.0).astype(jnp.bfloat16)
-                place_ref[side, pl.ds(r * tile, tile), pl.ds(j * tile, tile)] = block * chosen
+                chosen = [jnp.where(mark == float(side * CG + j), 1.0, 0.0).astype(jnp.bfloat16) for mark in marks]
+                place_ref[side, pl.ds(r * tile, tile), pl.ds(j * tile, tile)] = tiles[0] * chosen[0] + tiles[1] * chosen[1]
     width = CG * tile
     for side in range(2):
         depth = HALO * tile
@@ -75,23 +78,25 @@
     rows, slots, tile = a_tiles.shape[0], a_tiles.shape[1], a_tiles.shape[2]
     columns = rows + 2 * HALO
     coarse = lax.rem(aggregate, CG)
-    marks = coarse.astype(jnp.bfloat16)
-
-    def halo(first, step):
-        inside = lax.broadcasted_iota(jnp.int32, (HALO, tile + MARK, tile), 1) < tile
-        block = jnp.pad(p_tiles[first : first + HALO], ((0, 0), (0, MARK), (0, 0)))
-        block = jnp.where(inside, block, marks[first : first + HALO, None, None])
-        return lax.ppermute(block, "dom", [(i, (i + step) % groups) for i in range(groups)])
-
-    before = halo(rows - HALO, 1)
-    ahead = halo(0, -1)
-
-    vmem = pl.BlockSpec(memory_space=pltpu.VMEM)
     side = lax.rem(col_tiles // (rows * members) - (lax.axis_index("dom") - 1 - groups), groups)
     near = coarse[:, None] * columns + lax.rem(col_tiles, rows) + rows * side - (rows - HALO)
     live = lax.broadcasted_iota(jnp.int32, col_tiles.shape, 1) < counts[:, None]
     table = jnp.clip(jnp.where(live, near, CG * columns), 0, CG * columns) + CORE * lax.rem(lax.axis_index("sub"), 2)
 
+    marks = coarse + jnp.where(lax.iota(jnp.int32, rows) < HALO, CG, 0)
+    inside = lax.broadcasted_iota(jnp.int32, (rows, tile + MARK, tile), 1) < tile
+    block = jnp.where(inside, jnp.pad(p_tiles, ((0, 0), (0, MARK), (0, 0))), marks.astype(jnp.bfloat16)[:, None, None])
+
+    even = lax.rem(lax.axis_index("dom"), 2) == 0
+    halos = []
+    for turn in range(2):
+        start = jnp.where(even == (turn == 0), rows - HALO, 0)
+        route = []
+        for i in range(turn, groups + turn, 2):
+            route += [(i % groups, (i + 1) % groups), ((i + 1) % groups, i % groups)]
+        halos.append(lax.ppermute(lax.dynamic_slice_in_dim(block, start, HALO), "dom", route))
+
+    vmem = pl.BlockSpec(memory_space=pltpu.VMEM)
     g, own = pl.pallas_call(
         front_kernel,
         out_shape=(
@@ -105,12 +110,13 @@
             pltpu.VMEM((CG * columns + 1, tile, tile), jnp.float32),
             pltpu.VMEM((CG * tile, rows * tile), jnp.bfloat16),
             pltpu.VMEM((rows * tile, CG * tile), jnp.bfloat16),
+            pltpu.VMEM(p_tiles.shape, jnp.bfloat16),
             pltpu.SemaphoreType.DMA((rows,)),
         ],
         compiler_params=pltpu.CompilerParams(vmem_limit_bytes=52 * 2**20),
         cost_estimate=pl.CostEstimate(flops=2 * 10**9, bytes_accessed=4 * 2**20, transcendentals=0),
         name="front",
-    )(table, a_tiles, p_tiles)
+    )(table, a_tiles, block)
 
     share = CG * tile // 2
     keep, send = pl.pallas_call(
@@ -122,7 +128,7 @@
         compiler_params=pltpu.CompilerParams(vmem_limit_bytes=24 * 2**20),
         cost_estimate=pl.CostEstimate(flops=3 * 10**8, bytes_accessed=3 * 2**20, transcendentals=0),
         name="back",
-    )(g, own, before, ahead)
+    )(g, own, *halos)
     other = lax.ppermute(send, "sub", [(i, i ^ 1) for i in range(members)])
     chip = (keep.astype(jnp.float32) + other.astype(jnp.float32)).astype(jnp.bfloat16)
     cores = [list(range(core, members, 2)) for core in range(2)]

time: 54.9 us -> 52 us (0.947)
  local copies, waits for them, and re-layouts: 1.91 us -> 0.02 us
  starting transfers between devices: 27.6 us -> 26.5 us
  other arithmetic: 2.61 us -> 3.61 us
  Pallas kernels: 5.07 us -> 4.36 us
    ppermute x1, starting transfers between devices: 4.01 us -> 2.86 us  [local(): other = lax.ppermute(send, 'sub', [(i, i ^ 1) for i in range(members)])]
    select_n x1, other arithmetic: 0.12 us -> 1.11 us  [local(): jnp.where(inside, jnp.pad(p_tiles, ((0, 0), (0, MARK), (0, 0))), marks.as...]
    slice x2 -> x0, local copies, waits for them, and re-layouts: 0.96 us -> none  [the longest x1 0.88 us: halo(): block = jnp.pad(p_tiles[first:first + HALO], ((0, 0), (0, MARK), (0, 0)))]
    unnamed x2 -> x0, local copies, waits for them, and re-layouts: 0.95 us -> none
    pallas_call x1, Pallas kernels: 4.59 us -> 3.83 us  [local(): pl.pallas_call(front_kernel, out_shape=(jax.ShapeDtypeStruct((CG * tile,...]
  transfers between devices with their start and end apart: 3 -> 3, of which waited for: 2 -> 1; matrix products, arithmetic and copies ran while one was open for 1% -> 1% of each run, Pallas kernels for 8% -> 7%
where the time goes in v3:
time: 52 us; the launch traced here: 51.7 us
  starting transfers between devices  26.5 us (51%)
  blocking collectives  15.2 us (29%)
  Pallas kernels  4.36 us (8%)
  other arithmetic  3.61 us (7%)
  waiting for transfers between devices  1.9 us (4%)
    ppermute x2, starting transfers between devices, local(): lax.ppermute(lax.dynamic_slice_in_dim(block, start, HALO), 'dom', route)  23.6 us
    all_to_all x1, blocking collectives, local(): lax.all_to_all(chip.reshape(members // 2, -1, chip.shape[1]), 'sub', 0, 0...  15.2 us
    pallas_call x1, Pallas kernels, local(): pl.pallas_call(front_kernel, out_shape=(jax.ShapeDtypeStruct((CG * tile,...  3.83 us
    ppermute x1, starting transfers between devices, local(): other = lax.ppermute(send, 'sub', [(i, i ^ 1) for i in range(members)])  2.86 us
    ppermute x1, waiting for transfers between devices, local(): other = lax.ppermute(send, 'sub', [(i, i ^ 1) for i in range(members)])  1.89 us
    select_n x1, other arithmetic, local(): jnp.where(inside, jnp.pad(p_tiles, ((0, 0), (0, MARK), (0, 0))), marks.as...  1.11 us
  transfers between devices with their start and end apart: 3, of which 1 were waited for; matrix products, arithmetic and copies ran while one was open for 1% of the time, Pallas kernels for 7%

profile of v3, /device:TPU:1, one launch (start us, length us, event | category | flops | bytes accessed | tf_op | source)
XLA Modules:
  0.0 51.7 jit_solution(17073186739219523019)
XLA Ops:
  0.0 0.7 %fusion.13 = (bf16[8]{0:T(256)(128)(2,1)S(1)}, s32[8]{0:T(128)S(1)}) fusion(s32[8]{0:T(128)} %param.8), kind=kLoop, calls=%fused_computation.29 | loop fusion | flops 80 | bytes 80 | tf_op jit(solution)/shard_map/convert_element_type | solution.py:88
  0.7 1.1 %pad_select_fusion.block_ref = bf16[8,144,128]{2,1,0:T(8,128)(2,1)S(1)} fusion(bf16[8,128,128]{2,1,0:T(8,128)(2,1)} %param.9, pred[144]{0:T(512)(128)(4,1)S(1)} %iota_compare_fusion.1, bf16[8]{0:T(256)(128)(2,1)S(1)} %get-tuple-element.13), kind=kLoop, calls=%fused_computation.2 | loop fusion | flops 147456 | bytes 557216 | tf_op jit(solution)/shard_map/jit(_where)/select_n | solution.py:88
  1.8 21.7 %collective-permute-start.1 = (bf16[2,144,128]{2,1,0:T(8,128)(2,1)S(1)}, bf16[2,144,128]{2,1,0:T(8,128)(2,1)S(1)}, u32[]{:S(2)}, u32[]{:S(2)}) collective-permute-start(bf16[2,144,128]{2,1,0:T(8,128)(2,1)S(1)} %get-tuple-element.15), channel_id=1, source_target_pairs={{8,16},{16,8},{24,32},{32,24},{40,48},{48,40},{56,64},{64,56},{72,... | collective-permute-start | bytes 221192 | tf_op jit(solution)/shard_map/ppermute | solution.py:97
  23.5 1.9 %collective-permute-start = (bf16[2,144,128]{2,1,0:T(8,128)(2,1)S(1)}, bf16[2,144,128]{2,1,0:T(8,128)(2,1)S(1)}, u32[]{:S(2)}, u32[]{:S(2)}) collective-permute-start(bf16[2,144,128]{2,1,0:T(8,128)(2,1)S(1)} %get-tuple-element.16), channel_id=1, source_target_pairs={{0,8},{8,0},{16,24},{24,16},{32,40},{40,32},{48,56},{56,48},{64,72... | collective-permute-start | bytes 221192 | tf_op jit(solution)/shard_map/ppermute | solution.py:97
  25.5 0.8 %fusion.5.table_ref = s32[8,8]{1,0:T(8,128)S(1)} fusion(s32[8,8]{1,0:T(8,128)} %param.6, s32[]{:T(128)S(6)} %mul.12, s32[]{:T(128)S(6)} %sub.21, s32[8]{0:T(128)S(1)} %broadcast_multiply_fusion, s32[8]{0:T(128)} %param.7), kind=kLoop, calls=%fused_computation.15 | loop fusion | flops 2112 | bytes 584 | tf_op jit(solution)/shard_map/add | solution.py:84
  26.2 3.8 %front.1 = (bf16[512,512]{1,0:T(8,128)(2,1)S(1)}, bf16[512,512]{1,0:T(8,128)(2,1)S(1)}) custom-call(s32[8,8]{1,0:T(8,128)S(1)} %fusion.5.table_ref, bf16[8,8,128,128]{3,2,1,0:T(8,128)(2,1)} %a_hbm.1, bf16[8,144,128]{2,1,0:T(8,128)(2,1)S(1)} %pad_select_fusion.block_ref), custom_call_target="tpu_custom_call" | custom-call | flops 2000000000 | bytes 4194304 | tf_op jit(solution)/shard_map/front/pallas_call | solution.py:100
  30.1 0.0 collective-permute-done.1.second_ref
  30.1 0.0 collective-permute-done.first_ref
  30.1 0.5 %back.1 = (bf16[256,1536]{1,0:T(8,128)(2,1)S(1)}, bf16[256,1536]{1,0:T(8,128)(2,1)S(1)}) custom-call(bf16[512,512]{1,0:T(8,128)(2,1)S(1)} %get-tuple-element.9.g_ref, bf16[512,512]{1,0:T(8,128)(2,1)S(1)} %get-tuple-element.10.own_ref, bf16[2,144,128]{2,1,0:T(8,128)(2,1)S(1)} %collective-permute-done.first_ref, ...), custom_call_target="tpu_custom_call" | custom-call | flops 300000000 | bytes 3145728 | tf_op jit(solution)/shard_map/back/pallas_call | solution.py:122
  30.6 2.9 %collective-permute-start.2 = (bf16[256,1536]{1,0:T(8,128)(2,1)S(1)}, bf16[256,1536]{1,0:T(8,128)(2,1)S(1)}, u32[]{:S(2)}, u32[]{:S(2)}) collective-permute-start(bf16[256,1536]{1,0:T(8,128)(2,1)S(1)} %get-tuple-element.12), channel_id=1, source_target_pairs={{0,1},{1,0},{2,3},{3,2},{4,5},{5,4},{6,7},{7,6},{8,9},{9,8},{10,11... | collective-permute-start | bytes 2359304 | tf_op jit(solution)/shard_map/ppermute | solution.py:132
  33.5 1.9 %collective-permute-done.2 = bf16[256,1536]{1,0:T(8,128)(2,1)S(1)} collective-permute-done((bf16[256,1536]{1,0:T(8,128)(2,1)S(1)}, bf16[256,1536]{1,0:T(8,128)(2,1)S(1)}, u32[]{:S(2)}, u32[]{:S(2)}) %collective-permute-start.2) | collective-permute-done | bytes 786464 | tf_op jit(solution)/shard_map/ppermute | solution.py:132
  35.4 0.2 add_convert_fusion
  35.6 15.2 %all_to_all.5 = bf16[4,64,1536]{2,1,0:T(8,128)(2,1)S(1)} all-to-all(bf16[4,64,1536]{2,1,0:T(8,128)(2,1)S(1)} %bitcast.1), channel_id=1, replica_groups={{0,2,4,6},{1,3,5,7},{8,10,12,14},{9,11,13,15},{16,18,20,22},{17,19,21,2..., dimensions={0} | all-to-all | bytes 1572864 | tf_op jit(solution)/shard_map/all_to_all | solution.py:135
  50.8 0.9 %convert_reduce_fusion = f32[64,1536]{1,0:T(8,128)} fusion(bf16[4,64,1536]{2,1,0:T(8,128)(2,1)S(1)} %all_to_all.5), kind=kLoop, calls=%fused_computation | loop fusion | flops 688128 | bytes 1179648 | tf_op jit(solution)/shard_map/reduce_sum | solution.py:136
  (3 shorter events, 0.0 us)
Async XLA Ops:
  1.8 28.2 %collective-permute-start.1 = (bf16[2,144,128]{2,1,0:T(8,128)(2,1)S(1)}, bf16[2,144,128]{2,1,0:T(8,128)(2,1)S(1)}, u32[]{:S(2)}, u32[]{:S(2)}) collective-permute-start(bf16[2,144,128]{2,1,0:T(8,128)(2,1)S(1)} %get-tuple-element.15), channel_id=1, source_target_pairs={{8,16},{16,8},{24,32},{32,24},{40,48},{48,40},{56,64},{64,56},{72,... | collective-permute-start | bytes 221192 | tf_op jit(solution)/shard_map/ppermute | solution.py:97
  23.5 6.6 %collective-permute-start = (bf16[2,144,128]{2,1,0:T(8,128)(2,1)S(1)}, bf16[2,144,128]{2,1,0:T(8,128)(2,1)S(1)}, u32[]{:S(2)}, u32[]{:S(2)}) collective-permute-start(bf16[2,144,128]{2,1,0:T(8,128)(2,1)S(1)} %get-tuple-element.16), channel_id=1, source_target_pairs={{0,8},{8,0},{16,24},{24,16},{32,40},{40,32},{48,56},{56,48},{64,72... | collective-permute-start | bytes 221192 | tf_op jit(solution)/shard_map/ppermute | solution.py:97
  30.6 4.8 %collective-permute-start.2 = (bf16[256,1536]{1,0:T(8,128)(2,1)S(1)}, bf16[256,1536]{1,0:T(8,128)(2,1)S(1)}, u32[]{:S(2)}, u32[]{:S(2)}) collective-permute-start(bf16[256,1536]{1,0:T(8,128)(2,1)S(1)} %get-tuple-element.12), channel_id=1, source_target_pairs={{0,1},{1,0},{2,3},{3,2},{4,5},{5,4},{6,7},{7,6},{8,9},{9,8},{10,11... | collective-permute-start | bytes 2359304 | tf_op jit(solution)/shard_map/ppermute | solution.py:132

commit v4 on v3

--- a/solution.py
+++ b/solution.py
@@ -10,21 +10,49 @@
 CG = 4
 HALO = 2
 MARK = 16
-CORE = 64
 
 
-def front_kernel(table_ref, a_hbm, block_ref, g_ref, own_ref, a_ref, acc_ref, gown_ref, place_ref, pt_ref, sems):
+def pack_kernel(agg_hbm, p_hbm, first_ref, second_ref, agg_ref, ends_ref, sems):
+    rows, tile = p_hbm.shape[0], p_hbm.shape[1]
+    copies = [
+        pltpu.make_async_copy(agg_hbm, agg_ref, sems.at[0]),
+        pltpu.make_async_copy(p_hbm.at[pl.ds(0, HALO)], ends_ref.at[0], sems.at[1]),
+        pltpu.make_async_copy(p_hbm.at[pl.ds(rows - HALO, HALO)], ends_ref.at[1], sems.at[2]),
+    ]
+    for copy in copies:
+        copy.start()
+    for copy in copies:
+        copy.wait()
+    odd = lax.rem(agg_ref[0] // CG, 2)
+    for turn, ref in enumerate((first_ref, second_ref)):
+        tail = 1 - odd if turn == 0 else odd
+        for r in range(HALO):
+            mark = lax.rem(agg_ref[tail * (rows - HALO) + r], CG) + (1 - tail) * CG
+            ref[r, pl.ds(0, tile), :] = ends_ref[tail, r]
+            ref[r, pl.ds(tile, MARK), :] = jnp.full((MARK, tile), mark.astype(jnp.float32)).astype(jnp.bfloat16)
+
+
+def front_kernel(
+    groups, members, col_hbm, count_hbm, agg_hbm, a_hbm, p_hbm, g_ref, own_ref,
+    col_ref, count_ref, agg_ref, a_ref, p_ref, acc_ref, gown_ref, place_ref, pt_ref, sems, small_sems,
+):
     rows, slots, tile = a_hbm.shape[0], a_hbm.shape[1], a_hbm.shape[2]
     columns = rows + 2 * HALO
     half = tile // 2
     copies = [pltpu.make_async_copy(a_hbm.at[t], a_ref.at[t], sems.at[t]) for t in range(rows)]
-    for copy in copies:
+    pairs = ((col_hbm, col_ref), (count_hbm, count_ref), (agg_hbm, agg_ref), (p_hbm, p_ref))
+    small = [pltpu.make_async_copy(source, to, small_sems.at[i]) for i, (source, to) in enumerate(pairs)]
+    for copy in small + copies:
         copy.start()
     acc_ref[...] = jnp.zeros_like(acc_ref)
-    core = table_ref[0, 0] // CORE
+    for copy in small:
+        copy.wait()
+    device = col_ref[0, 0] // rows
+    my_group = device // members
+    core = lax.rem(device, 2)
     for r in range(rows):
-        coarse = lax.rem(table_ref[r, 0], CORE) // columns
-        p_r = block_ref[r, pl.ds(0, tile), :]
+        coarse = lax.rem(agg_ref[r], CG)
+        p_r = p_ref[r]
         pt_ref[r] = p_r.T
         for j in range(CG):
             place_ref[pl.ds(r * tile, tile), pl.ds(j * tile, tile)] = jnp.where(coarse == j, p_r, jnp.zeros_like(p_r))
@@ -36,7 +64,12 @@
             both = jnp.concatenate([a_ref[t, 2 * pair], a_ref[t, 2 * pair + 1]], axis=1)
             terms = jnp.dot(pt_ref[t], both, preferred_element_type=jnp.float32)
             for side in range(2):
-                at = lax.rem(table_ref[t, 2 * pair + side], CORE)
+                k = 2 * pair + side
+                column = col_ref[t, k]
+                offset = lax.rem(column // (rows * members) - my_group + 1 + groups, groups)
+                near = lax.rem(column, rows) + rows * offset - (rows - HALO)
+                at = jnp.where(k < count_ref[t], lax.rem(agg_ref[t], CG) * columns + near, CG * columns)
+                at = jnp.clip(at, 0, CG * columns)
                 acc_ref[at] += terms[:, side * tile : (side + 1) * tile]
     for i in range(CG):
         for part in range(2):
@@ -77,46 +110,54 @@
 def local(groups, members, a_tiles, col_tiles, counts, aggregate, p_tiles):
     rows, slots, tile = a_tiles.shape[0], a_tiles.shape[1], a_tiles.shape[2]
     columns = rows + 2 * HALO
-    coarse = lax.rem(aggregate, CG)
-    side = lax.rem(col_tiles // (rows * members) - (lax.axis_index("dom") - 1 - groups), groups)
-    near = coarse[:, None] * columns + lax.rem(col_tiles, rows) + rows * side - (rows - HALO)
-    live = lax.broadcasted_iota(jnp.int32, col_tiles.shape, 1) < counts[:, None]
-    table = jnp.clip(jnp.where(live, near, CG * columns), 0, CG * columns) + CORE * lax.rem(lax.axis_index("sub"), 2)
-
-    marks = coarse + jnp.where(lax.iota(jnp.int32, rows) < HALO, CG, 0)
-    inside = lax.broadcasted_iota(jnp.int32, (rows, tile + MARK, tile), 1) < tile
-    block = jnp.where(inside, jnp.pad(p_tiles, ((0, 0), (0, MARK), (0, 0))), marks.astype(jnp.bfloat16)[:, None, None])
-
-    even = lax.rem(lax.axis_index("dom"), 2) == 0
+    hbm = pl.BlockSpec(memory_space=pltpu.HBM)
+    keep_in_hbm = functools.partial(pltpu.with_memory_space_constraint, memory_space=pltpu.HBM)
+    a_tiles, col_tiles, counts, aggregate, p_tiles = map(keep_in_hbm, (a_tiles, col_tiles, counts, aggregate, p_tiles))
+    vmem = pl.BlockSpec(memory_space=pltpu.VMEM)
+    blocks = pl.pallas_call(
+        pack_kernel,
+        out_shape=(jax.ShapeDtypeStruct((HALO, tile + MARK, tile), jnp.bfloat16),) * 2,
+        in_specs=[hbm, hbm],
+        out_specs=(vmem, vmem),
+        scratch_shapes=[
+            pltpu.SMEM(aggregate.shape, jnp.int32),
+            pltpu.VMEM((2, HALO, tile, tile), jnp.bfloat16),
+            pltpu.SemaphoreType.DMA((3,)),
+        ],
+        name="pack",
+    )(aggregate, p_tiles)
     halos = []
-    for turn in range(2):
-        start = jnp.where(even == (turn == 0), rows - HALO, 0)
+    for turn, block in enumerate(blocks):
         route = []
         for i in range(turn, groups + turn, 2):
             route += [(i % groups, (i + 1) % groups), ((i + 1) % groups, i % groups)]
-        halos.append(lax.ppermute(lax.dynamic_slice_in_dim(block, start, HALO), "dom", route))
+        halos.append(lax.ppermute(block, "dom", route))
 
-    vmem = pl.BlockSpec(memory_space=pltpu.VMEM)
     g, own = pl.pallas_call(
-        front_kernel,
+        functools.partial(front_kernel, groups, members),
         out_shape=(
             jax.ShapeDtypeStruct((CG * tile, 2 * HALO * tile), jnp.bfloat16),
             jax.ShapeDtypeStruct((CG * tile, CG * tile), jnp.bfloat16),
         ),
-        in_specs=[pl.BlockSpec(memory_space=pltpu.SMEM), pl.BlockSpec(memory_space=pl.ANY), vmem],
+        in_specs=[hbm] * 5,
         out_specs=(vmem, vmem),
         scratch_shapes=[
+            pltpu.SMEM(col_tiles.shape, jnp.int32),
+            pltpu.SMEM(counts.shape, jnp.int32),
+            pltpu.SMEM(aggregate.shape, jnp.int32),
             pltpu.VMEM(a_tiles.shape, jnp.bfloat16),
+            pltpu.VMEM(p_tiles.shape, jnp.bfloat16),
             pltpu.VMEM((CG * columns + 1, tile, tile), jnp.float32),
             pltpu.VMEM((CG * tile, rows * tile), jnp.bfloat16),
             pltpu.VMEM((rows * tile, CG * tile), jnp.bfloat16),
             pltpu.VMEM(p_tiles.shape, jnp.bfloat16),
             pltpu.SemaphoreType.DMA((rows,)),
+            pltpu.SemaphoreType.DMA((4,)),
         ],
-        compiler_params=pltpu.CompilerParams(vmem_limit_bytes=52 * 2**20),
+        compiler_params=pltpu.CompilerParams(vmem_limit_bytes=24 * 2**20),
         cost_estimate=pl.CostEstimate(flops=2 * 10**9, bytes_accessed=4 * 2**20, transcendentals=0),
         name="front",
-    )(table, a_tiles, block)
+    )(col_tiles, counts, aggregate, a_tiles, p_tiles)
 
     share = CG * tile // 2
     keep, send = pl.pallas_call(

time: 52 us -> 51.3 us (0.987)
  other arithmetic: 3.61 us -> 1.05 us
  Pallas kernels: 4.36 us -> 5.73 us
    pallas_call x1 -> x2, Pallas kernels: 3.83 us -> 5.2 us  [the longest x1 3.65 us: local(): pl.pallas_call(functools.partial(front_kernel, groups, members), out_shap...]
    select_n x1 -> x0, other arithmetic: 1.11 us -> none  [local(): jnp.where(inside, jnp.pad(p_tiles, ((0, 0), (0, MARK), (0, 0))), marks.as...]
    add x1 -> x0, other arithmetic: 0.77 us -> none  [local(): jnp.clip(jnp.where(live, near, CG * columns), 0, CG * columns)]
    convert_element_type x1 -> x0, other arithmetic: 0.66 us -> none  [local(): marks.astype(jnp.bfloat16)[:, None, None]]
  transfers between devices with their start and end apart: 3 -> 3, of which waited for: 1 -> 1; matrix products, arithmetic and copies ran while one was open for 1% -> 0% of each run, Pallas kernels for 7% -> 7%
where the time goes in v4:
time: 51.3 us; the launch traced here: 51 us
  starting transfers between devices  27 us (53%)
  blocking collectives  15.2 us (30%)
  Pallas kernels  5.73 us (11%)
  waiting for transfers between devices  1.9 us (4%)
  other arithmetic  1.05 us (2%)
    ppermute x2, starting transfers between devices, local(): halos.append(lax.ppermute(block, 'dom', route))  23.9 us
    all_to_all x1, blocking collectives, local(): lax.all_to_all(chip.reshape(members // 2, -1, chip.shape[1]), 'sub', 0, 0...  15.2 us
    pallas_call x1, Pallas kernels, local(): pl.pallas_call(functools.partial(front_kernel, groups, members), out_shap...  3.65 us
    ppermute x1, starting transfers between devices, local(): other = lax.ppermute(send, 'sub', [(i, i ^ 1) for i in range(members)])  3.15 us
    ppermute x1, waiting for transfers between devices, local(): other = lax.ppermute(send, 'sub', [(i, i ^ 1) for i in range(members)])  1.89 us
    pallas_call x1, Pallas kernels, local(): pl.pallas_call(pack_kernel, out_shape=(jax.ShapeDtypeStruct((HALO, tile +...  1.56 us
  transfers between devices with their start and end apart: 3, of which 1 were waited for; matrix products, arithmetic and copies ran while one was open for 0% of the time, Pallas kernels for 7%

profile of v4, /device:TPU:1, one launch (start us, length us, event | category | flops | bytes accessed | tf_op | source)
XLA Modules:
  0.0 51.0 jit_solution(5191932325791008298)
XLA Ops:
  0.0 1.6 %pack.1 = (bf16[2,144,128]{2,1,0:T(8,128)(2,1)}, bf16[2,144,128]{2,1,0:T(8,128)(2,1)}) custom-call(s32[8]{0:T(128)} %agg_hbm.3, bf16[8,128,128]{2,1,0:T(8,128)(2,1)} %p_hbm.3), custom_call_target="tpu_custom_call" | custom-call | tf_op jit(solution)/shard_map/pack/pallas_call | solution.py:117
  1.6 4.8 %collective-permute-start = (bf16[2,144,128]{2,1,0:T(8,128)(2,1)}, bf16[2,144,128]{2,1,0:T(8,128)(2,1)S(1)}, u32[]{:S(2)}, u32[]{:S(2)}) collective-permute-start(bf16[2,144,128]{2,1,0:T(8,128)(2,1)} %get-tuple-element.13), channel_id=1, source_target_pairs={{0,8},{8,0},{16,24},{24,16},{32,40},{40,32},{48,56},{56,48},{64,72... | collective-permute-start | bytes 221192 | tf_op jit(solution)/shard_map/ppermute | solution.py:134
  6.4 19.0 %collective-permute-start.1 = (bf16[2,144,128]{2,1,0:T(8,128)(2,1)}, bf16[2,144,128]{2,1,0:T(8,128)(2,1)S(1)}, u32[]{:S(2)}, u32[]{:S(2)}) collective-permute-start(bf16[2,144,128]{2,1,0:T(8,128)(2,1)} %get-tuple-element.14), channel_id=1, source_target_pairs={{8,16},{16,8},{24,32},{32,24},{40,48},{48,40},{56,64},{64,56},{72,... | collective-permute-start | bytes 221192 | tf_op jit(solution)/shard_map/ppermute | solution.py:134
  25.4 3.6 %front.1 = (bf16[512,512]{1,0:T(8,128)(2,1)S(1)}, bf16[512,512]{1,0:T(8,128)(2,1)S(1)}) custom-call(s32[8,8]{1,0:T(8,128)} %col_hbm.1, s32[8]{0:T(128)} %count_hbm.1, s32[8]{0:T(128)} %agg_hbm.3, bf16[8,8,128,128]{3,2,1,0:T(8,128)(2,1)} %a_hbm.1, bf16[8,128,128]{2,1,0:T(8,128)(2,1)} %p_hbm.3), custom_call_target="tpu_custom_call" | custom-call | flops 2000000000 | bytes 4194304 | tf_op jit(solution)/shard_map/front/pallas_call | solution.py:136
  29.1 0.0 collective-permute-done.first_ref
  29.1 0.0 collective-permute-done.1.second_ref
  29.1 0.5 %back.1 = (bf16[256,1536]{1,0:T(8,128)(2,1)S(1)}, bf16[256,1536]{1,0:T(8,128)(2,1)S(1)}) custom-call(bf16[512,512]{1,0:T(8,128)(2,1)S(1)} %get-tuple-element.11.g_ref, bf16[512,512]{1,0:T(8,128)(2,1)S(1)} %get-tuple-element.12.own_ref, bf16[2,144,128]{2,1,0:T(8,128)(2,1)S(1)} %collective-permute-done.first_ref, ...), custom_call_target="tpu_custom_call" | custom-call | flops 300000000 | bytes 3145728 | tf_op jit(solution)/shard_map/back/pallas_call | solution.py:163
  29.6 3.1 %collective-permute-start.2 = (bf16[256,1536]{1,0:T(8,128)(2,1)S(1)}, bf16[256,1536]{1,0:T(8,128)(2,1)S(1)}, u32[]{:S(2)}, u32[]{:S(2)}) collective-permute-start(bf16[256,1536]{1,0:T(8,128)(2,1)S(1)} %get-tuple-element.16), channel_id=1, source_target_pairs={{0,1},{1,0},{2,3},{3,2},{4,5},{5,4},{6,7},{7,6},{8,9},{9,8},{10,11... | collective-permute-start | bytes 2359304 | tf_op jit(solution)/shard_map/ppermute | solution.py:173
  32.8 1.9 %collective-permute-done.2 = bf16[256,1536]{1,0:T(8,128)(2,1)S(1)} collective-permute-done((bf16[256,1536]{1,0:T(8,128)(2,1)S(1)}, bf16[256,1536]{1,0:T(8,128)(2,1)S(1)}, u32[]{:S(2)}, u32[]{:S(2)}) %collective-permute-start.2) | collective-permute-done | bytes 786464 | tf_op jit(solution)/shard_map/ppermute | solution.py:173
  34.7 0.2 add_convert_fusion
  34.9 15.2 %all_to_all.5 = bf16[4,64,1536]{2,1,0:T(8,128)(2,1)S(1)} all-to-all(bf16[4,64,1536]{2,1,0:T(8,128)(2,1)S(1)} %bitcast.1), channel_id=1, replica_groups={{0,2,4,6},{1,3,5,7},{8,10,12,14},{9,11,13,15},{16,18,20,22},{17,19,21,2..., dimensions={0} | all-to-all | bytes 1572864 | tf_op jit(solution)/shard_map/all_to_all | solution.py:176
  50.1 0.9 %convert_reduce_fusion = f32[64,1536]{1,0:T(8,128)} fusion(bf16[4,64,1536]{2,1,0:T(8,128)(2,1)S(1)} %all_to_all.5), kind=kLoop, calls=%fused_computation | loop fusion | flops 688128 | bytes 1179648 | tf_op jit(solution)/shard_map/reduce_sum | solution.py:177
Async XLA Ops:
  1.6 27.5 %collective-permute-start = (bf16[2,144,128]{2,1,0:T(8,128)(2,1)}, bf16[2,144,128]{2,1,0:T(8,128)(2,1)S(1)}, u32[]{:S(2)}, u32[]{:S(2)}) collective-permute-start(bf16[2,144,128]{2,1,0:T(8,128)(2,1)} %get-tuple-element.13), channel_id=1, source_target_pairs={{0,8},{8,0},{16,24},{24,16},{32,40},{40,32},{48,56},{56,48},{64,72... | collective-permute-start | bytes 221192 | tf_op jit(solution)/shard_map/ppermute | solution.py:134
  6.4 22.7 %collective-permute-start.1 = (bf16[2,144,128]{2,1,0:T(8,128)(2,1)}, bf16[2,144,128]{2,1,0:T(8,128)(2,1)S(1)}, u32[]{:S(2)}, u32[]{:S(2)}) collective-permute-start(bf16[2,144,128]{2,1,0:T(8,128)(2,1)} %get-tuple-element.14), channel_id=1, source_target_pairs={{8,16},{16,8},{24,32},{32,24},{40,48},{48,40},{56,64},{64,56},{72,... | collective-permute-start | bytes 221192 | tf_op jit(solution)/shard_map/ppermute | solution.py:134
  29.6 5.0 %collective-permute-start.2 = (bf16[256,1536]{1,0:T(8,128)(2,1)S(1)}, bf16[256,1536]{1,0:T(8,128)(2,1)S(1)}, u32[]{:S(2)}, u32[]{:S(2)}) collective-permute-start(bf16[256,1536]{1,0:T(8,128)(2,1)S(1)} %get-tuple-element.16), channel_id=1, source_target_pairs={{0,1},{1,0},{2,3},{3,2},{4,5},{5,4},{6,7},{7,6},{8,9},{9,8},{10,11... | collective-permute-start | bytes 2359304 | tf_op jit(solution)/shard_map/ppermute | solution.py:173

commit v5 on v4

--- a/solution.py
+++ b/solution.py
@@ -9,6 +9,7 @@
 
 CG = 4
 HALO = 2
+TURNS = ((3, 1, 2), (1, 3, 2))
 MARK = 16
 
 
@@ -25,11 +26,18 @@
         copy.wait()
     odd = lax.rem(agg_ref[0] // CG, 2)
     for turn, ref in enumerate((first_ref, second_ref)):
-        tail = 1 - odd if turn == 0 else odd
+        tail = odd if turn == 0 else 1 - odd
         for r in range(HALO):
             mark = lax.rem(agg_ref[tail * (rows - HALO) + r], CG) + (1 - tail) * CG
             ref[r, pl.ds(0, tile), :] = ends_ref[tail, r]
             ref[r, pl.ds(tile, MARK), :] = jnp.full((MARK, tile), mark.astype(jnp.float32)).astype(jnp.bfloat16)
+
+
+def turn_of(apart, core):
+    place = 0
+    for turn, step in enumerate(TURNS[core], start=1):
+        place = jnp.where(apart == step, turn, place)
+    return place
 
 
 def front_kernel(
@@ -50,6 +58,7 @@
     device = col_ref[0, 0] // rows
     my_group = device // members
     core = lax.rem(device, 2)
+    chip = lax.rem(device, members) // 2
     for r in range(rows):
         coarse = lax.rem(agg_ref[r], CG)
         p_r = p_ref[r]
@@ -74,7 +83,8 @@
     for i in range(CG):
         for part in range(2):
             first = pl.multiple_of((core if part == 1 else 1 - core) * half, half)
-            to = pl.ds((part * CG + i) * half, half)
+            turn = jnp.where(core == 1 - part, turn_of(i ^ chip, 0), turn_of(i ^ chip, 1))
+            to = pl.ds(pl.multiple_of((part * CG + turn) * half, half), half)
             for c in range(columns):
                 block = acc_ref[i * columns + c, pl.ds(first, half), :].astype(jnp.bfloat16)
                 if c < HALO:
@@ -129,7 +139,7 @@
     halos = []
     for turn, block in enumerate(blocks):
         route = []
-        for i in range(turn, groups + turn, 2):
+        for i in range(1 - turn, groups + 1 - turn, 2):
             route += [(i % groups, (i + 1) % groups), ((i + 1) % groups, i % groups)]
         halos.append(lax.ppermute(block, "dom", route))
 
@@ -172,9 +182,12 @@
     )(g, own, *halos)
     other = lax.ppermute(send, "sub", [(i, i ^ 1) for i in range(members)])
     chip = (keep.astype(jnp.float32) + other.astype(jnp.float32)).astype(jnp.bfloat16)
-    cores = [list(range(core, members, 2)) for core in range(2)]
-    parts = lax.all_to_all(chip.reshape(members // 2, -1, chip.shape[1]), "sub", 0, 0, axis_index_groups=cores)
-    return parts.astype(jnp.float32).sum(axis=0)
+    parts = chip.reshape(members // 2, -1, chip.shape[1])
+    total = parts[0].astype(jnp.float32)
+    for turn in range(1, members // 2):
+        route = [(i, i ^ (2 * TURNS[i % 2][turn - 1])) for i in range(members)]
+        total += lax.ppermute(parts[turn], "sub", route).astype(jnp.float32)
+    return total
 
 
 def solution(mesh):

time: 51.3 us -> 52 us (1.014)
  blocking collectives: 15.2 us -> 0 us
  starting transfers between devices: 27 us -> 36.8 us
  waiting for transfers between devices: 1.9 us -> 7.81 us
    all_to_all x1 -> x0, blocking collectives: 15.2 us -> none  [local(): lax.all_to_all(chip.reshape(members // 2, -1, chip.shape[1]), 'sub', 0, 0...]
    ppermute x0 -> x3, starting transfers between devices: none -> 9.58 us  [local(): total += lax.ppermute(parts[turn], 'sub', route).astype(jnp.float32)]
    ppermute x0 -> x3, waiting for transfers between devices: none -> 5.92 us  [local(): total += lax.ppermute(parts[turn], 'sub', route).astype(jnp.float32)]
    reduce_sum x1 -> x0, other arithmetic: 0.86 us -> none  [local(): return parts.astype(jnp.float32).sum(axis=0)]
    add x0 -> x1, other arithmetic: none -> 0.84 us  [local(): total += lax.ppermute(parts[turn], 'sub', route).astype(jnp.float32)]
  transfers between devices with their start and end apart: 3 -> 6, of which waited for: 1 -> 3; matrix products, arithmetic and copies ran while one was open for 0% -> 0% of each run, Pallas kernels for 7% -> 7%
where the time goes in v5:
time: 52 us; the launch traced here: 51.6 us
  starting transfers between devices  36.8 us (71%)
  waiting for transfers between devices  7.81 us (15%)
  Pallas kernels  5.85 us (11%)
  other arithmetic  1.03 us (2%)
    ppermute x2, starting transfers between devices, local(): halos.append(lax.ppermute(block, 'dom', route))  23.6 us
    ppermute x3, starting transfers between devices, local(): total += lax.ppermute(parts[turn], 'sub', route).astype(jnp.float32)  9.58 us
    ppermute x3, waiting for transfers between devices, local(): total += lax.ppermute(parts[turn], 'sub', route).astype(jnp.float32)  5.92 us
    pallas_call x1, Pallas kernels, local(): pl.pallas_call(functools.partial(front_kernel, groups, members), out_shap...  3.76 us
    ppermute x1, starting transfers between devices, local(): other = lax.ppermute(send, 'sub', [(i, i ^ 1) for i in range(members)])  3.6 us
    ppermute x1, waiting for transfers between devices, local(): other = lax.ppermute(send, 'sub', [(i, i ^ 1) for i in range(members)])  1.89 us
    pallas_call x1, Pallas kernels, local(): pl.pallas_call(pack_kernel, out_shape=(jax.ShapeDtypeStruct((HALO, tile +...  1.56 us
  transfers between devices with their start and end apart: 6, of which 3 were waited for; matrix products, arithmetic and copies ran while one was open for 0% of the time, Pallas kernels for 7%

profile of v5, /device:TPU:1, one launch (start us, length us, event | category | flops | bytes accessed | tf_op | source)
XLA Modules:
  0.0 51.6 jit_solution(14434065944698059215)
XLA Ops:
  0.0 1.6 %pack.1 = (bf16[2,144,128]{2,1,0:T(8,128)(2,1)}, bf16[2,144,128]{2,1,0:T(8,128)(2,1)}) custom-call(s32[8]{0:T(128)} %agg_hbm.3, bf16[8,128,128]{2,1,0:T(8,128)(2,1)} %p_hbm.3), custom_call_target="tpu_custom_call" | custom-call | tf_op jit(solution)/shard_map/pack/pallas_call | solution.py:127
  1.6 21.7 %collective-permute-start = (bf16[2,144,128]{2,1,0:T(8,128)(2,1)}, bf16[2,144,128]{2,1,0:T(8,128)(2,1)S(1)}, u32[]{:S(2)}, u32[]{:S(2)}) collective-permute-start(bf16[2,144,128]{2,1,0:T(8,128)(2,1)} %get-tuple-element.13), channel_id=1, source_target_pairs={{8,16},{16,8},{24,32},{32,24},{40,48},{48,40},{56,64},{64,56},{72,... | collective-permute-start | bytes 221192 | tf_op jit(solution)/shard_map/ppermute | solution.py:144
  23.3 1.9 %collective-permute-start.1 = (bf16[2,144,128]{2,1,0:T(8,128)(2,1)}, bf16[2,144,128]{2,1,0:T(8,128)(2,1)S(1)}, u32[]{:S(2)}, u32[]{:S(2)}) collective-permute-start(bf16[2,144,128]{2,1,0:T(8,128)(2,1)} %get-tuple-element.14), channel_id=1, source_target_pairs={{0,8},{8,0},{16,24},{24,16},{32,40},{40,32},{48,56},{56,48},{64,72... | collective-permute-start | bytes 221192 | tf_op jit(solution)/shard_map/ppermute | solution.py:144
  25.2 3.8 %front.1 = (bf16[512,512]{1,0:T(8,128)(2,1)S(1)}, bf16[512,512]{1,0:T(8,128)(2,1)S(1)}) custom-call(s32[8,8]{1,0:T(8,128)} %col_hbm.1, s32[8]{0:T(128)} %count_hbm.1, s32[8]{0:T(128)} %agg_hbm.3, bf16[8,8,128,128]{3,2,1,0:T(8,128)(2,1)} %a_hbm.1, bf16[8,128,128]{2,1,0:T(8,128)(2,1)} %p_hbm.3), custom_call_target="tpu_custom_call" | custom-call | flops 2000000000 | bytes 4194304 | tf_op jit(solution)/shard_map/front/pallas_call | solution.py:146
  28.9 0.0 collective-permute-done.first_ref
  29.0 0.0 collective-permute-done.1.second_ref
  29.0 0.5 %back.1 = (bf16[256,1536]{1,0:T(8,128)(2,1)S(1)}, bf16[256,1536]{1,0:T(8,128)(2,1)S(1)}) custom-call(bf16[512,512]{1,0:T(8,128)(2,1)S(1)} %get-tuple-element.11.g_ref, bf16[512,512]{1,0:T(8,128)(2,1)S(1)} %get-tuple-element.12.own_ref, bf16[2,144,128]{2,1,0:T(8,128)(2,1)S(1)} %collective-permute-done.first_ref, ...), custom_call_target="tpu_custom_call" | custom-call | flops 300000000 | bytes 3145728 | tf_op jit(solution)/shard_map/back/pallas_call | solution.py:173
  29.5 3.6 %collective-permute-start.2 = (bf16[256,1536]{1,0:T(8,128)(2,1)S(1)}, bf16[256,1536]{1,0:T(8,128)(2,1)S(1)}, u32[]{:S(2)}, u32[]{:S(2)}) collective-permute-start(bf16[256,1536]{1,0:T(8,128)(2,1)S(1)} %get-tuple-element.16), channel_id=1, source_target_pairs={{0,1},{1,0},{2,3},{3,2},{4,5},{5,4},{6,7},{7,6},{8,9},{9,8},{10,11... | collective-permute-start | bytes 2359304 | tf_op jit(solution)/shard_map/ppermute | solution.py:183
  33.1 1.9 %collective-permute-done.2 = bf16[256,1536]{1,0:T(8,128)(2,1)S(1)} collective-permute-done((bf16[256,1536]{1,0:T(8,128)(2,1)S(1)}, bf16[256,1536]{1,0:T(8,128)(2,1)S(1)}, u32[]{:S(2)}, u32[]{:S(2)}) %collective-permute-start.2) | collective-permute-done | bytes 786464 | tf_op jit(solution)/shard_map/ppermute | solution.py:183
  35.0 0.2 add_convert_fusion
  35.2 3.1 %collective-permute-start.3 = (bf16[64,1536]{1,0:T(8,128)(2,1)S(1)}, bf16[64,1536]{1,0:T(8,128)(2,1)S(1)}, u32[]{:S(2)}, u32[]{:S(2)}) collective-permute-start(bf16[64,1536]{1,0:T(8,128)(2,1)S(1)} %get-tuple-element.17), channel_id=1, source_target_pairs={{0,6},{1,3},{2,4},{3,1},{4,2},{5,7},{6,0},{7,5},{8,14},{9,11},{10,... | collective-permute-start | bytes 589832 | tf_op jit(solution)/shard_map/ppermute | solution.py:189
  38.4 4.4 %collective-permute-start.5 = (bf16[64,1536]{1,0:T(8,128)(2,1)S(1)}, bf16[64,1536]{1,0:T(8,128)(2,1)S(1)}, u32[]{:S(2)}, u32[]{:S(2)}) collective-permute-start(bf16[64,1536]{1,0:T(8,128)(2,1)S(1)} %get-tuple-element.18), channel_id=1, source_target_pairs={{0,4},{1,5},{2,6},{3,7},{4,0},{5,1},{6,2},{7,3},{8,12},{9,13},{10,... | collective-permute-start | bytes 589832 | tf_op jit(solution)/shard_map/ppermute | solution.py:189
  42.7 2.1 %collective-permute-start.4 = (bf16[64,1536]{1,0:T(8,128)(2,1)S(1)}, bf16[64,1536]{1,0:T(8,128)(2,1)S(1)}, u32[]{:S(2)}, u32[]{:S(2)}) collective-permute-start(bf16[64,1536]{1,0:T(8,128)(2,1)S(1)} %get-tuple-element.19), channel_id=1, source_target_pairs={{0,2},{1,7},{2,0},{3,5},{4,6},{5,3},{6,4},{7,1},{8,10},{9,15},{10,... | collective-permute-start | bytes 589832 | tf_op jit(solution)/shard_map/ppermute | solution.py:189
  44.9 0.0 collective-permute-done.3
  44.9 2.2 %collective-permute-done.5 = bf16[64,1536]{1,0:T(8,128)(2,1)S(1)} collective-permute-done((bf16[64,1536]{1,0:T(8,128)(2,1)S(1)}, bf16[64,1536]{1,0:T(8,128)(2,1)S(1)}, u32[]{:S(2)}, u32[]{:S(2)}) %collective-permute-start.5) | collective-permute-done | bytes 196640 | tf_op jit(solution)/shard_map/ppermute | solution.py:189
  47.1 3.7 %collective-permute-done.4 = bf16[64,1536]{1,0:T(8,128)(2,1)S(1)} collective-permute-done((bf16[64,1536]{1,0:T(8,128)(2,1)S(1)}, bf16[64,1536]{1,0:T(8,128)(2,1)S(1)}, u32[]{:S(2)}, u32[]{:S(2)}) %collective-permute-start.4) | collective-permute-done | bytes 196640 | tf_op jit(solution)/shard_map/ppermute | solution.py:189
  50.8 0.8 %convert_add_fusion = f32[64,1536]{1,0:T(8,128)} fusion(bf16[64,1536]{1,0:T(8,128)(2,1)S(1)} %collective-permute-done.5, bf16[64,1536]{1,0:T(8,128)(2,1)S(1)} %collective-permute-done.4, bf16[64,1536]{1,0:T(8,128)(2,1)S(1)} %collective-permute-done.3, bf16[256,1536]{1,0:T(8,128)(2,1)S(1)} %add_convert_fusion), kind=kLoop, calls=%fused_computation.1 | loop fusion | flops 688128 | bytes 1179648 | tf_op jit(solution)/shard_map/add | solution.py:189
  (1 shorter events, 0.0 us)
Async XLA Ops:
  1.6 27.4 %collective-permute-start = (bf16[2,144,128]{2,1,0:T(8,128)(2,1)}, bf16[2,144,128]{2,1,0:T(8,128)(2,1)S(1)}, u32[]{:S(2)}, u32[]{:S(2)}) collective-permute-start(bf16[2,144,128]{2,1,0:T(8,128)(2,1)} %get-tuple-element.13), channel_id=1, source_target_pairs={{8,16},{16,8},{24,32},{32,24},{40,48},{48,40},{56,64},{64,56},{72,... | collective-permute-start | bytes 221192 | tf_op jit(solution)/shard_map/ppermute | solution.py:144
  23.3 5.7 %collective-permute-start.1 = (bf16[2,144,128]{2,1,0:T(8,128)(2,1)}, bf16[2,144,128]{2,1,0:T(8,128)(2,1)S(1)}, u32[]{:S(2)}, u32[]{:S(2)}) collective-permute-start(bf16[2,144,128]{2,1,0:T(8,128)(2,1)} %get-tuple-element.14), channel_id=1, source_target_pairs={{0,8},{8,0},{16,24},{24,16},{32,40},{40,32},{48,56},{56,48},{64,72... | collective-permute-start | bytes 221192 | tf_op jit(solution)/shard_map/ppermute | solution.py:144
  29.5 5.5 %collective-permute-start.2 = (bf16[256,1536]{1,0:T(8,128)(2,1)S(1)}, bf16[256,1536]{1,0:T(8,128)(2,1)S(1)}, u32[]{:S(2)}, u32[]{:S(2)}) collective-permute-start(bf16[256,1536]{1,0:T(8,128)(2,1)S(1)} %get-tuple-element.16), channel_id=1, source_target_pairs={{0,1},{1,0},{2,3},{3,2},{4,5},{5,4},{6,7},{7,6},{8,9},{9,8},{10,11... | collective-permute-start | bytes 2359304 | tf_op jit(solution)/shard_map/ppermute | solution.py:183
  35.2 9.6 %collective-permute-start.3 = (bf16[64,1536]{1,0:T(8,128)(2,1)S(1)}, bf16[64,1536]{1,0:T(8,128)(2,1)S(1)}, u32[]{:S(2)}, u32[]{:S(2)}) collective-permute-start(bf16[64,1536]{1,0:T(8,128)(2,1)S(1)} %get-tuple-element.17), channel_id=1, source_target_pairs={{0,6},{1,3},{2,4},{3,1},{4,2},{5,7},{6,0},{7,5},{8,14},{9,11},{10,... | collective-permute-start | bytes 589832 | tf_op jit(solution)/shard_map/ppermute | solution.py:189
  38.4 8.7 %collective-permute-start.5 = (bf16[64,1536]{1,0:T(8,128)(2,1)S(1)}, bf16[64,1536]{1,0:T(8,128)(2,1)S(1)}, u32[]{:S(2)}, u32[]{:S(2)}) collective-permute-start(bf16[64,1536]{1,0:T(8,128)(2,1)S(1)} %get-tuple-element.18), channel_id=1, source_target_pairs={{0,4},{1,5},{2,6},{3,7},{4,0},{5,1},{6,2},{7,3},{8,12},{9,13},{10,... | collective-permute-start | bytes 589832 | tf_op jit(solution)/shard_map/ppermute | solution.py:189
  42.7 8.0 %collective-permute-start.4 = (bf16[64,1536]{1,0:T(8,128)(2,1)S(1)}, bf16[64,1536]{1,0:T(8,128)(2,1)S(1)}, u32[]{:S(2)}, u32[]{:S(2)}) collective-permute-start(bf16[64,1536]{1,0:T(8,128)(2,1)S(1)} %get-tuple-element.19), channel_id=1, source_target_pairs={{0,2},{1,7},{2,0},{3,5},{4,6},{5,3},{6,4},{7,1},{8,10},{9,15},{10,... | collective-permute-start | bytes 589832 | tf_op jit(solution)/shard_map/ppermute | solution.py:189

commit v6 on v5

--- a/solution.py
+++ b/solution.py
@@ -9,7 +9,7 @@
 
 CG = 4
 HALO = 2
-TURNS = ((3, 1, 2), (1, 3, 2))
+TURNS = ((2, 1, 3), (3, 1, 2))
 MARK = 16
 
 

time: 52 us -> 50.8 us (0.977)
  the two profiles are of different devices: /device:TPU:1 before, /device:TPU:2 now
where the time goes in v6:
time: 50.8 us; the launch traced here: 50.4 us
  starting transfers between devices  35.4 us (70%)
  waiting for transfers between devices  8.01 us (16%)
  Pallas kernels  5.85 us (12%)
  other arithmetic  1.03 us (2%)
    ppermute x2, starting transfers between devices, local(): halos.append(lax.ppermute(block, 'dom', route))  23 us
    ppermute x3, starting transfers between devices, local(): total += lax.ppermute(parts[turn], 'sub', route).astype(jnp.float32)  10.4 us
    ppermute x3, waiting for transfers between devices, local(): total += lax.ppermute(parts[turn], 'sub', route).astype(jnp.float32)  5 us
    pallas_call x1, Pallas kernels, local(): pl.pallas_call(functools.partial(front_kernel, groups, members), out_shap...  3.76 us
    ppermute x1, waiting for transfers between devices, local(): other = lax.ppermute(send, 'sub', [(i, i ^ 1) for i in range(members)])  2.25 us
    ppermute x1, starting transfers between devices, local(): other = lax.ppermute(send, 'sub', [(i, i ^ 1) for i in range(members)])  1.92 us
    pallas_call x1, Pallas kernels, local(): pl.pallas_call(pack_kernel, out_shape=(jax.ShapeDtypeStruct((HALO, tile +...  1.56 us
  transfers between devices with their start and end apart: 6, of which 4 were waited for; matrix products, arithmetic and copies ran while one was open for 0% of the time, Pallas kernels for 7%

profile of v6, /device:TPU:2, one launch (start us, length us, event | category | flops | bytes accessed | tf_op | source)
XLA Modules:
  0.0 50.4 jit_solution(962979509613792262)
XLA Ops:
  0.0 1.6 %pack.1 = (bf16[2,144,128]{2,1,0:T(8,128)(2,1)}, bf16[2,144,128]{2,1,0:T(8,128)(2,1)}) custom-call(s32[8]{0:T(128)} %agg_hbm.3, bf16[8,128,128]{2,1,0:T(8,128)(2,1)} %p_hbm.3), custom_call_target="tpu_custom_call" | custom-call | tf_op jit(solution)/shard_map/pack/pallas_call | solution.py:127
  1.6 21.1 %collective-permute-start = (bf16[2,144,128]{2,1,0:T(8,128)(2,1)}, bf16[2,144,128]{2,1,0:T(8,128)(2,1)S(1)}, u32[]{:S(2)}, u32[]{:S(2)}) collective-permute-start(bf16[2,144,128]{2,1,0:T(8,128)(2,1)} %get-tuple-element.13), channel_id=1, source_target_pairs={{8,16},{16,8},{24,32},{32,24},{40,48},{48,40},{56,64},{64,56},{72,... | collective-permute-start | bytes 221192 | tf_op jit(solution)/shard_map/ppermute | solution.py:144
  22.7 1.9 %collective-permute-start.1 = (bf16[2,144,128]{2,1,0:T(8,128)(2,1)}, bf16[2,144,128]{2,1,0:T(8,128)(2,1)S(1)}, u32[]{:S(2)}, u32[]{:S(2)}) collective-permute-start(bf16[2,144,128]{2,1,0:T(8,128)(2,1)} %get-tuple-element.14), channel_id=1, source_target_pairs={{0,8},{8,0},{16,24},{24,16},{32,40},{40,32},{48,56},{56,48},{64,72... | collective-permute-start | bytes 221192 | tf_op jit(solution)/shard_map/ppermute | solution.py:144
  24.6 3.8 %front.1 = (bf16[512,512]{1,0:T(8,128)(2,1)S(1)}, bf16[512,512]{1,0:T(8,128)(2,1)S(1)}) custom-call(s32[8,8]{1,0:T(8,128)} %col_hbm.1, s32[8]{0:T(128)} %count_hbm.1, s32[8]{0:T(128)} %agg_hbm.3, bf16[8,8,128,128]{3,2,1,0:T(8,128)(2,1)} %a_hbm.1, bf16[8,128,128]{2,1,0:T(8,128)(2,1)} %p_hbm.3), custom_call_target="tpu_custom_call" | custom-call | flops 2000000000 | bytes 4194304 | tf_op jit(solution)/shard_map/front/pallas_call | solution.py:146
  28.4 0.0 collective-permute-done.first_ref
  28.4 0.7 %collective-permute-done.1.second_ref = bf16[2,144,128]{2,1,0:T(8,128)(2,1)S(1)} collective-permute-done((bf16[2,144,128]{2,1,0:T(8,128)(2,1)}, bf16[2,144,128]{2,1,0:T(8,128)(2,1)S(1)}, u32[]{:S(2)}, u32[]{:S(2)}) %collective-permute-start.1) | collective-permute-done | bytes 73760 | tf_op jit(solution)/shard_map/ppermute | solution.py:144
  29.2 0.5 %back.1 = (bf16[256,1536]{1,0:T(8,128)(2,1)S(1)}, bf16[256,1536]{1,0:T(8,128)(2,1)S(1)}) custom-call(bf16[512,512]{1,0:T(8,128)(2,1)S(1)} %get-tuple-element.11.g_ref, bf16[512,512]{1,0:T(8,128)(2,1)S(1)} %get-tuple-element.12.own_ref, bf16[2,144,128]{2,1,0:T(8,128)(2,1)S(1)} %collective-permute-done.first_ref, ...), custom_call_target="tpu_custom_call" | custom-call | flops 300000000 | bytes 3145728 | tf_op jit(solution)/shard_map/back/pallas_call | solution.py:173
  29.7 1.9 %collective-permute-start.2 = (bf16[256,1536]{1,0:T(8,128)(2,1)S(1)}, bf16[256,1536]{1,0:T(8,128)(2,1)S(1)}, u32[]{:S(2)}, u32[]{:S(2)}) collective-permute-start(bf16[256,1536]{1,0:T(8,128)(2,1)S(1)} %get-tuple-element.16), channel_id=1, source_target_pairs={{0,1},{1,0},{2,3},{3,2},{4,5},{5,4},{6,7},{7,6},{8,9},{9,8},{10,11... | collective-permute-start | bytes 2359304 | tf_op jit(solution)/shard_map/ppermute | solution.py:183
  31.6 2.3 %collective-permute-done.2 = bf16[256,1536]{1,0:T(8,128)(2,1)S(1)} collective-permute-done((bf16[256,1536]{1,0:T(8,128)(2,1)S(1)}, bf16[256,1536]{1,0:T(8,128)(2,1)S(1)}, u32[]{:S(2)}, u32[]{:S(2)}) %collective-permute-start.2) | collective-permute-done | bytes 786464 | tf_op jit(solution)/shard_map/ppermute | solution.py:183
  33.9 0.2 add_convert_fusion
  34.1 4.0 %collective-permute-start.3 = (bf16[64,1536]{1,0:T(8,128)(2,1)S(1)}, bf16[64,1536]{1,0:T(8,128)(2,1)S(1)}, u32[]{:S(2)}, u32[]{:S(2)}) collective-permute-start(bf16[64,1536]{1,0:T(8,128)(2,1)S(1)} %get-tuple-element.17), channel_id=1, source_target_pairs={{0,4},{1,7},{2,6},{3,5},{4,0},{5,3},{6,2},{7,1},{8,12},{9,15},{10,... | collective-permute-start | bytes 589832 | tf_op jit(solution)/shard_map/ppermute | solution.py:189
  38.2 1.9 %collective-permute-start.5 = (bf16[64,1536]{1,0:T(8,128)(2,1)S(1)}, bf16[64,1536]{1,0:T(8,128)(2,1)S(1)}, u32[]{:S(2)}, u32[]{:S(2)}) collective-permute-start(bf16[64,1536]{1,0:T(8,128)(2,1)S(1)} %get-tuple-element.18), channel_id=1, source_target_pairs={{0,6},{1,5},{2,4},{3,7},{4,2},{5,1},{6,0},{7,3},{8,14},{9,13},{10,... | collective-permute-start | bytes 589832 | tf_op jit(solution)/shard_map/ppermute | solution.py:189
  40.1 4.5 %collective-permute-start.4 = (bf16[64,1536]{1,0:T(8,128)(2,1)S(1)}, bf16[64,1536]{1,0:T(8,128)(2,1)S(1)}, u32[]{:S(2)}, u32[]{:S(2)}) collective-permute-start(bf16[64,1536]{1,0:T(8,128)(2,1)S(1)} %get-tuple-element.19), channel_id=1, source_target_pairs={{0,2},{1,3},{2,0},{3,1},{4,6},{5,7},{6,4},{7,5},{8,10},{9,11},{10,... | collective-permute-start | bytes 589832 | tf_op jit(solution)/shard_map/ppermute | solution.py:189
  44.6 0.0 collective-permute-done.3
  44.6 3.0 %collective-permute-done.5 = bf16[64,1536]{1,0:T(8,128)(2,1)S(1)} collective-permute-done((bf16[64,1536]{1,0:T(8,128)(2,1)S(1)}, bf16[64,1536]{1,0:T(8,128)(2,1)S(1)}, u32[]{:S(2)}, u32[]{:S(2)}) %collective-permute-start.5) | collective-permute-done | bytes 196640 | tf_op jit(solution)/shard_map/ppermute | solution.py:189
  47.6 2.0 %collective-permute-done.4 = bf16[64,1536]{1,0:T(8,128)(2,1)S(1)} collective-permute-done((bf16[64,1536]{1,0:T(8,128)(2,1)S(1)}, bf16[64,1536]{1,0:T(8,128)(2,1)S(1)}, u32[]{:S(2)}, u32[]{:S(2)}) %collective-permute-start.4) | collective-permute-done | bytes 196640 | tf_op jit(solution)/shard_map/ppermute | solution.py:189
  49.6 0.8 %convert_add_fusion = f32[64,1536]{1,0:T(8,128)} fusion(bf16[64,1536]{1,0:T(8,128)(2,1)S(1)} %collective-permute-done.5, bf16[64,1536]{1,0:T(8,128)(2,1)S(1)} %collective-permute-done.4, bf16[64,1536]{1,0:T(8,128)(2,1)S(1)} %collective-permute-done.3, bf16[256,1536]{1,0:T(8,128)(2,1)S(1)} %add_convert_fusion), kind=kLoop, calls=%fused_computation.1 | loop fusion | flops 688128 | bytes 1179648 | tf_op jit(solution)/shard_map/add | solution.py:189
  (1 shorter events, 0.0 us)
Async XLA Ops:
  1.6 26.8 %collective-permute-start = (bf16[2,144,128]{2,1,0:T(8,128)(2,1)}, bf16[2,144,128]{2,1,0:T(8,128)(2,1)S(1)}, u32[]{:S(2)}, u32[]{:S(2)}) collective-permute-start(bf16[2,144,128]{2,1,0:T(8,128)(2,1)} %get-tuple-element.13), channel_id=1, source_target_pairs={{8,16},{16,8},{24,32},{32,24},{40,48},{48,40},{56,64},{64,56},{72,... | collective-permute-start | bytes 221192 | tf_op jit(solution)/shard_map/ppermute | solution.py:144
  22.7 6.5 %collective-permute-start.1 = (bf16[2,144,128]{2,1,0:T(8,128)(2,1)}, bf16[2,144,128]{2,1,0:T(8,128)(2,1)S(1)}, u32[]{:S(2)}, u32[]{:S(2)}) collective-permute-start(bf16[2,144,128]{2,1,0:T(8,128)(2,1)} %get-tuple-element.14), channel_id=1, source_target_pairs={{0,8},{8,0},{16,24},{24,16},{32,40},{40,32},{48,56},{56,48},{64,72... | collective-permute-start | bytes 221192 | tf_op jit(solution)/shard_map/ppermute | solution.py:144
  29.7 4.2 %collective-permute-start.2 = (bf16[256,1536]{1,0:T(8,128)(2,1)S(1)}, bf16[256,1536]{1,0:T(8,128)(2,1)S(1)}, u32[]{:S(2)}, u32[]{:S(2)}) collective-permute-start(bf16[256,1536]{1,0:T(8,128)(2,1)S(1)} %get-tuple-element.16), channel_id=1, source_target_pairs={{0,1},{1,0},{2,3},{3,2},{4,5},{5,4},{6,7},{7,6},{8,9},{9,8},{10,11... | collective-permute-start | bytes 2359304 | tf_op jit(solution)/shard_map/ppermute | solution.py:183
  34.1 10.4 %collective-permute-start.3 = (bf16[64,1536]{1,0:T(8,128)(2,1)S(1)}, bf16[64,1536]{1,0:T(8,128)(2,1)S(1)}, u32[]{:S(2)}, u32[]{:S(2)}) collective-permute-start(bf16[64,1536]{1,0:T(8,128)(2,1)S(1)} %get-tuple-element.17), channel_id=1, source_target_pairs={{0,4},{1,7},{2,6},{3,5},{4,0},{5,3},{6,2},{7,1},{8,12},{9,15},{10,... | collective-permute-start | bytes 589832 | tf_op jit(solution)/shard_map/ppermute | solution.py:189
  38.2 9.4 %collective-permute-start.5 = (bf16[64,1536]{1,0:T(8,128)(2,1)S(1)}, bf16[64,1536]{1,0:T(8,128)(2,1)S(1)}, u32[]{:S(2)}, u32[]{:S(2)}) collective-permute-start(bf16[64,1536]{1,0:T(8,128)(2,1)S(1)} %get-tuple-element.18), channel_id=1, source_target_pairs={{0,6},{1,5},{2,4},{3,7},{4,2},{5,1},{6,0},{7,3},{8,14},{9,13},{10,... | collective-permute-start | bytes 589832 | tf_op jit(solution)/shard_map/ppermute | solution.py:189
  40.1 9.5 %collective-permute-start.4 = (bf16[64,1536]{1,0:T(8,128)(2,1)S(1)}, bf16[64,1536]{1,0:T(8,128)(2,1)S(1)}, u32[]{:S(2)}, u32[]{:S(2)}) collective-permute-start(bf16[64,1536]{1,0:T(8,128)(2,1)S(1)} %get-tuple-element.19), channel_id=1, source_target_pairs={{0,2},{1,3},{2,0},{3,1},{4,6},{5,7},{6,4},{7,5},{8,10},{9,11},{10,... | collective-permute-start | bytes 589832 | tf_op jit(solution)/shard_map/ppermute | solution.py:189

commit v7 on v6

--- a/solution.py
+++ b/solution.py
@@ -26,7 +26,7 @@
         copy.wait()
     odd = lax.rem(agg_ref[0] // CG, 2)
     for turn, ref in enumerate((first_ref, second_ref)):
-        tail = odd if turn == 0 else 1 - odd
+        tail = 1 - odd if turn == 0 else odd
         for r in range(HALO):
             mark = lax.rem(agg_ref[tail * (rows - HALO) + r], CG) + (1 - tail) * CG
             ref[r, pl.ds(0, tile), :] = ends_ref[tail, r]
@@ -41,20 +41,12 @@
 
 
 def front_kernel(
-    groups, members, col_hbm, count_hbm, agg_hbm, a_hbm, p_hbm, g_ref, own_ref,
-    col_ref, count_ref, agg_ref, a_ref, p_ref, acc_ref, gown_ref, place_ref, pt_ref, sems, small_sems,
+    groups, members, col_ref, count_ref, agg_ref, a_ref, p_ref, g_ref, own_ref, acc_ref, gown_ref, place_ref, pt_ref
 ):
-    rows, slots, tile = a_hbm.shape[0], a_hbm.shape[1], a_hbm.shape[2]
+    rows, slots, tile = a_ref.shape[0], a_ref.shape[1], a_ref.shape[2]
     columns = rows + 2 * HALO
     half = tile // 2
-    copies = [pltpu.make_async_copy(a_hbm.at[t], a_ref.at[t], sems.at[t]) for t in range(rows)]
-    pairs = ((col_hbm, col_ref), (count_hbm, count_ref), (agg_hbm, agg_ref), (p_hbm, p_ref))
-    small = [pltpu.make_async_copy(source, to, small_sems.at[i]) for i, (source, to) in enumerate(pairs)]
-    for copy in small + copies:
-        copy.start()
     acc_ref[...] = jnp.zeros_like(acc_ref)
-    for copy in small:
-        copy.wait()
     device = col_ref[0, 0] // rows
     my_group = device // members
     core = lax.rem(device, 2)
@@ -66,9 +58,6 @@
         for j in range(CG):
             place_ref[pl.ds(r * tile, tile), pl.ds(j * tile, tile)] = jnp.where(coarse == j, p_r, jnp.zeros_like(p_r))
     for t in range(rows):
-        if t % (rows // 2) == 0:
-            for copy in copies[t : t + rows // 2]:
-                copy.wait()
         for pair in range(slots // 2):
             both = jnp.concatenate([a_ref[t, 2 * pair], a_ref[t, 2 * pair + 1]], axis=1)
             terms = jnp.dot(pt_ref[t], both, preferred_element_type=jnp.float32)
@@ -121,8 +110,8 @@
     rows, slots, tile = a_tiles.shape[0], a_tiles.shape[1], a_tiles.shape[2]
     columns = rows + 2 * HALO
     hbm = pl.BlockSpec(memory_space=pltpu.HBM)
+    smem = pl.BlockSpec(memory_space=pltpu.SMEM)
     keep_in_hbm = functools.partial(pltpu.with_memory_space_constraint, memory_space=pltpu.HBM)
-    a_tiles, col_tiles, counts, aggregate, p_tiles = map(keep_in_hbm, (a_tiles, col_tiles, counts, aggregate, p_tiles))
     vmem = pl.BlockSpec(memory_space=pltpu.VMEM)
     blocks = pl.pallas_call(
         pack_kernel,
@@ -134,12 +123,13 @@
             pltpu.VMEM((2, HALO, tile, tile), jnp.bfloat16),
             pltpu.SemaphoreType.DMA((3,)),
         ],
+        cost_estimate=pl.CostEstimate(flops=10**9, bytes_accessed=64 * 2**20, transcendentals=0),
         name="pack",
-    )(aggregate, p_tiles)
+    )(keep_in_hbm(aggregate), keep_in_hbm(p_tiles))
     halos = []
     for turn, block in enumerate(blocks):
         route = []
-        for i in range(1 - turn, groups + 1 - turn, 2):
+        for i in range(turn, groups + turn, 2):
             route += [(i % groups, (i + 1) % groups), ((i + 1) % groups, i % groups)]
         halos.append(lax.ppermute(block, "dom", route))
 
@@ -149,20 +139,13 @@
             jax.ShapeDtypeStruct((CG * tile, 2 * HALO * tile), jnp.bfloat16),
             jax.ShapeDtypeStruct((CG * tile, CG * tile), jnp.bfloat16),
         ),
-        in_specs=[hbm] * 5,
+        in_specs=[smem] * 3 + [vmem] * 2,
         out_specs=(vmem, vmem),
         scratch_shapes=[
-            pltpu.SMEM(col_tiles.shape, jnp.int32),
-            pltpu.SMEM(counts.shape, jnp.int32),
-            pltpu.SMEM(aggregate.shape, jnp.int32),
-            pltpu.VMEM(a_tiles.shape, jnp.bfloat16),
-            pltpu.VMEM(p_tiles.shape, jnp.bfloat16),
             pltpu.VMEM((CG * columns + 1, tile, tile), jnp.float32),
             pltpu.VMEM((CG * tile, rows * tile), jnp.bfloat16),
             pltpu.VMEM((rows * tile, CG * tile), jnp.bfloat16),
             pltpu.VMEM(p_tiles.shape, jnp.bfloat16),
-            pltpu.SemaphoreType.DMA((rows,)),
-            pltpu.SemaphoreType.DMA((4,)),
         ],
         compiler_params=pltpu.CompilerParams(vmem_limit_bytes=24 * 2**20),
         cost_estimate=pl.CostEstimate(flops=2 * 10**9, bytes_accessed=4 * 2**20, transcendentals=0),

time: 50.8 us -> 49.8 us (0.980)
  the two profiles are of different devices: /device:TPU:2 before, /device:TPU:1 now
where the time goes in v7:
time: 49.8 us; the launch traced here: 48.8 us
  starting transfers between devices  36 us (72%)
  waiting for transfers between devices  6.53 us (13%)
  Pallas kernels  5.02 us (10%)
  other arithmetic  1.03 us (2%)
    ppermute x2, starting transfers between devices, local(): halos.append(lax.ppermute(block, 'dom', route))  23.9 us
    ppermute x3, starting transfers between devices, local(): total += lax.ppermute(parts[turn], 'sub', route).astype(jnp.float32)  8.98 us
    ppermute x3, waiting for transfers between devices, local(): total += lax.ppermute(parts[turn], 'sub', route).astype(jnp.float32)  4.64 us
    ppermute x1, starting transfers between devices, local(): other = lax.ppermute(send, 'sub', [(i, i ^ 1) for i in range(members)])  3.15 us
    pallas_call x1, Pallas kernels, local(): pl.pallas_call(functools.partial(front_kernel, groups, members), out_shap...  2.79 us
    ppermute x1, waiting for transfers between devices, local(): other = lax.ppermute(send, 'sub', [(i, i ^ 1) for i in range(members)])  1.89 us
    pallas_call x1, Pallas kernels, local(): pl.pallas_call(pack_kernel, out_shape=(jax.ShapeDtypeStruct((HALO, tile +...  1.7 us
  transfers between devices with their start and end apart: 6, of which 4 were waited for; matrix products, arithmetic and copies ran while one was open for 0% of the time, Pallas kernels for 6%

profile of v7, /device:TPU:1, one launch (start us, length us, event | category | flops | bytes accessed | tf_op | source)
XLA Modules:
  0.0 48.8 jit_solution(1289886750070963243)
XLA Ops:
  0.0 0.0 copy-start.2
  0.0 0.0 copy-start
  0.0 1.7 %pack.1 = (bf16[2,144,128]{2,1,0:T(8,128)(2,1)}, bf16[2,144,128]{2,1,0:T(8,128)(2,1)}) custom-call(s32[8]{0:T(128)} %agg_hbm.1, bf16[8,128,128]{2,1,0:T(8,128)(2,1)} %p_hbm.1), custom_call_target="tpu_custom_call" | custom-call | flops 1000000000 | bytes 67108864 | tf_op jit(solution)/shard_map/pack/pallas_call | solution.py:116
  1.7 4.8 %collective-permute-start = (bf16[2,144,128]{2,1,0:T(8,128)(2,1)}, bf16[2,144,128]{2,1,0:T(8,128)(2,1)S(1)}, u32[]{:S(2)}, u32[]{:S(2)}) collective-permute-start(bf16[2,144,128]{2,1,0:T(8,128)(2,1)} %get-tuple-element.13), channel_id=1, source_target_pairs={{0,8},{8,0},{16,24},{24,16},{32,40},{40,32},{48,56},{56,48},{64,72... | collective-permute-start | bytes 221192 | tf_op jit(solution)/shard_map/ppermute | solution.py:134
  6.6 19.0 %collective-permute-start.1 = (bf16[2,144,128]{2,1,0:T(8,128)(2,1)}, bf16[2,144,128]{2,1,0:T(8,128)(2,1)S(1)}, u32[]{:S(2)}, u32[]{:S(2)}) collective-permute-start(bf16[2,144,128]{2,1,0:T(8,128)(2,1)} %get-tuple-element.14), channel_id=1, source_target_pairs={{8,16},{16,8},{24,32},{32,24},{40,48},{48,40},{56,64},{64,56},{72,... | collective-permute-start | bytes 221192 | tf_op jit(solution)/shard_map/ppermute | solution.py:134
  25.6 0.0 copy-done.1
  25.6 0.0 copy-done.4
  25.6 0.0 copy-done.3
  25.6 0.0 copy-done.2
  25.7 0.0 copy-done
  25.7 2.8 %front.1 = (bf16[512,512]{1,0:T(8,128)(2,1)S(1)}, bf16[512,512]{1,0:T(8,128)(2,1)S(1)}) custom-call(s32[8,8]{1,0:T(8,128)S(1)} %copy-done.2, s32[8]{0:T(128)S(1)} %copy-done.3, s32[8]{0:T(128)S(1)} %copy-done.4, bf16[8,8,128,128]{3,2,1,0:T(8,128)(2,1)S(1)} %copy-done, bf16[8,128,128]{2,1,0:T(8,128)(2,1)S(1)} %copy-done.1), custom_call_target="tpu_custom_call" | custom-call | flops 2000000000 | bytes 4194304 | tf_op jit(solution)/shard_map/front/pallas_call | solution.py:136
  28.5 0.0 collective-permute-done.first_ref
  28.5 0.0 collective-permute-done.1.second_ref
  28.5 0.5 %back.1 = (bf16[256,1536]{1,0:T(8,128)(2,1)S(1)}, bf16[256,1536]{1,0:T(8,128)(2,1)S(1)}) custom-call(bf16[512,512]{1,0:T(8,128)(2,1)S(1)} %get-tuple-element.11.g_ref, bf16[512,512]{1,0:T(8,128)(2,1)S(1)} %get-tuple-element.12.own_ref, bf16[2,144,128]{2,1,0:T(8,128)(2,1)S(1)} %collective-permute-done.first_ref, ...), custom_call_target="tpu_custom_call" | custom-call | flops 300000000 | bytes 3145728 | tf_op jit(solution)/shard_map/back/pallas_call | solution.py:156
  29.0 3.2 %collective-permute-start.2 = (bf16[256,1536]{1,0:T(8,128)(2,1)S(1)}, bf16[256,1536]{1,0:T(8,128)(2,1)S(1)}, u32[]{:S(2)}, u32[]{:S(2)}) collective-permute-start(bf16[256,1536]{1,0:T(8,128)(2,1)S(1)} %get-tuple-element.16), channel_id=1, source_target_pairs={{0,1},{1,0},{2,3},{3,2},{4,5},{5,4},{6,7},{7,6},{8,9},{9,8},{10,11... | collective-permute-start | bytes 2359304 | tf_op jit(solution)/shard_map/ppermute | solution.py:166
  32.2 1.9 %collective-permute-done.2 = bf16[256,1536]{1,0:T(8,128)(2,1)S(1)} collective-permute-done((bf16[256,1536]{1,0:T(8,128)(2,1)S(1)}, bf16[256,1536]{1,0:T(8,128)(2,1)S(1)}, u32[]{:S(2)}, u32[]{:S(2)}) %collective-permute-start.2) | collective-permute-done | bytes 786464 | tf_op jit(solution)/shard_map/ppermute | solution.py:166
  34.1 0.2 add_convert_fusion
  34.3 4.4 %collective-permute-start.3 = (bf16[64,1536]{1,0:T(8,128)(2,1)S(1)}, bf16[64,1536]{1,0:T(8,128)(2,1)S(1)}, u32[]{:S(2)}, u32[]{:S(2)}) collective-permute-start(bf16[64,1536]{1,0:T(8,128)(2,1)S(1)} %get-tuple-element.17), channel_id=1, source_target_pairs={{0,4},{1,7},{2,6},{3,5},{4,0},{5,3},{6,2},{7,1},{8,12},{9,15},{10,... | collective-permute-start | bytes 589832 | tf_op jit(solution)/shard_map/ppermute | solution.py:172
  38.7 2.4 %collective-permute-start.5 = (bf16[64,1536]{1,0:T(8,128)(2,1)S(1)}, bf16[64,1536]{1,0:T(8,128)(2,1)S(1)}, u32[]{:S(2)}, u32[]{:S(2)}) collective-permute-start(bf16[64,1536]{1,0:T(8,128)(2,1)S(1)} %get-tuple-element.18), channel_id=1, source_target_pairs={{0,6},{1,5},{2,4},{3,7},{4,2},{5,1},{6,0},{7,3},{8,14},{9,13},{10,... | collective-permute-start | bytes 589832 | tf_op jit(solution)/shard_map/ppermute | solution.py:172
  41.1 2.2 %collective-permute-start.4 = (bf16[64,1536]{1,0:T(8,128)(2,1)S(1)}, bf16[64,1536]{1,0:T(8,128)(2,1)S(1)}, u32[]{:S(2)}, u32[]{:S(2)}) collective-permute-start(bf16[64,1536]{1,0:T(8,128)(2,1)S(1)} %get-tuple-element.19), channel_id=1, source_target_pairs={{0,2},{1,3},{2,0},{3,1},{4,6},{5,7},{6,4},{7,5},{8,10},{9,11},{10,... | collective-permute-start | bytes 589832 | tf_op jit(solution)/shard_map/ppermute | solution.py:172
  43.3 3.0 %collective-permute-done.3 = bf16[64,1536]{1,0:T(8,128)(2,1)S(1)} collective-permute-done((bf16[64,1536]{1,0:T(8,128)(2,1)S(1)}, bf16[64,1536]{1,0:T(8,128)(2,1)S(1)}, u32[]{:S(2)}, u32[]{:S(2)}) %collective-permute-start.3) | collective-permute-done | bytes 196640 | tf_op jit(solution)/shard_map/ppermute | solution.py:172
  46.3 0.4 collective-permute-done.5
  46.7 1.2 %collective-permute-done.4 = bf16[64,1536]{1,0:T(8,128)(2,1)S(1)} collective-permute-done((bf16[64,1536]{1,0:T(8,128)(2,1)S(1)}, bf16[64,1536]{1,0:T(8,128)(2,1)S(1)}, u32[]{:S(2)}, u32[]{:S(2)}) %collective-permute-start.4) | collective-permute-done | bytes 196640 | tf_op jit(solution)/shard_map/ppermute | solution.py:172
  48.0 0.8 %convert_add_fusion = f32[64,1536]{1,0:T(8,128)} fusion(bf16[64,1536]{1,0:T(8,128)(2,1)S(1)} %collective-permute-done.5, bf16[64,1536]{1,0:T(8,128)(2,1)S(1)} %collective-permute-done.4, bf16[64,1536]{1,0:T(8,128)(2,1)S(1)} %collective-permute-done.3, bf16[256,1536]{1,0:T(8,128)(2,1)S(1)} %add_convert_fusion), kind=kLoop, calls=%fused_computation.1 | loop fusion | flops 688128 | bytes 1179648 | tf_op jit(solution)/shard_map/add | solution.py:172
  (4 shorter events, 0.0 us)
Async XLA Ops:
  0.0 25.6 %copy-start.1 = (bf16[8,128,128]{2,1,0:T(8,128)(2,1)S(1)}, bf16[8,128,128]{2,1,0:T(8,128)(2,1)}, u32[]{:S(2)}) copy-start(bf16[8,128,128]{2,1,0:T(8,128)(2,1)} %p_hbm.1) | copy-start | bytes 786436
  0.0 25.6 %copy-start.4 = (s32[8]{0:T(128)S(1)}, s32[8]{0:T(128)}, u32[]{:S(2)}) copy-start(s32[8]{0:T(128)} %agg_hbm.1) | copy-start | bytes 100
  0.0 25.6 %copy-start.3 = (s32[8]{0:T(128)S(1)}, s32[8]{0:T(128)}, u32[]{:S(2)}) copy-start(s32[8]{0:T(128)} %count_ref.1) | copy-start | bytes 100
  0.0 25.6 %copy-start.2 = (s32[8,8]{1,0:T(8,128)S(1)}, s32[8,8]{1,0:T(8,128)}, u32[]{:S(2)}) copy-start(s32[8,8]{1,0:T(8,128)} %col_ref.1) | copy-start | bytes 772
  0.0 25.6 %copy-start = (bf16[8,8,128,128]{3,2,1,0:T(8,128)(2,1)S(1)}, bf16[8,8,128,128]{3,2,1,0:T(8,128)(2,1)}, u32[]{:S(2)}) copy-start(bf16[8,8,128,128]{3,2,1,0:T(8,128)(2,1)} %a_ref.1) | copy-start | bytes 6291460
  1.7 26.7 %collective-permute-start = (bf16[2,144,128]{2,1,0:T(8,128)(2,1)}, bf16[2,144,128]{2,1,0:T(8,128)(2,1)S(1)}, u32[]{:S(2)}, u32[]{:S(2)}) collective-permute-start(bf16[2,144,128]{2,1,0:T(8,128)(2,1)} %get-tuple-element.13), channel_id=1, source_target_pairs={{0,8},{8,0},{16,24},{24,16},{32,40},{40,32},{48,56},{56,48},{64,72... | collective-permute-start | bytes 221192 | tf_op jit(solution)/shard_map/ppermute | solution.py:134
  6.6 21.9 %collective-permute-start.1 = (bf16[2,144,128]{2,1,0:T(8,128)(2,1)}, bf16[2,144,128]{2,1,0:T(8,128)(2,1)S(1)}, u32[]{:S(2)}, u32[]{:S(2)}) collective-permute-start(bf16[2,144,128]{2,1,0:T(8,128)(2,1)} %get-tuple-element.14), channel_id=1, source_target_pairs={{8,16},{16,8},{24,32},{32,24},{40,48},{48,40},{56,64},{64,56},{72,... | collective-permute-start | bytes 221192 | tf_op jit(solution)/shard_map/ppermute | solution.py:134
  29.0 5.1 %collective-permute-start.2 = (bf16[256,1536]{1,0:T(8,128)(2,1)S(1)}, bf16[256,1536]{1,0:T(8,128)(2,1)S(1)}, u32[]{:S(2)}, u32[]{:S(2)}) collective-permute-start(bf16[256,1536]{1,0:T(8,128)(2,1)S(1)} %get-tuple-element.16), channel_id=1, source_target_pairs={{0,1},{1,0},{2,3},{3,2},{4,5},{5,4},{6,7},{7,6},{8,9},{9,8},{10,11... | collective-permute-start | bytes 2359304 | tf_op jit(solution)/shard_map/ppermute | solution.py:166
  34.3 12.0 %collective-permute-start.3 = (bf16[64,1536]{1,0:T(8,128)(2,1)S(1)}, bf16[64,1536]{1,0:T(8,128)(2,1)S(1)}, u32[]{:S(2)}, u32[]{:S(2)}) collective-permute-start(bf16[64,1536]{1,0:T(8,128)(2,1)S(1)} %get-tuple-element.17), channel_id=1, source_target_pairs={{0,4},{1,7},{2,6},{3,5},{4,0},{5,3},{6,2},{7,1},{8,12},{9,15},{10,... | collective-permute-start | bytes 589832 | tf_op jit(solution)/shard_map/ppermute | solution.py:172
  38.7 8.0 %collective-permute-start.5 = (bf16[64,1536]{1,0:T(8,128)(2,1)S(1)}, bf16[64,1536]{1,0:T(8,128)(2,1)S(1)}, u32[]{:S(2)}, u32[]{:S(2)}) collective-permute-start(bf16[64,1536]{1,0:T(8,128)(2,1)S(1)} %get-tuple-element.18), channel_id=1, source_target_pairs={{0,6},{1,5},{2,4},{3,7},{4,2},{5,1},{6,0},{7,3},{8,14},{9,13},{10,... | collective-permute-start | bytes 589832 | tf_op jit(solution)/shard_map/ppermute | solution.py:172
  41.1 6.8 %collective-permute-start.4 = (bf16[64,1536]{1,0:T(8,128)(2,1)S(1)}, bf16[64,1536]{1,0:T(8,128)(2,1)S(1)}, u32[]{:S(2)}, u32[]{:S(2)}) collective-permute-start(bf16[64,1536]{1,0:T(8,128)(2,1)S(1)} %get-tuple-element.19), channel_id=1, source_target_pairs={{0,2},{1,3},{2,0},{3,1},{4,6},{5,7},{6,4},{7,5},{8,10},{9,11},{10,... | collective-permute-start | bytes 589832 | tf_op jit(solution)/shard_map/ppermute | solution.py:172

commit v8 on v7

--- a/solution.py
+++ b/solution.py
@@ -41,7 +41,8 @@
 
 
 def front_kernel(
-    groups, members, col_ref, count_ref, agg_ref, a_ref, p_ref, g_ref, own_ref, acc_ref, gown_ref, place_ref, pt_ref
+    groups, members, col_ref, count_ref, agg_ref, a_ref, p_ref,
+    g_ref, gown_ref, place_ref, acc_ref, pt_ref,
 ):
     rows, slots, tile = a_ref.shape[0], a_ref.shape[1], a_ref.shape[2]
     columns = rows + 2 * HALO
@@ -82,10 +83,9 @@
                     g_ref[to, pl.ds((c - rows) * tile, tile)] = block
                 else:
                     gown_ref[to, pl.ds((c - HALO) * tile, tile)] = block
-    own_ref[...] = jnp.dot(gown_ref[...], place_ref[...], preferred_element_type=jnp.float32).astype(jnp.bfloat16)
 
 
-def back_kernel(g_ref, own_ref, first_ref, second_ref, out_ref, send_ref, place_ref):
+def back_kernel(half, g_ref, gown_ref, placed_ref, first_ref, second_ref, out_ref, place_ref):
     tile = first_ref.shape[2]
     rows = out_ref.shape[0]
     for r in range(HALO):
@@ -96,14 +96,14 @@
                 chosen = [jnp.where(mark == float(side * CG + j), 1.0, 0.0).astype(jnp.bfloat16) for mark in marks]
                 place_ref[side, pl.ds(r * tile, tile), pl.ds(j * tile, tile)] = tiles[0] * chosen[0] + tiles[1] * chosen[1]
     width = CG * tile
+    depth = HALO * tile
+    at = pl.ds(half * rows, rows)
+    own = jnp.dot(gown_ref[at, :], placed_ref[...], preferred_element_type=jnp.float32)
+    out_ref[:, pl.ds(width, width)] = own.astype(jnp.bfloat16)
     for side in range(2):
-        depth = HALO * tile
-        result = jnp.dot(g_ref[:, pl.ds(side * depth, depth)], place_ref[side], preferred_element_type=jnp.float32).astype(jnp.bfloat16)
-        at = pl.ds(2 * side * width, width)
-        send_ref[:, at] = result[:rows]
-        out_ref[:, at] = result[rows:]
-    send_ref[:, pl.ds(width, width)] = own_ref[pl.ds(0, rows), :]
-    out_ref[:, pl.ds(width, width)] = own_ref[pl.ds(rows, rows), :]
+        columns = g_ref[at, pl.ds(side * depth, depth)]
+        result = jnp.dot(columns, place_ref[side], preferred_element_type=jnp.float32)
+        out_ref[:, pl.ds(2 * side * width, width)] = result.astype(jnp.bfloat16)
 
 
 def local(groups, members, a_tiles, col_tiles, counts, aggregate, p_tiles):
@@ -133,18 +133,17 @@
             route += [(i % groups, (i + 1) % groups), ((i + 1) % groups, i % groups)]
         halos.append(lax.ppermute(block, "dom", route))
 
-    g, own = pl.pallas_call(
+    operands = pl.pallas_call(
         functools.partial(front_kernel, groups, members),
         out_shape=(
             jax.ShapeDtypeStruct((CG * tile, 2 * HALO * tile), jnp.bfloat16),
-            jax.ShapeDtypeStruct((CG * tile, CG * tile), jnp.bfloat16),
+            jax.ShapeDtypeStruct((CG * tile, rows * tile), jnp.bfloat16),
+            jax.ShapeDtypeStruct((rows * tile, CG * tile), jnp.bfloat16),
         ),
         in_specs=[smem] * 3 + [vmem] * 2,
-        out_specs=(vmem, vmem),
+        out_specs=(vmem,) * 3,
         scratch_shapes=[
             pltpu.VMEM((CG * columns + 1, tile, tile), jnp.float32),
-            pltpu.VMEM((CG * tile, rows * tile), jnp.bfloat16),
-            pltpu.VMEM((rows * tile, CG * tile), jnp.bfloat16),
             pltpu.VMEM(p_tiles.shape, jnp.bfloat16),
         ],
         compiler_params=pltpu.CompilerParams(vmem_limit_bytes=24 * 2**20),
@@ -152,18 +151,20 @@
         name="front",
     )(col_tiles, counts, aggregate, a_tiles, p_tiles)
 
-    share = CG * tile // 2
-    keep, send = pl.pallas_call(
-        back_kernel,
-        out_shape=(jax.ShapeDtypeStruct((share, 3 * CG * tile), jnp.bfloat16),) * 2,
-        in_specs=[vmem] * 4,
-        out_specs=(vmem, vmem),
-        scratch_shapes=[pltpu.VMEM((2, HALO * tile, CG * tile), jnp.bfloat16)],
-        compiler_params=pltpu.CompilerParams(vmem_limit_bytes=24 * 2**20),
-        cost_estimate=pl.CostEstimate(flops=3 * 10**8, bytes_accessed=3 * 2**20, transcendentals=0),
-        name="back",
-    )(g, own, *halos)
-    other = lax.ppermute(send, "sub", [(i, i ^ 1) for i in range(members)])
+    def rows_of(half):
+        return pl.pallas_call(
+            functools.partial(back_kernel, half),
+            out_shape=jax.ShapeDtypeStruct((CG * tile // 2, 3 * CG * tile), jnp.bfloat16),
+            in_specs=[vmem] * 5,
+            out_specs=vmem,
+            scratch_shapes=[pltpu.VMEM((2, HALO * tile, CG * tile), jnp.bfloat16)],
+            compiler_params=pltpu.CompilerParams(vmem_limit_bytes=24 * 2**20),
+            cost_estimate=pl.CostEstimate(flops=4 * 10**8, bytes_accessed=4 * 2**20, transcendentals=0),
+            name="back",
+        )(*operands, *halos)
+
+    other = lax.ppermute(rows_of(0), "sub", [(i, i ^ 1) for i in range(members)])
+    keep = rows_of(1)
     chip = (keep.astype(jnp.float32) + other.astype(jnp.float32)).astype(jnp.bfloat16)
     parts = chip.reshape(members // 2, -1, chip.shape[1])
     total = parts[0].astype(jnp.float32)

time: 49.8 us -> 49.5 us (level)
  waiting for transfers between devices: 6.53 us -> 5.95 us
    pallas_call x1, Pallas kernels: 2.79 us -> 2.12 us  [local(): pl.pallas_call(functools.partial(front_kernel, groups, members), out_shap...]
    pallas_call x1 -> x2, Pallas kernels: 0.53 us -> 1.19 us  [rows_of(): pl.pallas_call(functools.partial(back_kernel, half), out_shape=jax.ShapeD...]
    ppermute x1, waiting for transfers between devices: 1.89 us -> 1.29 us  [local(): lax.ppermute(rows_of(0), 'sub', [(i, i ^ 1) for i in range(members)])]
where the time goes in v8:
time: 49.5 us; the launch traced here: 48.5 us
  starting transfers between devices  36.3 us (73%)
  waiting for transfers between devices  5.95 us (12%)
  Pallas kernels  5.02 us (10%)
  other arithmetic  1.03 us (2%)
    ppermute x2, starting transfers between devices, local(): halos.append(lax.ppermute(block, 'dom', route))  23.9 us
    ppermute x3, starting transfers between devices, local(): total += lax.ppermute(parts[turn], 'sub', route).astype(jnp.float32)  8.98 us
    ppermute x3, waiting for transfers between devices, local(): total += lax.ppermute(parts[turn], 'sub', route).astype(jnp.float32)  4.65 us
    ppermute x1, starting transfers between devices, local(): lax.ppermute(rows_of(0), 'sub', [(i, i ^ 1) for i in range(members)])  3.47 us
    pallas_call x1, Pallas kernels, local(): pl.pallas_call(functools.partial(front_kernel, groups, members), out_shap...  2.12 us
    pallas_call x1, Pallas kernels, local(): pl.pallas_call(pack_kernel, out_shape=(jax.ShapeDtypeStruct((HALO, tile +...  1.71 us
    ppermute x1, waiting for transfers between devices, local(): lax.ppermute(rows_of(0), 'sub', [(i, i ^ 1) for i in range(members)])  1.29 us
    pallas_call x2, Pallas kernels, rows_of(): pl.pallas_call(functools.partial(back_kernel, half), out_shape=jax.ShapeD...  1.19 us
  transfers between devices with their start and end apart: 6, of which 4 were waited for; matrix products, arithmetic and copies ran while one was open for 0% of the time, Pallas kernels for 6%

profile of v8, /device:TPU:1, one launch (start us, length us, event | category | flops | bytes accessed | tf_op | source)
XLA Modules:
  0.0 48.5 jit_solution(8932521459058367156)
XLA Ops:
  0.0 0.0 copy-start.2
  0.0 0.0 copy-start
  0.0 1.7 %pack.1 = (bf16[2,144,128]{2,1,0:T(8,128)(2,1)}, bf16[2,144,128]{2,1,0:T(8,128)(2,1)}) custom-call(s32[8]{0:T(128)} %agg_hbm.1, bf16[8,128,128]{2,1,0:T(8,128)(2,1)} %p_hbm.1), custom_call_target="tpu_custom_call" | custom-call | flops 1000000000 | bytes 67108864 | tf_op jit(solution)/shard_map/pack/pallas_call | solution.py:116
  1.7 4.8 %collective-permute-start = (bf16[2,144,128]{2,1,0:T(8,128)(2,1)}, bf16[2,144,128]{2,1,0:T(8,128)(2,1)S(1)}, u32[]{:S(2)}, u32[]{:S(2)}) collective-permute-start(bf16[2,144,128]{2,1,0:T(8,128)(2,1)} %get-tuple-element.13), channel_id=1, source_target_pairs={{0,8},{8,0},{16,24},{24,16},{32,40},{40,32},{48,56},{56,48},{64,72... | collective-permute-start | bytes 221192 | tf_op jit(solution)/shard_map/ppermute | solution.py:134
  6.6 19.0 %collective-permute-start.1 = (bf16[2,144,128]{2,1,0:T(8,128)(2,1)}, bf16[2,144,128]{2,1,0:T(8,128)(2,1)S(1)}, u32[]{:S(2)}, u32[]{:S(2)}) collective-permute-start(bf16[2,144,128]{2,1,0:T(8,128)(2,1)} %get-tuple-element.14), channel_id=1, source_target_pairs={{8,16},{16,8},{24,32},{32,24},{40,48},{48,40},{56,64},{64,56},{72,... | collective-permute-start | bytes 221192 | tf_op jit(solution)/shard_map/ppermute | solution.py:134
  25.6 0.0 copy-done.1
  25.6 0.0 copy-done.4
  25.6 0.0 copy-done.3
  25.6 0.0 copy-done.2
  25.7 2.1 %front.1 = (bf16[512,512]{1,0:T(8,128)(2,1)S(1)}, bf16[512,1024]{1,0:T(8,128)(2,1)S(1)}, bf16[1024,512]{1,0:T(8,128)(2,1)S(1)}) custom-call(s32[8,8]{1,0:T(8,128)S(1)} %copy-done.2, s32[8]{0:T(128)S(1)} %copy-done.3, s32[8]{0:T(128)S(1)} %copy-done.4, bf16[8,8,128,128]{3,2,1,0:T(8,128)(2,1)S(1)} %copy-done, bf16[8,128,128]{2,1,0:T(8,128)(2,1)S(1)} %copy-done.1), custom_call_target="tpu_custom_call" | custom-call | flops 2000000000 | bytes 4194304 | tf_op jit(solution)/shard_map/front/pallas_call | solution.py:136
  27.8 0.0 collective-permute-done.first_ref
  27.8 0.0 collective-permute-done.1.second_ref
  27.8 0.6 %back.3 = bf16[256,1536]{1,0:T(8,128)(2,1)S(1)} custom-call(bf16[512,512]{1,0:T(8,128)(2,1)S(1)} %get-tuple-element.10.g_ref, bf16[512,1024]{1,0:T(8,128)(2,1)S(1)} %get-tuple-element.11.gown_ref, bf16[1024,512]{1,0:T(8,128)(2,1)S(1)} %get-tuple-element.12.placed_ref, bf16[2,144,128]{2,1,0:T(8,128)(2,1)S(1)} %collective-permute-done.first_ref, ...), custom_call_target="tpu_custom_call" | custom-call | flops 400000000 | bytes 4194304 | tf_op jit(solution)/shard_map/back/pallas_call | solution.py:155
  28.4 3.5 %collective-permute-start.2 = (bf16[256,1536]{1,0:T(8,128)(2,1)S(1)}, bf16[256,1536]{1,0:T(8,128)(2,1)S(1)}, u32[]{:S(2)}, u32[]{:S(2)}) collective-permute-start(bf16[256,1536]{1,0:T(8,128)(2,1)S(1)} %back.3), channel_id=1, source_target_pairs={{0,1},{1,0},{2,3},{3,2},{4,5},{5,4},{6,7},{7,6},{8,9},{9,8},{10,11... | collective-permute-start | bytes 2359304 | tf_op jit(solution)/shard_map/ppermute | solution.py:166
  31.9 0.6 %back.2 = bf16[256,1536]{1,0:T(8,128)(2,1)S(1)} custom-call(bf16[512,512]{1,0:T(8,128)(2,1)S(1)} %get-tuple-element.10.g_ref, bf16[512,1024]{1,0:T(8,128)(2,1)S(1)} %get-tuple-element.11.gown_ref, bf16[1024,512]{1,0:T(8,128)(2,1)S(1)} %get-tuple-element.12.placed_ref, bf16[2,144,128]{2,1,0:T(8,128)(2,1)S(1)} %collective-permute-done.first_ref, ...), custom_call_target="tpu_custom_call" | custom-call | flops 400000000 | bytes 4194304 | tf_op jit(solution)/shard_map/back/pallas_call | solution.py:155
  32.5 1.3 %collective-permute-done.2 = bf16[256,1536]{1,0:T(8,128)(2,1)S(1)} collective-permute-done((bf16[256,1536]{1,0:T(8,128)(2,1)S(1)}, bf16[256,1536]{1,0:T(8,128)(2,1)S(1)}, u32[]{:S(2)}, u32[]{:S(2)}) %collective-permute-start.2) | collective-permute-done | bytes 786464 | tf_op jit(solution)/shard_map/ppermute | solution.py:166
  33.8 0.2 add_convert_fusion
  34.0 4.4 %collective-permute-start.3 = (bf16[64,1536]{1,0:T(8,128)(2,1)S(1)}, bf16[64,1536]{1,0:T(8,128)(2,1)S(1)}, u32[]{:S(2)}, u32[]{:S(2)}) collective-permute-start(bf16[64,1536]{1,0:T(8,128)(2,1)S(1)} %get-tuple-element.15), channel_id=1, source_target_pairs={{0,4},{1,7},{2,6},{3,5},{4,0},{5,3},{6,2},{7,1},{8,12},{9,15},{10,... | collective-permute-start | bytes 589832 | tf_op jit(solution)/shard_map/ppermute | solution.py:173
  38.4 2.4 %collective-permute-start.5 = (bf16[64,1536]{1,0:T(8,128)(2,1)S(1)}, bf16[64,1536]{1,0:T(8,128)(2,1)S(1)}, u32[]{:S(2)}, u32[]{:S(2)}) collective-permute-start(bf16[64,1536]{1,0:T(8,128)(2,1)S(1)} %get-tuple-element.16), channel_id=1, source_target_pairs={{0,6},{1,5},{2,4},{3,7},{4,2},{5,1},{6,0},{7,3},{8,14},{9,13},{10,... | collective-permute-start | bytes 589832 | tf_op jit(solution)/shard_map/ppermute | solution.py:173
  40.9 2.2 %collective-permute-start.4 = (bf16[64,1536]{1,0:T(8,128)(2,1)S(1)}, bf16[64,1536]{1,0:T(8,128)(2,1)S(1)}, u32[]{:S(2)}, u32[]{:S(2)}) collective-permute-start(bf16[64,1536]{1,0:T(8,128)(2,1)S(1)} %get-tuple-element.17), channel_id=1, source_target_pairs={{0,2},{1,3},{2,0},{3,1},{4,6},{5,7},{6,4},{7,5},{8,10},{9,11},{10,... | collective-permute-start | bytes 589832 | tf_op jit(solution)/shard_map/ppermute | solution.py:173
  43.0 3.0 %collective-permute-done.3 = bf16[64,1536]{1,0:T(8,128)(2,1)S(1)} collective-permute-done((bf16[64,1536]{1,0:T(8,128)(2,1)S(1)}, bf16[64,1536]{1,0:T(8,128)(2,1)S(1)}, u32[]{:S(2)}, u32[]{:S(2)}) %collective-permute-start.3) | collective-permute-done | bytes 196640 | tf_op jit(solution)/shard_map/ppermute | solution.py:173
  46.0 0.4 collective-permute-done.5
  46.4 1.2 %collective-permute-done.4 = bf16[64,1536]{1,0:T(8,128)(2,1)S(1)} collective-permute-done((bf16[64,1536]{1,0:T(8,128)(2,1)S(1)}, bf16[64,1536]{1,0:T(8,128)(2,1)S(1)}, u32[]{:S(2)}, u32[]{:S(2)}) %collective-permute-start.4) | collective-permute-done | bytes 196640 | tf_op jit(solution)/shard_map/ppermute | solution.py:173
  47.7 0.8 %convert_add_fusion = f32[64,1536]{1,0:T(8,128)} fusion(bf16[64,1536]{1,0:T(8,128)(2,1)S(1)} %collective-permute-done.5, bf16[64,1536]{1,0:T(8,128)(2,1)S(1)} %collective-permute-done.4, bf16[64,1536]{1,0:T(8,128)(2,1)S(1)} %collective-permute-done.3, bf16[256,1536]{1,0:T(8,128)(2,1)S(1)} %add_convert_fusion), kind=kLoop, calls=%fused_computation.1 | loop fusion | flops 688128 | bytes 1179648 | tf_op jit(solution)/shard_map/add | solution.py:173
  (5 shorter events, 0.0 us)
Async XLA Ops:
  0.0 25.6 %copy-start.1 = (bf16[8,128,128]{2,1,0:T(8,128)(2,1)S(1)}, bf16[8,128,128]{2,1,0:T(8,128)(2,1)}, u32[]{:S(2)}) copy-start(bf16[8,128,128]{2,1,0:T(8,128)(2,1)} %p_hbm.1) | copy-start | bytes 786436
  0.0 25.6 %copy-start.4 = (s32[8]{0:T(128)S(1)}, s32[8]{0:T(128)}, u32[]{:S(2)}) copy-start(s32[8]{0:T(128)} %agg_hbm.1) | copy-start | bytes 100
  0.0 25.6 %copy-start.3 = (s32[8]{0:T(128)S(1)}, s32[8]{0:T(128)}, u32[]{:S(2)}) copy-start(s32[8]{0:T(128)} %count_ref.1) | copy-start | bytes 100
  0.0 25.6 %copy-start.2 = (s32[8,8]{1,0:T(8,128)S(1)}, s32[8,8]{1,0:T(8,128)}, u32[]{:S(2)}) copy-start(s32[8,8]{1,0:T(8,128)} %col_ref.1) | copy-start | bytes 772
  0.0 25.6 %copy-start = (bf16[8,8,128,128]{3,2,1,0:T(8,128)(2,1)S(1)}, bf16[8,8,128,128]{3,2,1,0:T(8,128)(2,1)}, u32[]{:S(2)}) copy-start(bf16[8,8,128,128]{3,2,1,0:T(8,128)(2,1)} %a_ref.1) | copy-start | bytes 6291460
  1.7 26.1 %collective-permute-start = (bf16[2,144,128]{2,1,0:T(8,128)(2,1)}, bf16[2,144,128]{2,1,0:T(8,128)(2,1)S(1)}, u32[]{:S(2)}, u32[]{:S(2)}) collective-permute-start(bf16[2,144,128]{2,1,0:T(8,128)(2,1)} %get-tuple-element.13), channel_id=1, source_target_pairs={{0,8},{8,0},{16,24},{24,16},{32,40},{40,32},{48,56},{56,48},{64,72... | collective-permute-start | bytes 221192 | tf_op jit(solution)/shard_map/ppermute | solution.py:134
  6.6 21.2 %collective-permute-start.1 = (bf16[2,144,128]{2,1,0:T(8,128)(2,1)}, bf16[2,144,128]{2,1,0:T(8,128)(2,1)S(1)}, u32[]{:S(2)}, u32[]{:S(2)}) collective-permute-start(bf16[2,144,128]{2,1,0:T(8,128)(2,1)} %get-tuple-element.14), channel_id=1, source_target_pairs={{8,16},{16,8},{24,32},{32,24},{40,48},{48,40},{56,64},{64,56},{72,... | collective-permute-start | bytes 221192 | tf_op jit(solution)/shard_map/ppermute | solution.py:134
  28.4 5.4 %collective-permute-start.2 = (bf16[256,1536]{1,0:T(8,128)(2,1)S(1)}, bf16[256,1536]{1,0:T(8,128)(2,1)S(1)}, u32[]{:S(2)}, u32[]{:S(2)}) collective-permute-start(bf16[256,1536]{1,0:T(8,128)(2,1)S(1)} %back.3), channel_id=1, source_target_pairs={{0,1},{1,0},{2,3},{3,2},{4,5},{5,4},{6,7},{7,6},{8,9},{9,8},{10,11... | collective-permute-start | bytes 2359304 | tf_op jit(solution)/shard_map/ppermute | solution.py:166
  34.0 12.0 %collective-permute-start.3 = (bf16[64,1536]{1,0:T(8,128)(2,1)S(1)}, bf16[64,1536]{1,0:T(8,128)(2,1)S(1)}, u32[]{:S(2)}, u32[]{:S(2)}) collective-permute-start(bf16[64,1536]{1,0:T(8,128)(2,1)S(1)} %get-tuple-element.15), channel_id=1, source_target_pairs={{0,4},{1,7},{2,6},{3,5},{4,0},{5,3},{6,2},{7,1},{8,12},{9,15},{10,... | collective-permute-start | bytes 589832 | tf_op jit(solution)/shard_map/ppermute | solution.py:173
  38.4 8.0 %collective-permute-start.5 = (bf16[64,1536]{1,0:T(8,128)(2,1)S(1)}, bf16[64,1536]{1,0:T(8,128)(2,1)S(1)}, u32[]{:S(2)}, u32[]{:S(2)}) collective-permute-start(bf16[64,1536]{1,0:T(8,128)(2,1)S(1)} %get-tuple-element.16), channel_id=1, source_target_pairs={{0,6},{1,5},{2,4},{3,7},{4,2},{5,1},{6,0},{7,3},{8,14},{9,13},{10,... | collective-permute-start | bytes 589832 | tf_op jit(solution)/shard_map/ppermute | solution.py:173
  40.9 6.8 %collective-permute-start.4 = (bf16[64,1536]{1,0:T(8,128)(2,1)S(1)}, bf16[64,1536]{1,0:T(8,128)(2,1)S(1)}, u32[]{:S(2)}, u32[]{:S(2)}) collective-permute-start(bf16[64,1536]{1,0:T(8,128)(2,1)S(1)} %get-tuple-element.17), channel_id=1, source_target_pairs={{0,2},{1,3},{2,0},{3,1},{4,6},{5,7},{6,4},{7,5},{8,10},{9,11},{10,... | collective-permute-start | bytes 589832 | tf_op jit(solution)/shard_map/ppermute | solution.py:173

commit v9 on v8

--- a/solution.py
+++ b/solution.py
@@ -165,12 +165,15 @@
 
     other = lax.ppermute(rows_of(0), "sub", [(i, i ^ 1) for i in range(members)])
     keep = rows_of(1)
-    chip = (keep.astype(jnp.float32) + other.astype(jnp.float32)).astype(jnp.bfloat16)
-    parts = chip.reshape(members // 2, -1, chip.shape[1])
-    total = parts[0].astype(jnp.float32)
+    share = keep.shape[0] // (members // 2)
+    parts = []
+    for turn in range(members // 2):
+        at = slice(turn * share, (turn + 1) * share)
+        parts.append(keep[at].astype(jnp.float32) + other[at].astype(jnp.float32))
+    total = parts[0]
     for turn in range(1, members // 2):
         route = [(i, i ^ (2 * TURNS[i % 2][turn - 1])) for i in range(members)]
-        total += lax.ppermute(parts[turn], "sub", route).astype(jnp.float32)
+        total += lax.ppermute(parts[turn].astype(jnp.bfloat16), "sub", route).astype(jnp.float32)
     return total
 
 

time: 49.5 us -> 49.4 us (level)
  no operation moved by 1% of the time
where the time goes in v9:
time: 49.4 us; the launch traced here: 48.4 us
  starting transfers between devices  36.3 us (73%)
  waiting for transfers between devices  5.95 us (12%)
  Pallas kernels  5.02 us (10%)
  other arithmetic  1 us (2%)
    ppermute x2, starting transfers between devices, local(): halos.append(lax.ppermute(block, 'dom', route))  23.9 us
    ppermute x3, starting transfers between devices, local(): lax.ppermute(parts[turn].astype(jnp.bfloat16), 'sub', route)  8.98 us
    ppermute x3, waiting for transfers between devices, local(): lax.ppermute(parts[turn].astype(jnp.bfloat16), 'sub', route)  4.65 us
    ppermute x1, starting transfers between devices, local(): lax.ppermute(rows_of(0), 'sub', [(i, i ^ 1) for i in range(members)])  3.47 us
    pallas_call x1, Pallas kernels, local(): pl.pallas_call(functools.partial(front_kernel, groups, members), out_shap...  2.12 us
    pallas_call x1, Pallas kernels, local(): pl.pallas_call(pack_kernel, out_shape=(jax.ShapeDtypeStruct((HALO, tile +...  1.71 us
    ppermute x1, waiting for transfers between devices, local(): lax.ppermute(rows_of(0), 'sub', [(i, i ^ 1) for i in range(members)])  1.29 us
    pallas_call x2, Pallas kernels, rows_of(): pl.pallas_call(functools.partial(back_kernel, half), out_shape=jax.ShapeD...  1.19 us
  transfers between devices with their start and end apart: 6, of which 4 were waited for; matrix products, arithmetic and copies ran while one was open for 0% of the time, Pallas kernels for 6%

profile of v9, /device:TPU:1, one launch (start us, length us, event | category | flops | bytes accessed | tf_op | source)
XLA Modules:
  0.0 48.4 jit_solution(14819633390598007319)
XLA Ops:
  0.0 0.0 copy-start.2
  0.0 0.0 copy-start
  0.0 1.7 %pack.1 = (bf16[2,144,128]{2,1,0:T(8,128)(2,1)}, bf16[2,144,128]{2,1,0:T(8,128)(2,1)}) custom-call(s32[8]{0:T(128)} %agg_hbm.1, bf16[8,128,128]{2,1,0:T(8,128)(2,1)} %p_hbm.1), custom_call_target="tpu_custom_call" | custom-call | flops 1000000000 | bytes 67108864 | tf_op jit(solution)/shard_map/pack/pallas_call | solution.py:116
  1.7 4.8 %collective-permute-start = (bf16[2,144,128]{2,1,0:T(8,128)(2,1)}, bf16[2,144,128]{2,1,0:T(8,128)(2,1)S(1)}, u32[]{:S(2)}, u32[]{:S(2)}) collective-permute-start(bf16[2,144,128]{2,1,0:T(8,128)(2,1)} %get-tuple-element.13), channel_id=1, source_target_pairs={{0,8},{8,0},{16,24},{24,16},{32,40},{40,32},{48,56},{56,48},{64,72... | collective-permute-start | bytes 221192 | tf_op jit(solution)/shard_map/ppermute | solution.py:134
  6.6 19.0 %collective-permute-start.1 = (bf16[2,144,128]{2,1,0:T(8,128)(2,1)}, bf16[2,144,128]{2,1,0:T(8,128)(2,1)S(1)}, u32[]{:S(2)}, u32[]{:S(2)}) collective-permute-start(bf16[2,144,128]{2,1,0:T(8,128)(2,1)} %get-tuple-element.14), channel_id=1, source_target_pairs={{8,16},{16,8},{24,32},{32,24},{40,48},{48,40},{56,64},{64,56},{72,... | collective-permute-start | bytes 221192 | tf_op jit(solution)/shard_map/ppermute | solution.py:134
  25.6 0.0 copy-done.1
  25.6 0.0 copy-done.4
  25.6 0.0 copy-done.3
  25.6 0.0 copy-done.2
  25.7 2.1 %front.1 = (bf16[512,512]{1,0:T(8,128)(2,1)S(1)}, bf16[512,1024]{1,0:T(8,128)(2,1)S(1)}, bf16[1024,512]{1,0:T(8,128)(2,1)S(1)}) custom-call(s32[8,8]{1,0:T(8,128)S(1)} %copy-done.2, s32[8]{0:T(128)S(1)} %copy-done.3, s32[8]{0:T(128)S(1)} %copy-done.4, bf16[8,8,128,128]{3,2,1,0:T(8,128)(2,1)S(1)} %copy-done, bf16[8,128,128]{2,1,0:T(8,128)(2,1)S(1)} %copy-done.1), custom_call_target="tpu_custom_call" | custom-call | flops 2000000000 | bytes 4194304 | tf_op jit(solution)/shard_map/front/pallas_call | solution.py:136
  27.8 0.0 collective-permute-done.first_ref
  27.8 0.0 collective-permute-done.1.second_ref
  27.8 0.6 %back.3 = bf16[256,1536]{1,0:T(8,128)(2,1)S(1)} custom-call(bf16[512,512]{1,0:T(8,128)(2,1)S(1)} %get-tuple-element.10.g_ref, bf16[512,1024]{1,0:T(8,128)(2,1)S(1)} %get-tuple-element.11.gown_ref, bf16[1024,512]{1,0:T(8,128)(2,1)S(1)} %get-tuple-element.12.placed_ref, bf16[2,144,128]{2,1,0:T(8,128)(2,1)S(1)} %collective-permute-done.first_ref, ...), custom_call_target="tpu_custom_call" | custom-call | flops 400000000 | bytes 4194304 | tf_op jit(solution)/shard_map/back/pallas_call | solution.py:155
  28.4 3.5 %collective-permute-start.2 = (bf16[256,1536]{1,0:T(8,128)(2,1)S(1)}, bf16[256,1536]{1,0:T(8,128)(2,1)S(1)}, u32[]{:S(2)}, u32[]{:S(2)}) collective-permute-start(bf16[256,1536]{1,0:T(8,128)(2,1)S(1)} %back.3), channel_id=1, source_target_pairs={{0,1},{1,0},{2,3},{3,2},{4,5},{5,4},{6,7},{7,6},{8,9},{9,8},{10,11... | collective-permute-start | bytes 2359304 | tf_op jit(solution)/shard_map/ppermute | solution.py:166
  31.9 0.6 %back.2 = bf16[256,1536]{1,0:T(8,128)(2,1)S(1)} custom-call(bf16[512,512]{1,0:T(8,128)(2,1)S(1)} %get-tuple-element.10.g_ref, bf16[512,1024]{1,0:T(8,128)(2,1)S(1)} %get-tuple-element.11.gown_ref, bf16[1024,512]{1,0:T(8,128)(2,1)S(1)} %get-tuple-element.12.placed_ref, bf16[2,144,128]{2,1,0:T(8,128)(2,1)S(1)} %collective-permute-done.first_ref, ...), custom_call_target="tpu_custom_call" | custom-call | flops 400000000 | bytes 4194304 | tf_op jit(solution)/shard_map/back/pallas_call | solution.py:155
  32.5 1.3 %collective-permute-done.2 = bf16[256,1536]{1,0:T(8,128)(2,1)S(1)} collective-permute-done((bf16[256,1536]{1,0:T(8,128)(2,1)S(1)}, bf16[256,1536]{1,0:T(8,128)(2,1)S(1)}, u32[]{:S(2)}, u32[]{:S(2)}) %collective-permute-start.2) | collective-permute-done | bytes 786464 | tf_op jit(solution)/shard_map/ppermute | solution.py:166
  33.8 0.1 add_convert_fusion.2
  33.9 4.4 %collective-permute-start.3 = (bf16[64,1536]{1,0:T(8,128)(2,1)S(1)}, bf16[64,1536]{1,0:T(8,128)(2,1)S(1)}, u32[]{:S(2)}, u32[]{:S(2)}) collective-permute-start(bf16[64,1536]{1,0:T(8,128)(2,1)S(1)} %get-tuple-element.15), channel_id=1, source_target_pairs={{0,4},{1,7},{2,6},{3,5},{4,0},{5,3},{6,2},{7,1},{8,12},{9,15},{10,... | collective-permute-start | bytes 589832 | tf_op jit(solution)/shard_map/ppermute | solution.py:176
  38.3 2.4 %collective-permute-start.5 = (bf16[64,1536]{1,0:T(8,128)(2,1)S(1)}, bf16[64,1536]{1,0:T(8,128)(2,1)S(1)}, u32[]{:S(2)}, u32[]{:S(2)}) collective-permute-start(bf16[64,1536]{1,0:T(8,128)(2,1)S(1)} %get-tuple-element.16), channel_id=1, source_target_pairs={{0,6},{1,5},{2,4},{3,7},{4,2},{5,1},{6,0},{7,3},{8,14},{9,13},{10,... | collective-permute-start | bytes 589832 | tf_op jit(solution)/shard_map/ppermute | solution.py:176
  40.8 2.2 %collective-permute-start.4 = (bf16[64,1536]{1,0:T(8,128)(2,1)S(1)}, bf16[64,1536]{1,0:T(8,128)(2,1)S(1)}, u32[]{:S(2)}, u32[]{:S(2)}) collective-permute-start(bf16[64,1536]{1,0:T(8,128)(2,1)S(1)} %get-tuple-element.17), channel_id=1, source_target_pairs={{0,2},{1,3},{2,0},{3,1},{4,6},{5,7},{6,4},{7,5},{8,10},{9,11},{10,... | collective-permute-start | bytes 589832 | tf_op jit(solution)/shard_map/ppermute | solution.py:176
  42.9 3.0 %collective-permute-done.3 = bf16[64,1536]{1,0:T(8,128)(2,1)S(1)} collective-permute-done((bf16[64,1536]{1,0:T(8,128)(2,1)S(1)}, bf16[64,1536]{1,0:T(8,128)(2,1)S(1)}, u32[]{:S(2)}, u32[]{:S(2)}) %collective-permute-start.3) | collective-permute-done | bytes 196640 | tf_op jit(solution)/shard_map/ppermute | solution.py:176
  45.9 0.4 collective-permute-done.5
  46.3 1.2 %collective-permute-done.4 = bf16[64,1536]{1,0:T(8,128)(2,1)S(1)} collective-permute-done((bf16[64,1536]{1,0:T(8,128)(2,1)S(1)}, bf16[64,1536]{1,0:T(8,128)(2,1)S(1)}, u32[]{:S(2)}, u32[]{:S(2)}) %collective-permute-start.4) | collective-permute-done | bytes 196640 | tf_op jit(solution)/shard_map/ppermute | solution.py:176
  47.6 0.9 %convert_add_fusion = f32[64,1536]{1,0:T(8,128)} fusion(bf16[64,1536]{1,0:T(8,128)(2,1)S(1)} %collective-permute-done.5, bf16[64,1536]{1,0:T(8,128)(2,1)S(1)} %collective-permute-done.4, bf16[64,1536]{1,0:T(8,128)(2,1)S(1)} %collective-permute-done.3, bf16[256,1536]{1,0:T(8,128)(2,1)S(1)} %collective-permute-done.2, bf16[256,1536]{1,0:T(8,128)(2,1)S(1)} %back.2), kind=kLoop, calls=%fused_computation | loop fusion | flops 884736 | bytes 1376256 | tf_op jit(solution)/shard_map/add | solution.py:176
  (4 shorter events, 0.0 us)
Async XLA Ops:
  0.0 25.6 %copy-start.1 = (bf16[8,128,128]{2,1,0:T(8,128)(2,1)S(1)}, bf16[8,128,128]{2,1,0:T(8,128)(2,1)}, u32[]{:S(2)}) copy-start(bf16[8,128,128]{2,1,0:T(8,128)(2,1)} %p_hbm.1) | copy-start | bytes 786436
  0.0 25.6 %copy-start.4 = (s32[8]{0:T(128)S(1)}, s32[8]{0:T(128)}, u32[]{:S(2)}) copy-start(s32[8]{0:T(128)} %agg_hbm.1) | copy-start | bytes 100
  0.0 25.6 %copy-start.3 = (s32[8]{0:T(128)S(1)}, s32[8]{0:T(128)}, u32[]{:S(2)}) copy-start(s32[8]{0:T(128)} %count_ref.1) | copy-start | bytes 100
  0.0 25.6 %copy-start.2 = (s32[8,8]{1,0:T(8,128)S(1)}, s32[8,8]{1,0:T(8,128)}, u32[]{:S(2)}) copy-start(s32[8,8]{1,0:T(8,128)} %col_ref.1) | copy-start | bytes 772
  0.0 25.6 %copy-start = (bf16[8,8,128,128]{3,2,1,0:T(8,128)(2,1)S(1)}, bf16[8,8,128,128]{3,2,1,0:T(8,128)(2,1)}, u32[]{:S(2)}) copy-start(bf16[8,8,128,128]{3,2,1,0:T(8,128)(2,1)} %a_ref.1) | copy-start | bytes 6291460
  1.7 26.1 %collective-permute-start = (bf16[2,144,128]{2,1,0:T(8,128)(2,1)}, bf16[2,144,128]{2,1,0:T(8,128)(2,1)S(1)}, u32[]{:S(2)}, u32[]{:S(2)}) collective-permute-start(bf16[2,144,128]{2,1,0:T(8,128)(2,1)} %get-tuple-element.13), channel_id=1, source_target_pairs={{0,8},{8,0},{16,24},{24,16},{32,40},{40,32},{48,56},{56,48},{64,72... | collective-permute-start | bytes 221192 | tf_op jit(solution)/shard_map/ppermute | solution.py:134
  6.6 21.2 %collective-permute-start.1 = (bf16[2,144,128]{2,1,0:T(8,128)(2,1)}, bf16[2,144,128]{2,1,0:T(8,128)(2,1)S(1)}, u32[]{:S(2)}, u32[]{:S(2)}) collective-permute-start(bf16[2,144,128]{2,1,0:T(8,128)(2,1)} %get-tuple-element.14), channel_id=1, source_target_pairs={{8,16},{16,8},{24,32},{32,24},{40,48},{48,40},{56,64},{64,56},{72,... | collective-permute-start | bytes 221192 | tf_op jit(solution)/shard_map/ppermute | solution.py:134
  28.4 5.4 %collective-permute-start.2 = (bf16[256,1536]{1,0:T(8,128)(2,1)S(1)}, bf16[256,1536]{1,0:T(8,128)(2,1)S(1)}, u32[]{:S(2)}, u32[]{:S(2)}) collective-permute-start(bf16[256,1536]{1,0:T(8,128)(2,1)S(1)} %back.3), channel_id=1, source_target_pairs={{0,1},{1,0},{2,3},{3,2},{4,5},{5,4},{6,7},{7,6},{8,9},{9,8},{10,11... | collective-permute-start | bytes 2359304 | tf_op jit(solution)/shard_map/ppermute | solution.py:166
  33.9 12.0 %collective-permute-start.3 = (bf16[64,1536]{1,0:T(8,128)(2,1)S(1)}, bf16[64,1536]{1,0:T(8,128)(2,1)S(1)}, u32[]{:S(2)}, u32[]{:S(2)}) collective-permute-start(bf16[64,1536]{1,0:T(8,128)(2,1)S(1)} %get-tuple-element.15), channel_id=1, source_target_pairs={{0,4},{1,7},{2,6},{3,5},{4,0},{5,3},{6,2},{7,1},{8,12},{9,15},{10,... | collective-permute-start | bytes 589832 | tf_op jit(solution)/shard_map/ppermute | solution.py:176
  38.3 8.0 %collective-permute-start.5 = (bf16[64,1536]{1,0:T(8,128)(2,1)S(1)}, bf16[64,1536]{1,0:T(8,128)(2,1)S(1)}, u32[]{:S(2)}, u32[]{:S(2)}) collective-permute-start(bf16[64,1536]{1,0:T(8,128)(2,1)S(1)} %get-tuple-element.16), channel_id=1, source_target_pairs={{0,6},{1,5},{2,4},{3,7},{4,2},{5,1},{6,0},{7,3},{8,14},{9,13},{10,... | collective-permute-start | bytes 589832 | tf_op jit(solution)/shard_map/ppermute | solution.py:176
  40.8 6.8 %collective-permute-start.4 = (bf16[64,1536]{1,0:T(8,128)(2,1)S(1)}, bf16[64,1536]{1,0:T(8,128)(2,1)S(1)}, u32[]{:S(2)}, u32[]{:S(2)}) collective-permute-start(bf16[64,1536]{1,0:T(8,128)(2,1)S(1)} %get-tuple-element.17), channel_id=1, source_target_pairs={{0,2},{1,3},{2,0},{3,1},{4,6},{5,7},{6,4},{7,5},{8,10},{9,11},{10,... | collective-permute-start | bytes 589832 | tf_op jit(solution)/shard_map/ppermute | solution.py:176

commit v10 on v8

--- a/solution.py
+++ b/solution.py
@@ -9,7 +9,7 @@
 
 CG = 4
 HALO = 2
-TURNS = ((2, 1, 3), (3, 1, 2))
+TURNS = ((2, 3, 1), (2, 1, 3))
 MARK = 16
 
 

time: 49.5 us -> 49.8 us (level); the launches traced: 48.5 us -> 49.5 us
  waiting for transfers between devices: 5.95 us -> 6.55 us
    ppermute x3, waiting for transfers between devices: 4.65 us -> 5.26 us  [local(): total += lax.ppermute(parts[turn], 'sub', route).astype(jnp.float32)]
  transfers between devices with their start and end apart: 6 -> 6, of which waited for: 4 -> 4; matrix products, arithmetic and copies ran while one was open for 0% -> 0% of each run, Pallas kernels for 6% -> 5%
where the time goes in v10:
time: 49.8 us; the launch traced here: 49.5 us
  starting transfers between devices  36.7 us (74%)
  waiting for transfers between devices  6.55 us (13%)
  Pallas kernels  5.01 us (10%)
  other arithmetic  1.03 us (2%)
    ppermute x2, starting transfers between devices, local(): halos.append(lax.ppermute(block, 'dom', route))  23.9 us
    ppermute x3, starting transfers between devices, local(): total += lax.ppermute(parts[turn], 'sub', route).astype(jnp.float32)  9.34 us
    ppermute x3, waiting for transfers between devices, local(): total += lax.ppermute(parts[turn], 'sub', route).astype(jnp.float32)  5.26 us
    ppermute x1, starting transfers between devices, local(): lax.ppermute(rows_of(0), 'sub', [(i, i ^ 1) for i in range(members)])  3.47 us
    pallas_call x1, Pallas kernels, local(): pl.pallas_call(functools.partial(front_kernel, groups, members), out_shap...  2.11 us
    pallas_call x1, Pallas kernels, local(): pl.pallas_call(pack_kernel, out_shape=(jax.ShapeDtypeStruct((HALO, tile +...  1.71 us
    ppermute x1, waiting for transfers between devices, local(): lax.ppermute(rows_of(0), 'sub', [(i, i ^ 1) for i in range(members)])  1.29 us
    pallas_call x2, Pallas kernels, rows_of(): pl.pallas_call(functools.partial(back_kernel, half), out_shape=jax.ShapeD...  1.19 us
  transfers between devices with their start and end apart: 6, of which 4 were waited for; matrix products, arithmetic and copies ran while one was open for 0% of the time, Pallas kernels for 5%

profile of v10, /device:TPU:1, one launch (start us, length us, event | category | flops | bytes accessed | tf_op | source)
XLA Modules:
  0.0 49.5 jit_solution(15816672895239383061)
XLA Ops:
  0.0 0.0 copy-start.2
  0.0 0.0 copy-start
  0.0 1.7 %pack.1 = (bf16[2,144,128]{2,1,0:T(8,128)(2,1)}, bf16[2,144,128]{2,1,0:T(8,128)(2,1)}) custom-call(s32[8]{0:T(128)} %agg_hbm.1, bf16[8,128,128]{2,1,0:T(8,128)(2,1)} %p_hbm.1), custom_call_target="tpu_custom_call" | custom-call | flops 1000000000 | bytes 67108864 | tf_op jit(solution)/shard_map/pack/pallas_call | solution.py:116
  1.7 4.8 %collective-permute-start = (bf16[2,144,128]{2,1,0:T(8,128)(2,1)}, bf16[2,144,128]{2,1,0:T(8,128)(2,1)S(1)}, u32[]{:S(2)}, u32[]{:S(2)}) collective-permute-start(bf16[2,144,128]{2,1,0:T(8,128)(2,1)} %get-tuple-element.13), channel_id=1, source_target_pairs={{0,8},{8,0},{16,24},{24,16},{32,40},{40,32},{48,56},{56,48},{64,72... | collective-permute-start | bytes 221192 | tf_op jit(solution)/shard_map/ppermute | solution.py:134
  6.6 19.0 %collective-permute-start.1 = (bf16[2,144,128]{2,1,0:T(8,128)(2,1)}, bf16[2,144,128]{2,1,0:T(8,128)(2,1)S(1)}, u32[]{:S(2)}, u32[]{:S(2)}) collective-permute-start(bf16[2,144,128]{2,1,0:T(8,128)(2,1)} %get-tuple-element.14), channel_id=1, source_target_pairs={{8,16},{16,8},{24,32},{32,24},{40,48},{48,40},{56,64},{64,56},{72,... | collective-permute-start | bytes 221192 | tf_op jit(solution)/shard_map/ppermute | solution.py:134
  25.6 0.0 copy-done.1
  25.6 0.0 copy-done.4
  25.6 0.0 copy-done.3
  25.6 0.0 copy-done.2
  25.7 2.1 %front.1 = (bf16[512,512]{1,0:T(8,128)(2,1)S(1)}, bf16[512,1024]{1,0:T(8,128)(2,1)S(1)}, bf16[1024,512]{1,0:T(8,128)(2,1)S(1)}) custom-call(s32[8,8]{1,0:T(8,128)S(1)} %copy-done.2, s32[8]{0:T(128)S(1)} %copy-done.3, s32[8]{0:T(128)S(1)} %copy-done.4, bf16[8,8,128,128]{3,2,1,0:T(8,128)(2,1)S(1)} %copy-done, bf16[8,128,128]{2,1,0:T(8,128)(2,1)S(1)} %copy-done.1), custom_call_target="tpu_custom_call" | custom-call | flops 2000000000 | bytes 4194304 | tf_op jit(solution)/shard_map/front/pallas_call | solution.py:136
  27.8 0.0 collective-permute-done.first_ref
  27.8 0.0 collective-permute-done.1.second_ref
  27.8 0.6 %back.3 = bf16[256,1536]{1,0:T(8,128)(2,1)S(1)} custom-call(bf16[512,512]{1,0:T(8,128)(2,1)S(1)} %get-tuple-element.10.g_ref, bf16[512,1024]{1,0:T(8,128)(2,1)S(1)} %get-tuple-element.11.gown_ref, bf16[1024,512]{1,0:T(8,128)(2,1)S(1)} %get-tuple-element.12.placed_ref, bf16[2,144,128]{2,1,0:T(8,128)(2,1)S(1)} %collective-permute-done.first_ref, ...), custom_call_target="tpu_custom_call" | custom-call | flops 400000000 | bytes 4194304 | tf_op jit(solution)/shard_map/back/pallas_call | solution.py:155
  28.4 3.5 %collective-permute-start.2 = (bf16[256,1536]{1,0:T(8,128)(2,1)S(1)}, bf16[256,1536]{1,0:T(8,128)(2,1)S(1)}, u32[]{:S(2)}, u32[]{:S(2)}) collective-permute-start(bf16[256,1536]{1,0:T(8,128)(2,1)S(1)} %back.3), channel_id=1, source_target_pairs={{0,1},{1,0},{2,3},{3,2},{4,5},{5,4},{6,7},{7,6},{8,9},{9,8},{10,11... | collective-permute-start | bytes 2359304 | tf_op jit(solution)/shard_map/ppermute | solution.py:166
  31.9 0.6 %back.2 = bf16[256,1536]{1,0:T(8,128)(2,1)S(1)} custom-call(bf16[512,512]{1,0:T(8,128)(2,1)S(1)} %get-tuple-element.10.g_ref, bf16[512,1024]{1,0:T(8,128)(2,1)S(1)} %get-tuple-element.11.gown_ref, bf16[1024,512]{1,0:T(8,128)(2,1)S(1)} %get-tuple-element.12.placed_ref, bf16[2,144,128]{2,1,0:T(8,128)(2,1)S(1)} %collective-permute-done.first_ref, ...), custom_call_target="tpu_custom_call" | custom-call | flops 400000000 | bytes 4194304 | tf_op jit(solution)/shard_map/back/pallas_call | solution.py:155
  32.5 1.3 %collective-permute-done.2 = bf16[256,1536]{1,0:T(8,128)(2,1)S(1)} collective-permute-done((bf16[256,1536]{1,0:T(8,128)(2,1)S(1)}, bf16[256,1536]{1,0:T(8,128)(2,1)S(1)}, u32[]{:S(2)}, u32[]{:S(2)}) %collective-permute-start.2) | collective-permute-done | bytes 786464 | tf_op jit(solution)/shard_map/ppermute | solution.py:166
  33.8 0.2 add_convert_fusion
  34.0 4.7 %collective-permute-start.3 = (bf16[64,1536]{1,0:T(8,128)(2,1)S(1)}, bf16[64,1536]{1,0:T(8,128)(2,1)S(1)}, u32[]{:S(2)}, u32[]{:S(2)}) collective-permute-start(bf16[64,1536]{1,0:T(8,128)(2,1)S(1)} %get-tuple-element.15), channel_id=1, source_target_pairs={{0,4},{1,5},{2,6},{3,7},{4,0},{5,1},{6,2},{7,3},{8,12},{9,13},{10,... | collective-permute-start | bytes 589832 | tf_op jit(solution)/shard_map/ppermute | solution.py:173
  38.7 2.8 %collective-permute-start.5 = (bf16[64,1536]{1,0:T(8,128)(2,1)S(1)}, bf16[64,1536]{1,0:T(8,128)(2,1)S(1)}, u32[]{:S(2)}, u32[]{:S(2)}) collective-permute-start(bf16[64,1536]{1,0:T(8,128)(2,1)S(1)} %get-tuple-element.16), channel_id=1, source_target_pairs={{0,2},{1,7},{2,0},{3,5},{4,6},{5,3},{6,4},{7,1},{8,10},{9,15},{10,... | collective-permute-start | bytes 589832 | tf_op jit(solution)/shard_map/ppermute | solution.py:173
  41.5 1.9 %collective-permute-start.4 = (bf16[64,1536]{1,0:T(8,128)(2,1)S(1)}, bf16[64,1536]{1,0:T(8,128)(2,1)S(1)}, u32[]{:S(2)}, u32[]{:S(2)}) collective-permute-start(bf16[64,1536]{1,0:T(8,128)(2,1)S(1)} %get-tuple-element.17), channel_id=1, source_target_pairs={{0,6},{1,3},{2,4},{3,1},{4,2},{5,7},{6,0},{7,5},{8,14},{9,11},{10,... | collective-permute-start | bytes 589832 | tf_op jit(solution)/shard_map/ppermute | solution.py:173
  43.4 0.1 collective-permute-done.3
  43.5 2.8 %collective-permute-done.5 = bf16[64,1536]{1,0:T(8,128)(2,1)S(1)} collective-permute-done((bf16[64,1536]{1,0:T(8,128)(2,1)S(1)}, bf16[64,1536]{1,0:T(8,128)(2,1)S(1)}, u32[]{:S(2)}, u32[]{:S(2)}) %collective-permute-start.5) | collective-permute-done | bytes 196640 | tf_op jit(solution)/shard_map/ppermute | solution.py:173
  46.3 2.3 %collective-permute-done.4 = bf16[64,1536]{1,0:T(8,128)(2,1)S(1)} collective-permute-done((bf16[64,1536]{1,0:T(8,128)(2,1)S(1)}, bf16[64,1536]{1,0:T(8,128)(2,1)S(1)}, u32[]{:S(2)}, u32[]{:S(2)}) %collective-permute-start.4) | collective-permute-done | bytes 196640 | tf_op jit(solution)/shard_map/ppermute | solution.py:173
  48.6 0.8 %convert_add_fusion = f32[64,1536]{1,0:T(8,128)} fusion(bf16[64,1536]{1,0:T(8,128)(2,1)S(1)} %collective-permute-done.5, bf16[64,1536]{1,0:T(8,128)(2,1)S(1)} %collective-permute-done.4, bf16[64,1536]{1,0:T(8,128)(2,1)S(1)} %collective-permute-done.3, bf16[256,1536]{1,0:T(8,128)(2,1)S(1)} %add_convert_fusion), kind=kLoop, calls=%fused_computation.1 | loop fusion | flops 688128 | bytes 1179648 | tf_op jit(solution)/shard_map/add | solution.py:173
  (5 shorter events, 0.0 us)
Async XLA Ops:
  0.0 25.6 %copy-start.1 = (bf16[8,128,128]{2,1,0:T(8,128)(2,1)S(1)}, bf16[8,128,128]{2,1,0:T(8,128)(2,1)}, u32[]{:S(2)}) copy-start(bf16[8,128,128]{2,1,0:T(8,128)(2,1)} %p_hbm.1) | copy-start | bytes 786436
  0.0 25.6 %copy-start.4 = (s32[8]{0:T(128)S(1)}, s32[8]{0:T(128)}, u32[]{:S(2)}) copy-start(s32[8]{0:T(128)} %agg_hbm.1) | copy-start | bytes 100
  0.0 25.6 %copy-start.3 = (s32[8]{0:T(128)S(1)}, s32[8]{0:T(128)}, u32[]{:S(2)}) copy-start(s32[8]{0:T(128)} %count_ref.1) | copy-start | bytes 100
  0.0 25.6 %copy-start.2 = (s32[8,8]{1,0:T(8,128)S(1)}, s32[8,8]{1,0:T(8,128)}, u32[]{:S(2)}) copy-start(s32[8,8]{1,0:T(8,128)} %col_ref.1) | copy-start | bytes 772
  0.0 25.6 %copy-start = (bf16[8,8,128,128]{3,2,1,0:T(8,128)(2,1)S(1)}, bf16[8,8,128,128]{3,2,1,0:T(8,128)(2,1)}, u32[]{:S(2)}) copy-start(bf16[8,8,128,128]{3,2,1,0:T(8,128)(2,1)} %a_ref.1) | copy-start | bytes 6291460
  1.7 26.0 %collective-permute-start = (bf16[2,144,128]{2,1,0:T(8,128)(2,1)}, bf16[2,144,128]{2,1,0:T(8,128)(2,1)S(1)}, u32[]{:S(2)}, u32[]{:S(2)}) collective-permute-start(bf16[2,144,128]{2,1,0:T(8,128)(2,1)} %get-tuple-element.13), channel_id=1, source_target_pairs={{0,8},{8,0},{16,24},{24,16},{32,40},{40,32},{48,56},{56,48},{64,72... | collective-permute-start | bytes 221192 | tf_op jit(solution)/shard_map/ppermute | solution.py:134
  6.6 21.2 %collective-permute-start.1 = (bf16[2,144,128]{2,1,0:T(8,128)(2,1)}, bf16[2,144,128]{2,1,0:T(8,128)(2,1)S(1)}, u32[]{:S(2)}, u32[]{:S(2)}) collective-permute-start(bf16[2,144,128]{2,1,0:T(8,128)(2,1)} %get-tuple-element.14), channel_id=1, source_target_pairs={{8,16},{16,8},{24,32},{32,24},{40,48},{48,40},{56,64},{64,56},{72,... | collective-permute-start | bytes 221192 | tf_op jit(solution)/shard_map/ppermute | solution.py:134
  28.4 5.4 %collective-permute-start.2 = (bf16[256,1536]{1,0:T(8,128)(2,1)S(1)}, bf16[256,1536]{1,0:T(8,128)(2,1)S(1)}, u32[]{:S(2)}, u32[]{:S(2)}) collective-permute-start(bf16[256,1536]{1,0:T(8,128)(2,1)S(1)} %back.3), channel_id=1, source_target_pairs={{0,1},{1,0},{2,3},{3,2},{4,5},{5,4},{6,7},{7,6},{8,9},{9,8},{10,11... | collective-permute-start | bytes 2359304 | tf_op jit(solution)/shard_map/ppermute | solution.py:166
  34.0 9.5 %collective-permute-start.3 = (bf16[64,1536]{1,0:T(8,128)(2,1)S(1)}, bf16[64,1536]{1,0:T(8,128)(2,1)S(1)}, u32[]{:S(2)}, u32[]{:S(2)}) collective-permute-start(bf16[64,1536]{1,0:T(8,128)(2,1)S(1)} %get-tuple-element.15), channel_id=1, source_target_pairs={{0,4},{1,5},{2,6},{3,7},{4,0},{5,1},{6,2},{7,3},{8,12},{9,13},{10,... | collective-permute-start | bytes 589832 | tf_op jit(solution)/shard_map/ppermute | solution.py:173
  38.7 7.6 %collective-permute-start.5 = (bf16[64,1536]{1,0:T(8,128)(2,1)S(1)}, bf16[64,1536]{1,0:T(8,128)(2,1)S(1)}, u32[]{:S(2)}, u32[]{:S(2)}) collective-permute-start(bf16[64,1536]{1,0:T(8,128)(2,1)S(1)} %get-tuple-element.16), channel_id=1, source_target_pairs={{0,2},{1,7},{2,0},{3,5},{4,6},{5,3},{6,4},{7,1},{8,10},{9,15},{10,... | collective-permute-start | bytes 589832 | tf_op jit(solution)/shard_map/ppermute | solution.py:173
  41.5 7.2 %collective-permute-start.4 = (bf16[64,1536]{1,0:T(8,128)(2,1)S(1)}, bf16[64,1536]{1,0:T(8,128)(2,1)S(1)}, u32[]{:S(2)}, u32[]{:S(2)}) collective-permute-start(bf16[64,1536]{1,0:T(8,128)(2,1)S(1)} %get-tuple-element.17), channel_id=1, source_target_pairs={{0,6},{1,3},{2,4},{3,1},{4,2},{5,7},{6,0},{7,5},{8,14},{9,11},{10,... | collective-permute-start | bytes 589832 | tf_op jit(solution)/shard_map/ppermute | solution.py:173
